TPU v7x, 32 devices: a whole 2x2x4 slice. The times are simulated.
32 devices in a mesh: spin: 2 (over x), orb: 16 (over z, y, core).
Axes of the slice: x: 2, y: 2, z: 4, core: 2. Of those that a mesh axis runs over, the one named last changes fastest.
Arguments:
- integrals: bfloat16 [2, 16, 256, 512], P('spin', None, None, 'orb'), may hold values from -0.875 to 0.875
- metric_factor: bfloat16 [512, 512], replicated, may hold values from -0.25 to 0.25
- occ_energy: float32 [2, 16], replicated, may hold values from -2.5 to -0.3
- virt_energy: float32 [2, 256], replicated, may hold values from 0.3 to 3
Outputs:
- gamma_out: float32 [2, 16, 256, 512], P('spin', 'orb')
- density: float32 [2, 256, 256], P('spin', 'orb')
All inputs are finite; a program needn't handle non-finite values.
Results may differ from a plain program's by a relative error of at most 0.0019.
Values may be sent and summed in bfloat16 or wider, within the bound.
No kernel may reach another device: no remote copies, remote signals or barrier semaphores. Data moves between devices by JAX's collectives and lax.ppermute only.
A program may use at most 192 MiB of HBM per device.

v0:
```python
import jax
import jax.numpy as jnp
from jax import lax
from jax.sharding import PartitionSpec as P


def pair_terms(left_block, right_block, e_left, e_right, v_left, v_right, antisym, weights):
    coupling = jnp.einsum(
        "iaq,jbq->ijab", left_block, right_block, preferred_element_type=jnp.float32
    )
    coupling = jnp.where(
        antisym[None, :, None, None], coupling - jnp.swapaxes(coupling, 2, 3), coupling
    )
    denominator = (
        e_left[:, None, None, None]
        + e_right[None, :, None, None]
        - v_left[None, None, :, None]
        - v_right[None, :, None, :]
    )
    amplitude = (coupling / denominator).astype(jnp.bfloat16)
    gamma_terms = jnp.einsum(
        "ijab,jbq->iaq", amplitude, right_block, preferred_element_type=jnp.float32
    )
    scaled = amplitude * weights[None, :, None, None].astype(jnp.bfloat16)
    density_terms = jnp.einsum(
        "ijac,ijbc->ab", scaled, amplitude, preferred_element_type=jnp.float32
    )
    return (gamma_terms, density_terms)


def in_blocks(block_step, totals, members):
    piece_rows = members[0].shape[0]
    block_size = 4
    blocked = tuple(
        (
            member.reshape((piece_rows // block_size, block_size) + member.shape[1:])
            for member in members
        )
    )

    def scan_step(carried, block_items):
        return (block_step(carried, block_items), None)

    totals, unused = lax.scan(scan_step, totals, blocked)
    return totals


def local(integrals, metric_factor, occ_energy, virt_energy):
    fitted = jnp.einsum(
        "soaq,qp->soap",
        lax.all_to_all(integrals, "orb", split_axis=1, concat_axis=3, tiled=True),
        metric_factor,
        preferred_element_type=jnp.float32,
    ).astype(jnp.bfloat16)
    own_block = fitted[0]
    block_rows = own_block.shape[0]
    orb_count = lax.axis_size("orb")
    occupied = block_rows * orb_count
    spin_index = lax.axis_index("spin")
    orbit_index = lax.axis_index("orb")
    other_spin = 1 - spin_index
    occ_same = lax.dynamic_index_in_dim(occ_energy, spin_index, 0, keepdims=False)
    virt_same = lax.dynamic_index_in_dim(virt_energy, spin_index, 0, keepdims=False)
    virt_other = lax.dynamic_index_in_dim(virt_energy, other_spin, 0, keepdims=False)
    own_energy = lax.dynamic_slice_in_dim(occ_same, orbit_index * block_rows, block_rows)
    virt_count = virt_same.shape[0]
    initial = (
        jnp.zeros(own_block.shape, jnp.float32),
        jnp.zeros((virt_count, virt_count), jnp.float32),
    )

    def accumulate(totals, right_block, e_right, v_right, antisym, weights):
        gamma_terms, density_terms = pair_terms(
            own_block, right_block, own_energy, e_right, virt_same, v_right, antisym, weights
        )
        return (totals[0] + gamma_terms, totals[1] + density_terms)

    occ_flat = occ_energy.reshape(2 * occupied)

    def fold_joint(totals, segment):
        piece_rows = segment.shape[1]
        row_index = jnp.arange(piece_rows, dtype=jnp.int32)
        same_spin = row_index // occupied == spin_index
        v_right = jnp.where(same_spin[:, None], virt_same[None, :], virt_other[None, :])
        weights = jnp.where(same_spin, 0.5, 1.0).astype(jnp.float32)

        def block_step(carried, block_items):
            block_part, e_block, v_block, same_block, weight_block = block_items
            return accumulate(carried, block_part, e_block, v_block, same_block, weight_block)

        return in_blocks(block_step, totals, (segment[0], occ_flat, v_right, same_spin, weights))

    gamma_terms, density_terms = fold_joint(
        initial, lax.all_gather(fitted, ("spin", "orb"), axis=1, tiled=True)
    )
    owned_rows = lax.psum_scatter(density_terms[None], "orb", scatter_dimension=1, tiled=True)
    return (gamma_terms[None], owned_rows / occupied)


def solution(mesh):
    return jax.shard_map(
        local,
        mesh=mesh,
        in_specs=(P("spin", None, None, "orb"), P(), P(), P()),
        out_specs=(P("spin", "orb", None, None), P("spin", "orb", None)),
        check_vma=False,
    )
```

profile of v0, /device:TPU:0, one launch (start us, length us, event | category | flops | bytes accessed | tf_op | source)
XLA Modules:
  0.0 213.9 jit_solution(3978620034879405700)
XLA Ops:
  7.2 17.6 %all_to_all.15 = bf16[1,16,256,32]{2,3,0,1:T(8,128)(2,1)S(1)} all-to-all(bf16[1,16,256,32]{2,3,0,1:T(8,128)(2,1)} %bitcast.93), channel_id=1, replica_groups=mesh['spin'=2,'orb'=16] {'orb'}, dimensions={1} | all-to-all | bytes 524288 | tf_op jit(solution)/shard_map/all_to_all | solution.py:51
  24.8 1.1 convolution_convert_fusion
  26.0 0.8 reshape_reshape.3
  26.7 1.3 dynamic_slice.33
  28.1 0.8 constant_dynamic-slice_fusion.2
  28.8 0.1 broadcast_select_fusion
  28.9 73.0 %all-gather.3.cloned.1.call-done = bf16[8192,512]{1,0:T(8,128)(2,1)} async-done(((bf16[256,512]{1,0:T(8,128)(2,1)}), bf16[8192,512]{1,0:T(8,128)(2,1)}) %all-gather.3.cloned.1.call-update) | async-done | bytes 8388624 | tf_op jit(solution)/shard_map/all_gather | solution.py:94
  101.9 49.0 %while.13 = (s32[]{:T(128)}, f32[1,256,512]{2,1,0:T(8,128)}, f32[256,256]{1,0:T(8,128)S(1)}, pred[8,4]{1,0:T(8,128)(4,1)S(1)}, bf16[8,4,256,512]{3,2,1,0:T(8,128...) while((s32[]{:T(128)}, f32[1,256,512]{2,1,0:T(8,128)}, ...), condition=%wide.region_1.2_spmd.clone, body=%wide.region_0.1_spmd.clone.sunk | while | flops 673055744 | bytes 10770672 | solution.py:44
  101.9 1.7 fusion.47
  103.6 0.3 copy.10
  104.0 0.6 fusion.48
  104.6 0.1 broadcast_subtract_fusion.2
  104.7 0.3 fusion.49
  105.0 2.5 %fusion.50 = f32[1,256,512]{2,1,0:T(8,128)} fusion(bf16[8,4,256,512]{3,2,1,0:T(8,128)(2,1)} %get-tuple-element.219, s32[]{:T(128)} %get-tuple-element.202, bf16[1,4,256,256]{3,2,1,0:T(8,128)(2,1)S(1)} %fusion.49, f32[1,256,512]{2,1,0:T(8,128)} %get-tuple-element.203, pred[]{:T(512)S(6)} %compare.11), kind=kOutput, calls=%fused_computation.2.clone.1 | convolution fusion | flops 268697600 | bytes 2621953 | tf_op jit(solution)/shard_map/while/body/eval_jaxpr/ijab,jbq->iaq/dot_general | solution.py:21
  107.5 0.4 fusion.52
  107.9 1.7 fusion.47
  109.6 0.3 copy.10
  110.0 0.6 fusion.48
  110.7 0.3 fusion.49
  111.0 2.6 %fusion.50 = f32[1,256,512]{2,1,0:T(8,128)} fusion(bf16[8,4,256,512]{3,2,1,0:T(8,128)(2,1)} %get-tuple-element.219, s32[]{:T(128)} %get-tuple-element.202, bf16[1,4,256,256]{3,2,1,0:T(8,128)(2,1)S(1)} %fusion.49, f32[1,256,512]{2,1,0:T(8,128)} %get-tuple-element.203, pred[]{:T(512)S(6)} %compare.11), kind=kOutput, calls=%fused_computation.2.clone.1 | convolution fusion | flops 268697600 | bytes 2621953 | tf_op jit(solution)/shard_map/while/body/eval_jaxpr/ijab,jbq->iaq/dot_general | solution.py:21
  113.6 0.4 fusion.52
  114.1 1.7 fusion.47
  115.8 0.3 copy.10
  116.1 0.6 fusion.48
  116.8 0.1 broadcast_subtract_fusion.2
  116.9 0.3 fusion.49
  117.2 2.6 %fusion.50 = f32[1,256,512]{2,1,0:T(8,128)} fusion(bf16[8,4,256,512]{3,2,1,0:T(8,128)(2,1)} %get-tuple-element.219, s32[]{:T(128)} %get-tuple-element.202, bf16[1,4,256,256]{3,2,1,0:T(8,128)(2,1)S(1)} %fusion.49, f32[1,256,512]{2,1,0:T(8,128)} %get-tuple-element.203, pred[]{:T(512)S(6)} %compare.11), kind=kOutput, calls=%fused_computation.2.clone.1 | convolution fusion | flops 268697600 | bytes 2621953 | tf_op jit(solution)/shard_map/while/body/eval_jaxpr/ijab,jbq->iaq/dot_general | solution.py:21
  119.8 0.4 fusion.52
  120.2 1.7 fusion.47
  121.9 0.3 copy.10
  122.3 0.6 fusion.48
  122.9 0.1 broadcast_subtract_fusion.2
  123.0 0.3 fusion.49
  123.3 2.6 %fusion.50 = f32[1,256,512]{2,1,0:T(8,128)} fusion(bf16[8,4,256,512]{3,2,1,0:T(8,128)(2,1)} %get-tuple-element.219, s32[]{:T(128)} %get-tuple-element.202, bf16[1,4,256,256]{3,2,1,0:T(8,128)(2,1)S(1)} %fusion.49, f32[1,256,512]{2,1,0:T(8,128)} %get-tuple-element.203, pred[]{:T(512)S(6)} %compare.11), kind=kOutput, calls=%fused_computation.2.clone.1 | convolution fusion | flops 268697600 | bytes 2621953 | tf_op jit(solution)/shard_map/while/body/eval_jaxpr/ijab,jbq->iaq/dot_general | solution.py:21
  125.9 0.4 fusion.52
  126.4 1.7 fusion.47
  128.1 0.3 copy.10
  128.4 0.6 fusion.48
  129.1 0.1 broadcast_subtract_fusion.2
  129.2 0.3 fusion.49
  129.5 2.6 %fusion.50 = f32[1,256,512]{2,1,0:T(8,128)} fusion(bf16[8,4,256,512]{3,2,1,0:T(8,128)(2,1)} %get-tuple-element.219, s32[]{:T(128)} %get-tuple-element.202, bf16[1,4,256,256]{3,2,1,0:T(8,128)(2,1)S(1)} %fusion.49, f32[1,256,512]{2,1,0:T(8,128)} %get-tuple-element.203, pred[]{:T(512)S(6)} %compare.11), kind=kOutput, calls=%fused_computation.2.clone.1 | convolution fusion | flops 268697600 | bytes 2621953 | tf_op jit(solution)/shard_map/while/body/eval_jaxpr/ijab,jbq->iaq/dot_general | solution.py:21
  132.1 0.4 fusion.52
  132.5 1.7 fusion.47
  134.2 0.3 copy.10
  134.6 0.6 fusion.48
  135.2 0.1 broadcast_subtract_fusion.2
  135.3 0.3 fusion.49
  135.6 2.6 %fusion.50 = f32[1,256,512]{2,1,0:T(8,128)} fusion(bf16[8,4,256,512]{3,2,1,0:T(8,128)(2,1)} %get-tuple-element.219, s32[]{:T(128)} %get-tuple-element.202, bf16[1,4,256,256]{3,2,1,0:T(8,128)(2,1)S(1)} %fusion.49, f32[1,256,512]{2,1,0:T(8,128)} %get-tuple-element.203, pred[]{:T(512)S(6)} %compare.11), kind=kOutput, calls=%fused_computation.2.clone.1 | convolution fusion | flops 268697600 | bytes 2621953 | tf_op jit(solution)/shard_map/while/body/eval_jaxpr/ijab,jbq->iaq/dot_general | solution.py:21
  138.2 0.4 fusion.52
  138.7 1.7 fusion.47
  140.4 0.3 copy.10
  140.7 0.6 fusion.48
  141.5 0.3 fusion.49
  141.8 2.6 %fusion.50 = f32[1,256,512]{2,1,0:T(8,128)} fusion(bf16[8,4,256,512]{3,2,1,0:T(8,128)(2,1)} %get-tuple-element.219, s32[]{:T(128)} %get-tuple-element.202, bf16[1,4,256,256]{3,2,1,0:T(8,128)(2,1)S(1)} %fusion.49, f32[1,256,512]{2,1,0:T(8,128)} %get-tuple-element.203, pred[]{:T(512)S(6)} %compare.11), kind=kOutput, calls=%fused_computation.2.clone.1 | convolution fusion | flops 268697600 | bytes 2621953 | tf_op jit(solution)/shard_map/while/body/eval_jaxpr/ijab,jbq->iaq/dot_general | solution.py:21
  144.4 0.4 fusion.52
  144.8 1.7 fusion.47
  146.5 0.3 copy.10
  146.9 0.6 fusion.48
  147.6 0.3 fusion.49
  147.9 2.6 %fusion.50 = f32[1,256,512]{2,1,0:T(8,128)} fusion(bf16[8,4,256,512]{3,2,1,0:T(8,128)(2,1)} %get-tuple-element.219, s32[]{:T(128)} %get-tuple-element.202, bf16[1,4,256,256]{3,2,1,0:T(8,128)(2,1)S(1)} %fusion.49, f32[1,256,512]{2,1,0:T(8,128)} %get-tuple-element.203, pred[]{:T(512)S(6)} %compare.11), kind=kOutput, calls=%fused_computation.2.clone.1 | convolution fusion | flops 268697600 | bytes 2621953 | tf_op jit(solution)/shard_map/while/body/eval_jaxpr/ijab,jbq->iaq/dot_general | solution.py:21
  150.5 0.4 fusion.52
  151.0 0.7 copy-done.1
  151.7 54.0 %reduce-scatter.2.cloned.1.call-done = f32[1,16,256]{2,1,0:T(8,128)} async-done(((f32[1,256,256]{2,1,0:T(8,128)}), f32[1,16,256]{2,1,0:T(8,128)}) %reduce-scatter.2.cloned.1.call-update) | async-done | bytes 16400 | tf_op jit(solution)/shard_map/reduce_scatter | solution.py:96
  205.7 1.3 broadcast_multiply_fusion
  (39 shorter events, 0.5 us)
Async XLA Ops:
  7.2 17.6 %copy-start = (bf16[512,512]{1,0:T(8,128)(2,1)S(1)}, bf16[512,512]{1,0:T(8,128)(2,1)}, u32[]{:S(2)}) copy-start(bf16[512,512]{1,0:T(8,128)(2,1)} %param.7) | copy-start | bytes 1572868
  7.2 94.7 %all-gather.3.cloned.1.call-start = ((), (), s32[]{:S(2)}) async-start(), calls=%async_computation.3 | async-start | bytes 8650752 | tf_op jit(solution)/shard_map/all_gather | solution.py:94
  25.9 179.8 %reduce-scatter.2.cloned.1.call-start = ((), (), s32[]{:S(2)}) async-start(), calls=%async_computation.2 | async-start | bytes 278528 | tf_op jit(solution)/shard_map/reduce_scatter | solution.py:96
  150.9 0.7 copy-start.1
Sparse Core Ops, SparseCore 0:
  26.0 75.8 all-gather.2
  151.8 53.8 reduce-scatter.1
where the time goes:
time: 215 us; the launch traced here: 214 us
  waiting for transfers between devices  127 us (59%)
  matrix products  38.8 us (18%)
  blocking collectives  17.6 us (8%)
  between operations  14.1 us (7%)
  other arithmetic  9.49 us (4%)
  local copies, waits for them, and re-layouts  6.28 us (3%)
    all_gather x1, waiting for transfers between devices, local(): lax.all_gather(fitted, ('spin', 'orb'), axis=1, tiled=True)  73 us
    reduce_scatter x1, waiting for transfers between devices, local(): lax.psum_scatter(density_terms[None], 'orb', scatter_dimension=1, tiled=T...  54 us
    dot_general x8, matrix products, pair_terms(): jnp.einsum('ijab,jbq->iaq', amplitude, right_block, preferred_element_typ...  20.6 us
    all_to_all x1, blocking collectives, local(): lax.all_to_all(integrals, 'orb', split_axis=1, concat_axis=3, tiled=True)  17.6 us
    dot_general x8, matrix products, pair_terms(): jnp.einsum('iaq,jbq->ijab', left_block, right_block, preferred_element_ty...  13.9 us
    add x8, other arithmetic, pair_terms(): e_left[:, None, None, None] + e_right[None, :, None, None]  5.11 us
  transfers between devices with their start and end apart: 2, of which 2 were waited for; matrix products, arithmetic and copies ran while one was open for 1% of the time, Pallas kernels for 0%

commit v1 on v0

v1 whole, which is shorter than its diff:
```python
import functools

import jax
import jax.numpy as jnp
import numpy as np
from jax import lax
from jax.experimental import pallas as pl
from jax.experimental.pallas import tpu as pltpu
from jax.sharding import PartitionSpec as P

VMEM_LIMIT = 48 * 1024 * 1024
NN = (((1,), (0,)), ((), ()))
NT = (((1,), (1,)), ((), ()))
TN = (((0,), (0,)), ((), ()))


def dot(left, right, dims):
    return lax.dot_general(left, right, dims, preferred_element_type=jnp.float32)


def chip_ring(orb_count):
    chips = orb_count // 2
    order = list(range(0, chips, 2)) + list(range(chips - 1 - chips % 2, 0, -2))
    following = {order[r]: order[(r + 1) % chips] for r in range(chips)}
    return order, following


def ring_moves(orb_count):
    _, following = chip_ring(orb_count)
    forward = [(2 * p, 2 * q) for p, q in following.items()]
    backward = [(2 * q + 1, 2 * p + 1) for p, q in following.items()]
    return forward + backward


def slice_sources(orb_count):
    order, _ = chip_ring(orb_count)
    chips = len(order)
    place = {chip: r for r, chip in enumerate(order)}
    table = []
    for device in range(orb_count):
        chip, core = device // 2, device % 2
        sources = [device, device ^ 1]
        for step in range(1, chips // 2 + 1):
            ahead = order[(place[chip] + (step if core else -step)) % chips]
            behind = order[(place[chip] - (step if core else -step)) % chips]
            if 2 * step == chips:
                sources += [2 * ahead + core, 2 * behind + 1 - core]
            else:
                sources += [2 * ahead + core, 2 * ahead + 1 - core]
                sources += [2 * behind + 1 - core, 2 * behind + core]
        table.append(sources)
    return np.asarray(table, np.int32)


def gather_slices(own, orb_count):
    moves = ring_moves(orb_count)
    swap = [(d, d ^ 1) for d in range(orb_count)]
    chips = orb_count // 2
    lanes = [own, lax.ppermute(own, "orb", swap)]
    gathered = list(lanes)
    for step in range(1, chips // 2 + 1):
        if 2 * step == chips:
            lanes = lanes[:1]
        lanes = [lax.ppermute(lane, "orb", moves) for lane in lanes]
        swapped = lax.ppermute(jnp.stack(lanes), "orb", swap)
        gathered += lanes + [swapped[n] for n in range(len(lanes))]
    return gathered


def fit_kernel(factor_ref, *refs):
    slices, out_ref = refs[:-1], refs[-1]
    for g in range(out_ref.shape[0]):
        raw = jnp.concatenate([piece[g] for piece in slices], axis=0)
        out_ref[g] = dot(factor_ref[...], raw, NN).astype(out_ref.dtype)


def fit(factor, slices, group):
    count, _, virt = slices[0].shape
    naux = factor.shape[0]
    return pl.pallas_call(
        fit_kernel,
        grid=(count // group,),
        in_specs=[pl.BlockSpec(factor.shape, lambda j: (0, 0))]
        + [pl.BlockSpec((group,) + s.shape[1:], lambda j: (j, 0, 0)) for s in slices],
        out_specs=pl.BlockSpec((group, naux, virt), lambda j: (j, 0, 0)),
        out_shape=jax.ShapeDtypeStruct((count, naux, virt), jnp.bfloat16),
        compiler_params=pltpu.CompilerParams(vmem_limit_bytes=VMEM_LIMIT),
        name="fit",
    )(factor, *slices)


def same_kernel(own_ref, pair_ref, own_block, blocks, v_col, v_row, gamma_ref, dens_ref, left):
    step = pl.program_id(0)

    @pl.when(step == 0)
    def _():
        left[...] = own_block[0].T
        gamma_ref[...] = jnp.zeros_like(gamma_ref)
        dens_ref[...] = jnp.zeros_like(dens_ref)

    group = blocks.shape[0]
    for g in range(group):
        right = blocks[g]
        coupling = dot(left[...], right, NN)
        coupling = coupling - coupling.T
        denominator = (pair_ref[step * group + g] - v_col[...]) - v_row[...]
        amplitude = (coupling / denominator).astype(jnp.bfloat16)
        gamma_ref[...] += dot(amplitude, right, NT)
        dens_ref[...] += 0.5 * dot(amplitude, amplitude, NT)


def same_spin(fitted, own_index, pair_energy, virt, group):
    count, naux, nv = fitted.shape
    whole = lambda shape: pl.BlockSpec(shape, lambda j, *_: (0,) * len(shape))
    return pl.pallas_call(
        same_kernel,
        grid_spec=pltpu.PrefetchScalarGridSpec(
            num_scalar_prefetch=2,
            grid=(count // group,),
            in_specs=[
                pl.BlockSpec((1, naux, nv), lambda j, own, pair: (own[0], 0, 0)),
                pl.BlockSpec((group, naux, nv), lambda j, own, pair: (j, 0, 0)),
                whole((nv, 1)),
                whole((1, nv)),
            ],
            out_specs=[whole((nv, naux)), whole((nv, nv))],
            scratch_shapes=[pltpu.VMEM((nv, naux), jnp.bfloat16)],
        ),
        out_shape=[
            jax.ShapeDtypeStruct((nv, naux), jnp.float32),
            jax.ShapeDtypeStruct((nv, nv), jnp.float32),
        ],
        compiler_params=pltpu.CompilerParams(vmem_limit_bytes=VMEM_LIMIT),
        name="same_spin",
    )(own_index, pair_energy, fitted, fitted, virt[:, None], virt[None, :])


def opposite_kernel(pair_ref, factor, raw, blocks, v_col, v_row, dens_in, gamma_ref, dens_ref, left):
    step = pl.program_id(0)

    @pl.when(step == 0)
    def _():
        left[...] = dot(factor[...], raw[...], NN).astype(left.dtype).T
        gamma_ref[...] = jnp.zeros_like(gamma_ref)
        dens_ref[...] = dens_in[...]

    group = blocks.shape[0]
    for g in range(group):
        right = blocks[g]
        coupling = dot(left[...], right, NN)
        denominator = (pair_ref[step * group + g] - v_col[...]) - v_row[...]
        amplitude = (coupling / denominator).astype(jnp.bfloat16)
        gamma_ref[...] += dot(amplitude, right, NT)
        dens_ref[...] += dot(amplitude, amplitude, TN)


def opposite_spin(fitted, factor, raw, pair_energy, virt_left, virt_right, dens, group):
    count, naux, nv = fitted.shape
    whole = lambda shape: pl.BlockSpec(shape, lambda j, *_: (0,) * len(shape))
    return pl.pallas_call(
        opposite_kernel,
        grid_spec=pltpu.PrefetchScalarGridSpec(
            num_scalar_prefetch=1,
            grid=(count // group,),
            in_specs=[
                whole(factor.shape),
                whole(raw.shape),
                pl.BlockSpec((group, naux, nv), lambda j, pair: (j, 0, 0)),
                whole((nv, 1)),
                whole((1, nv)),
                whole((nv, nv)),
            ],
            out_specs=[whole((nv, naux)), whole((nv, nv))],
            scratch_shapes=[pltpu.VMEM((nv, naux), jnp.bfloat16)],
        ),
        out_shape=[
            jax.ShapeDtypeStruct((nv, naux), jnp.float32),
            jax.ShapeDtypeStruct((nv, nv), jnp.float32),
        ],
        compiler_params=pltpu.CompilerParams(vmem_limit_bytes=VMEM_LIMIT),
        name="opposite_spin",
    )(pair_energy, factor, raw, fitted, virt_left[:, None], virt_right[None, :], dens)


def reduce_rows(total, orb_count):
    index = lax.axis_index("orb")
    bits = orb_count.bit_length() - 1
    rows = total.reshape((2,) * bits + (total.shape[0] // orb_count, total.shape[1]))
    for bit in range(bits):
        axis = bits - 1 - bit
        mine = (index >> bit) & 1
        moves = [(d, d ^ (1 << bit)) for d in range(orb_count)]
        kept = lax.dynamic_index_in_dim(rows, mine, axis, keepdims=False)
        sent = lax.dynamic_index_in_dim(rows, 1 - mine, axis, keepdims=False)
        rows = kept + lax.ppermute(sent, "orb", moves)
    return rows


def local(integrals, metric_factor, occ_energy, virt_energy, orb_count):
    spin_index = lax.axis_index("spin")
    orbit_index = lax.axis_index("orb")
    other_spin = 1 - spin_index
    pick = lambda array, n: lax.dynamic_index_in_dim(array, n, 0, keepdims=False)
    occ_same, occ_other = pick(occ_energy, spin_index), pick(occ_energy, other_spin)
    virt_same, virt_other = pick(virt_energy, spin_index), pick(virt_energy, other_spin)
    across = [(0, 1), (1, 0)]

    own = jnp.swapaxes(integrals[0], 1, 2)
    occupied, width, nv = own.shape
    naux = metric_factor.shape[0]
    sources = pick(jnp.asarray(slice_sources(orb_count)), orbit_index)
    factor = jnp.take(metric_factor.reshape(orb_count, width, naux), sources, axis=0)
    factor = factor.reshape(naux, naux).T

    slices = gather_slices(own, orb_count)
    own_row = [pick(s, orbit_index) for s in slices]
    early = len(slices) - 6 if len(slices) > 8 else len(slices) // 2
    raw_row = jnp.concatenate(
        [
            lax.ppermute(jnp.concatenate(own_row[:early]), "spin", across),
            lax.ppermute(jnp.concatenate(own_row[early:]), "spin", across),
        ]
    )
    if width % 16:
        slices = [jnp.concatenate(slices, axis=1)]
    fitted = fit(factor, slices, 2)

    own_energy, other_energy = pick(occ_same, orbit_index), pick(occ_other, orbit_index)
    gamma_same, dens = same_spin(fitted, orbit_index[None], own_energy + occ_same, virt_same, 2)
    gamma_other, dens = opposite_spin(
        fitted, factor, raw_row, other_energy + occ_same, virt_other, virt_same, dens, 2
    )
    returned = lax.ppermute(gamma_other, "spin", across)
    gamma = gamma_same + returned
    density = reduce_rows(dens, orb_count) / occupied
    return gamma[None, None], density[None]


def solution(mesh):
    return jax.shard_map(
        functools.partial(local, orb_count=mesh.shape["orb"]),
        mesh=mesh,
        in_specs=(P("spin", None, None, "orb"), P(), P(), P()),
        out_specs=(P("spin", "orb", None, None), P("spin", "orb", None)),
        check_vma=False,
    )
```

time: 215 us -> 78.9 us (0.37)
  waiting for transfers between devices: 127 us -> 22.5 us
  matrix products: 38.8 us -> 0 us
  Pallas kernels: 0 us -> 22 us
  starting transfers between devices: 0.08 us -> 21.9 us
  blocking collectives: 17.6 us -> 0 us
  between operations: 14.1 us -> 0.99 us
  other arithmetic: 9.49 us -> 4.36 us
    all_gather x1 -> x0, waiting for transfers between devices: 73 us -> none  [local(): lax.all_gather(fitted, ('spin', 'orb'), axis=1, tiled=True)]
    reduce_scatter x1 -> x0, waiting for transfers between devices: 54 us -> none  [local(): lax.psum_scatter(density_terms[None], 'orb', scatter_dimension=1, tiled=T...]
    dot_general x25 -> x0, matrix products: 38.8 us -> none  [the longest x8 20.6 us: pair_terms(): jnp.einsum('ijab,jbq->iaq', amplitude, right_block, preferred_element_typ...]
    ppermute x0 -> x19, waiting for transfers between devices: none -> 22.5 us  [the longest x7 9.29 us: gather_slices(): lanes = [lax.ppermute(lane, 'orb', moves) for lane in lanes]]
    pallas_call x0 -> x3, Pallas kernels: none -> 22 us  [the longest x1 9.04 us: same_spin(): pl.pallas_call(same_kernel, grid_spec=pltpu.PrefetchScalarGridSpec(num_sc...]
    ppermute x0 -> x19, starting transfers between devices: none -> 21.9 us  [the longest x7 12.6 us: gather_slices(): lanes = [lax.ppermute(lane, 'orb', moves) for lane in lanes]]
    all_to_all x1 -> x0, blocking collectives: 17.6 us -> none  [local(): lax.all_to_all(integrals, 'orb', split_axis=1, concat_axis=3, tiled=True)]
    add x8 -> x4, other arithmetic: 5.11 us -> 1.25 us  [the longest x1 1.22 us: local(): other_energy + occ_same]
  transfers between devices with their start and end apart: 2 -> 19, of which waited for: 2 -> 11; matrix products, arithmetic and copies ran while one was open for 1% -> 10% of each run, Pallas kernels for 0% -> 18%
where the time goes in v1:
time: 78.9 us; the launch traced here: 78.6 us
  waiting for transfers between devices  22.5 us (29%)
  Pallas kernels  22 us (28%)
  starting transfers between devices  21.9 us (28%)
  local copies, waits for them, and re-layouts  6.82 us (9%)
  other arithmetic  4.36 us (6%)
  between operations  0.99 us (1%)
    ppermute x7, starting transfers between devices, gather_slices(): lanes = [lax.ppermute(lane, 'orb', moves) for lane in lanes]  12.6 us
    ppermute x7, waiting for transfers between devices, gather_slices(): lanes = [lax.ppermute(lane, 'orb', moves) for lane in lanes]  9.29 us
    pallas_call x1, Pallas kernels, same_spin(): pl.pallas_call(same_kernel, grid_spec=pltpu.PrefetchScalarGridSpec(num_sc...  9.04 us
    ppermute x4, waiting for transfers between devices, reduce_rows(): rows = kept + lax.ppermute(sent, 'orb', moves)  8.32 us
    pallas_call x1, Pallas kernels, opposite_spin(): pl.pallas_call(opposite_kernel, grid_spec=pltpu.PrefetchScalarGridSpec(nu...  7.52 us
    pallas_call x1, Pallas kernels, fit(): pl.pallas_call(fit_kernel, grid=(count // group,), in_specs=[pl.BlockSpec...  5.47 us
    ppermute x1, waiting for transfers between devices, local(): returned = lax.ppermute(gamma_other, 'spin', across)  4.88 us
    ppermute x4, starting transfers between devices, reduce_rows(): rows = kept + lax.ppermute(sent, 'orb', moves)  4.87 us
  transfers between devices with their start and end apart: 19, of which 11 were waited for; matrix products, arithmetic and copies ran while one was open for 10% of the time, Pallas kernels for 18%

profile of v1, /device:TPU:0, one launch (start us, length us, event | category | flops | bytes accessed | tf_op | source)
XLA Modules:
  0.0 78.6 jit_solution(17740102556533018235)
XLA Ops:
  0.6 0.0 copy-start
  0.6 0.5 collective-permute-start
  1.2 2.6 %collective-permute-start.1 = (bf16[16,32,256]{2,1,0:T(8,128)(2,1)}, bf16[16,32,256]{2,1,0:T(8,128)(2,1)S(1)}, u32[]{:S(2)}, u32[]{:S(2)}) collective-permute-start(bf16[16,32,256]{2,1,0:T(8,128)(2,1)} %bitcast.113), channel_id=1, source_target_pairs={{0,4},{4,8},{8,12},{12,14},{14,10},{10,6},{6,2},{2,0},{5,1},{9,5},... | collective-permute-start | bytes 786440 | tf_op jit(solution)/shard_map/ppermute | solution.py:64
  3.8 0.7 fusion.3
  4.5 0.7 compare_and_fusion
  5.2 0.6 gather_fusion
  5.8 0.2 copy.7
  6.0 0.1 broadcast_in_dim.32
  6.1 0.1 broadcast_in_dim.33
  6.2 0.0 collective-permute-done.refs_1_
  6.2 1.6 %collective-permute-start.2 = (bf16[16,32,256]{2,1,0:T(8,128)(2,1)S(1)}, bf16[16,32,256]{2,1,0:T(8,128)(2,1)S(1)}, u32[]{:S(2)}, u32[]{:S(2)}) collective-permute-start(bf16[16,32,256]{2,1,0:T(8,128)(2,1)S(1)} %collective-permute-done.refs_1_), channel_id=1, source_target_pairs={{0,4},{4,8},{8,12},{12,14},{14,10},{10,6},{6,2},{2,0},{5,1},{9,5},... | collective-permute-start | bytes 786440 | tf_op jit(solution)/shard_map/ppermute | solution.py:64
  7.8 0.5 collective-permute-done.1.refs_2_
  8.3 2.1 %collective-permute-start.4 = (bf16[16,32,256]{2,1,0:T(8,128)(2,1)S(1)}, bf16[16,32,256]{2,1,0:T(8,128)(2,1)S(1)}, u32[]{:S(2)}, u32[]{:S(2)}) collective-permute-start(bf16[16,32,256]{2,1,0:T(8,128)(2,1)S(1)} %collective-permute-done.1.refs_2_), channel_id=1, source_target_pairs={{0,4},{4,8},{8,12},{12,14},{14,10},{10,6},{6,2},{2,0},{5,1},{9,5},... | collective-permute-start | bytes 786440 | tf_op jit(solution)/shard_map/ppermute | solution.py:64
  10.4 0.8 fusion.2
  11.1 0.1 copy.8.v_col
  11.3 0.1 copy.9.v_col
  11.4 1.3 %fusion.7 = (f32[1,1]{1,0:T(1,128)}, f32[1,1]{1,0:T(1,128)}) fusion(f32[2,16]{1,0:T(2,128)} %param.7, s32[]{:T(128)S(6)} %select_n.97, s32[]{:T(128)S(6)} %select_n.92, s32[]{:T(128)S(6)} %select_n.90), kind=kLoop, calls=%fused_computation.56 | loop fusion | bytes 28 | tf_op jit(solution)/shard_map/jit(dynamic_index_in_dim)/dynamic_slice | solution.py:203
  12.8 0.7 constant_dynamic-update-slice_fusion.9
  13.5 0.0 collective-permute-done.2.refs_3_
  13.5 1.6 %collective-permute-start.5 = (bf16[16,32,256]{2,1,0:T(8,128)(2,1)S(1)}, bf16[16,32,256]{2,1,0:T(8,128)(2,1)S(1)}, u32[]{:S(2)}, u32[]{:S(2)}) collective-permute-start(bf16[16,32,256]{2,1,0:T(8,128)(2,1)S(1)} %collective-permute-done.2.refs_3_), channel_id=1, source_target_pairs={{0,4},{4,8},{8,12},{12,14},{14,10},{10,6},{6,2},{2,0},{5,1},{9,5},... | collective-permute-start | bytes 786440 | tf_op jit(solution)/shard_map/ppermute | solution.py:64
  15.1 0.3 collective-permute-done.4.refs_6_
  15.4 1.6 %collective-permute-start.7 = (bf16[16,32,256]{2,1,0:T(8,128)(2,1)S(1)}, bf16[16,32,256]{2,1,0:T(8,128)(2,1)S(1)}, u32[]{:S(2)}, u32[]{:S(2)}) collective-permute-start(bf16[16,32,256]{2,1,0:T(8,128)(2,1)S(1)} %collective-permute-done.4.refs_6_), channel_id=1, source_target_pairs={{0,4},{4,8},{8,12},{12,14},{14,10},{10,6},{6,2},{2,0},{5,1},{9,5},... | collective-permute-start | bytes 786440 | tf_op jit(solution)/shard_map/ppermute | solution.py:64
  16.9 0.1 pad_maximum_fusion
  17.0 0.1 collective-permute-start.3
  17.1 2.8 %collective-permute-done.5.refs_7_ = bf16[16,32,256]{2,1,0:T(8,128)(2,1)S(1)} collective-permute-done((bf16[16,32,256]{2,1,0:T(8,128)(2,1)S(1)}, bf16[16,32,256]{2,1,0:T(8,128)(2,1)S(1)}, u32[]{:S(2)}, u32[]{:S(2)}) %collective-permute-start.5) | collective-permute-done | bytes 262176 | tf_op jit(solution)/shard_map/ppermute | solution.py:64
  19.9 1.6 %collective-permute-start.8 = (bf16[16,32,256]{2,1,0:T(8,128)(2,1)S(1)}, bf16[16,32,256]{2,1,0:T(8,128)(2,1)S(1)}, u32[]{:S(2)}, u32[]{:S(2)}) collective-permute-start(bf16[16,32,256]{2,1,0:T(8,128)(2,1)S(1)} %collective-permute-done.5.refs_7_), channel_id=1, source_target_pairs={{0,4},{4,8},{8,12},{12,14},{14,10},{10,6},{6,2},{2,0},{5,1},{9,5},... | collective-permute-start | bytes 786440 | tf_op jit(solution)/shard_map/ppermute | solution.py:64
  21.5 1.2 %collective-permute-done.7.refs_10_ = bf16[16,32,256]{2,1,0:T(8,128)(2,1)S(1)} collective-permute-done((bf16[16,32,256]{2,1,0:T(8,128)(2,1)S(1)}, bf16[16,32,256]{2,1,0:T(8,128)(2,1)S(1)}, u32[]{:S(2)}, u32[]{:S(2)}) %collective-permute-start.7) | collective-permute-done | bytes 262176 | tf_op jit(solution)/shard_map/ppermute | solution.py:64
  22.7 1.6 %collective-permute-start.10 = (bf16[16,32,256]{2,1,0:T(8,128)(2,1)S(1)}, bf16[16,32,256]{2,1,0:T(8,128)(2,1)S(1)}, u32[]{:S(2)}, u32[]{:S(2)}) collective-permute-start(bf16[16,32,256]{2,1,0:T(8,128)(2,1)S(1)} %collective-permute-done.7.refs_10_), channel_id=1, source_target_pairs={{0,4},{4,8},{8,12},{12,14},{14,10},{10,6},{6,2},{2,0},{5,1},{9,5},... | collective-permute-start | bytes 786440 | tf_op jit(solution)/shard_map/ppermute | solution.py:64
  24.3 0.1 pad_maximum_fusion.1
  24.3 0.1 collective-permute-start.6
  24.4 1.8 %collective-permute-done.8.refs_11_ = bf16[16,32,256]{2,1,0:T(8,128)(2,1)S(1)} collective-permute-done((bf16[16,32,256]{2,1,0:T(8,128)(2,1)S(1)}, bf16[16,32,256]{2,1,0:T(8,128)(2,1)S(1)}, u32[]{:S(2)}, u32[]{:S(2)}) %collective-permute-start.8) | collective-permute-done | bytes 262176 | tf_op jit(solution)/shard_map/ppermute | solution.py:64
  26.3 0.1 pad_maximum_fusion.2
  26.3 0.1 collective-permute-start.9
  26.4 2.7 %collective-permute-done.10.refs_14_ = bf16[16,32,256]{2,1,0:T(8,128)(2,1)S(1)} collective-permute-done((bf16[16,32,256]{2,1,0:T(8,128)(2,1)S(1)}, bf16[16,32,256]{2,1,0:T(8,128)(2,1)S(1)}, u32[]{:S(2)}, u32[]{:S(2)}) %collective-permute-start.10) | collective-permute-done | bytes 262176 | tf_op jit(solution)/shard_map/ppermute | solution.py:64
  29.1 0.0 collective-permute-start.11
  29.1 0.0 collective-permute-done.3
  29.1 0.1 fusion.5
  29.3 0.0 collective-permute-done.6
  29.3 0.1 fusion.4
  29.5 1.6 %collective-permute-start.12 = (bf16[320,256]{1,0:T(8,128)(2,1)S(1)}, bf16[320,256]{1,0:T(8,128)(2,1)S(1)}, u32[]{:S(2)}, u32[]{:S(2)}) collective-permute-start(bf16[320,256]{1,0:T(8,128)(2,1)S(1)} %constant_dynamic-update-slice_fusion), channel_id=1, source_target_pairs={{0,16},{16,0},{1,17},{17,1},{2,18},{18,2},{3,19},{19,3},{4,20},{20... | collective-permute-start | bytes 491528 | tf_op jit(solution)/shard_map/ppermute | solution.py:220
  31.0 0.0 collective-permute-done.9
  31.0 0.1 fusion.6
  31.2 0.0 collective-permute-done.11
  31.2 0.9 %collective-permute-start.13 = (bf16[192,256]{1,0:T(8,128)(2,1)S(1)}, bf16[192,256]{1,0:T(8,128)(2,1)S(1)}, u32[]{:S(2)}, u32[]{:S(2)}) collective-permute-start(bf16[192,256]{1,0:T(8,128)(2,1)S(1)} %constant_dynamic-update-slice_fusion.10), channel_id=1, source_target_pairs={{0,16},{16,0},{1,17},{17,1},{2,18},{18,2},{3,19},{19,3},{4,20},{20... | collective-permute-start | bytes 294920 | tf_op jit(solution)/shard_map/ppermute | solution.py:221
  32.1 1.2 %add_bitcast_fusion.1 = (f32[16]{0:T(128)S(1)}, f32[16]{0:T(128)S(1)}) fusion(f32[]{:T(128)} %bitcast.27, f32[2,16]{1,0:T(2,128)S(1)} %copy-done.4, s32[]{:T(128)S(6)} %select_n.89, f32[]{:T(128)} %bitcast.1), kind=kLoop, calls=%fused_computation.45 | loop fusion | flops 32 | bytes 204 | tf_op jit(solution)/shard_map/add | solution.py:231
  33.3 0.0 copy-done.3
  33.3 5.5 %fit.1.own_block.blocks = bf16[16,512,256]{2,1,0:T(8,128)(2,1)} custom-call(bf16[512,512]{1,0:T(8,128)(2,1)S(1)} %select_bitcast_fusion.factor_ref.factor, bf16[16,32,256]{2,1,0:T(8,128)(2,1)S(1)} %bitcast.114, bf16[16,32,256]{2,1,0:T(8,128)(2,1)S(1)} %collective-permute-done.refs_1_, bf16[16,32,256]{2,1,0:T(8,128)(2,1)S(1)} %collective-permute-done.1.refs_2_, ...), custom_call_target="tpu_custom_call" | custom-call | tf_op jit(solution)/shard_map/fit/pallas_call | solution.py:80
  38.8 2.2 %copy-done.1 = bf16[16,512,256]{2,1,0:T(8,128)(2,1)S(1)} copy-done((bf16[16,512,256]{2,1,0:T(8,128)(2,1)S(1)}, bf16[16,512,256]{2,1,0:T(8,128)(2,1)}, u32[]{:S(2)}) %copy-start.1) | copy-done | bytes 4194328
  41.0 9.0 %same_spin.1 = (f32[256,512]{1,0:T(8,128)S(1)}, f32[256,256]{1,0:T(8,128)S(1)}) custom-call(s32[1]{0:T(128)} %bitcast.own_ref, f32[16]{0:T(128)S(1)} %get-tuple-element.27.pair_ref, bf16[16,512,256]{2,1,0:T(8,128)(2,1)S(1)} %copy-done.1, bf16[16,512,256]{2,1,0:T(8,128)(2,1)S(1)} %copy-done.1, f32[256,1]{1,0:T(8,128)S(1)} %copy.8.v_col, ...), custom_call_target="tpu_custom_call" | custom-call | tf_op jit(solution)/shard_map/same_spin/pallas_call | solution.py:115
  50.0 0.0 collective-permute-done.12
  50.1 0.0 collective-permute-done.13
  50.1 7.5 %opposite_spin.1 = (f32[256,512]{1,0:T(8,128)S(1)}, f32[256,256]{1,0:T(8,128)S(1)}) custom-call(f32[16]{0:T(128)S(1)} %get-tuple-element.26.pair_ref, bf16[512,512]{1,0:T(8,128)(2,1)S(1)} %select_bitcast_fusion.factor_ref.factor, bf16[512,256]{1,0:T(8,128)(2,1)S(1)} %pad_maximum_fusion.3.raw, bf16[16,512,256]{2,1,0:T(8,128)(2,1)S(1)} %copy-done.2, ...), custom_call_target="tpu_custom_call" | custom-call | tf_op jit(solution)/shard_map/opposite_spin/pallas_call | solution.py:160
  57.7 0.1 collective-permute-start.15
  57.8 1.3 %collective-permute-done.15 = f32[2,2,2,16,256]{4,3,1,0,2:T(8,128)S(1)} collective-permute-done((f32[2,2,2,16,256]{4,3,1,0,2:T(8,128)S(1)}, f32[2,2,2,16,256]{4,3,1,0,2:T(8,128)S(1)}, u32[]{:S(2)}, u32[]{:S(2)}) %collective-permute-start.15) | collective-permute-done | bytes 131104 | tf_op jit(solution)/shard_map/ppermute | solution.py:195
  59.1 0.5 collective-permute-start.16
  59.7 3.8 %collective-permute-done.16 = f32[2,2,16,256]{3,2,1,0:T(8,128)S(1)} collective-permute-done((f32[2,2,16,256]{3,2,1,0:T(8,128)S(1)}, f32[2,2,16,256]{3,2,1,0:T(8,128)S(1)}, u32[]{:S(2)}, u32[]{:S(2)}) %collective-permute-start.16) | collective-permute-done | bytes 65568 | tf_op jit(solution)/shard_map/ppermute | solution.py:195
  63.5 1.6 %collective-permute-start.17 = (f32[2,16,256]{2,1,0:T(8,128)S(1)}, f32[2,16,256]{2,1,0:T(8,128)S(1)}, u32[]{:S(2)}, u32[]{:S(2)}) collective-permute-start(f32[2,16,256]{2,1,0:T(8,128)S(1)} %dynamic-slice_bitcast_fusion.1), channel_id=1, source_target_pairs={{0,4},{1,5},{2,6},{3,7},{4,0},{5,1},{6,2},{7,3},{8,12},{9,13},{10,... | collective-permute-start | bytes 98312 | tf_op jit(solution)/shard_map/ppermute | solution.py:195
  65.1 1.2 %collective-permute-start.14 = (f32[256,512]{1,0:T(8,128)S(1)}, f32[256,512]{1,0:T(8,128)S(1)}, u32[]{:S(2)}, u32[]{:S(2)}) collective-permute-start(f32[256,512]{1,0:T(8,128)S(1)} %get-tuple-element.8), channel_id=1, source_target_pairs={{0,16},{16,0},{1,17},{17,1},{2,18},{18,2},{3,19},{19,3},{4,20},{20... | collective-permute-start | bytes 1572872 | tf_op jit(solution)/shard_map/ppermute | solution.py:233
  66.4 1.1 %collective-permute-done.17 = f32[2,16,256]{2,1,0:T(8,128)S(1)} collective-permute-done((f32[2,16,256]{2,1,0:T(8,128)S(1)}, f32[2,16,256]{2,1,0:T(8,128)S(1)}, u32[]{:S(2)}, u32[]{:S(2)}) %collective-permute-start.17) | collective-permute-done | bytes 32800 | tf_op jit(solution)/shard_map/ppermute | solution.py:195
  67.5 2.6 %collective-permute-start.18 = (f32[16,256]{1,0:T(8,128)S(1)}, f32[16,256]{1,0:T(8,128)S(1)}, u32[]{:S(2)}, u32[]{:S(2)}) collective-permute-start(f32[16,256]{1,0:T(8,128)S(1)} %dynamic-slice_bitcast_fusion.2), channel_id=1, source_target_pairs={{0,8},{1,9},{2,10},{3,11},{4,12},{5,13},{6,14},{7,15},{8,0},{9,1},... | collective-permute-start | bytes 49160 | tf_op jit(solution)/shard_map/ppermute | solution.py:195
  70.2 2.1 %collective-permute-done.18 = f32[16,256]{1,0:T(8,128)S(1)} collective-permute-done((f32[16,256]{1,0:T(8,128)S(1)}, f32[16,256]{1,0:T(8,128)S(1)}, u32[]{:S(2)}, u32[]{:S(2)}) %collective-permute-start.18) | collective-permute-done | bytes 16416 | tf_op jit(solution)/shard_map/ppermute | solution.py:195
  72.2 0.6 fusion.1
  72.8 4.9 %collective-permute-done.14 = f32[256,512]{1,0:T(8,128)S(1)} collective-permute-done((f32[256,512]{1,0:T(8,128)S(1)}, f32[256,512]{1,0:T(8,128)S(1)}, u32[]{:S(2)}, u32[]{:S(2)}) %collective-permute-start.14) | collective-permute-done | bytes 524320 | tf_op jit(solution)/shard_map/ppermute | solution.py:233
  77.7 0.9 %add_bitcast_fusion = f32[1,1,256,512]{3,2,1,0:T(8,128)} fusion(f32[256,512]{1,0:T(8,128)S(1)} %get-tuple-element.6, f32[256,512]{1,0:T(8,128)S(1)} %collective-permute-done.14), kind=kLoop, calls=%fused_computation.4 | loop fusion | flops 131072 | bytes 1572864 | tf_op jit(solution)/shard_map/broadcast_in_dim | solution.py:236
  (33 shorter events, 0.3 us)
Async XLA Ops:
  0.6 4.6 %copy-start = (bf16[512,512]{1,0:T(8,128)(2,1)S(1)}, bf16[512,512]{1,0:T(8,128)(2,1)}, u32[]{:S(2)}) copy-start(bf16[512,512]{1,0:T(8,128)(2,1)} %param.6) | copy-start | bytes 1572868
  0.6 5.5 %collective-permute-start = (bf16[16,32,256]{2,1,0:T(8,128)(2,1)}, bf16[16,32,256]{2,1,0:T(8,128)(2,1)S(1)}, u32[]{:S(2)}, u32[]{:S(2)}) collective-permute-start(bf16[16,32,256]{2,1,0:T(8,128)(2,1)} %bitcast.112), channel_id=1, source_target_pairs={{0,1},{1,0},{2,3},{3,2},{4,5},{5,4},{6,7},{7,6},{8,9},{9,8},{10,11... | collective-permute-start | bytes 786440 | tf_op jit(solution)/shard_map/ppermute | solution.py:59
  1.2 7.1 %collective-permute-start.1 = (bf16[16,32,256]{2,1,0:T(8,128)(2,1)}, bf16[16,32,256]{2,1,0:T(8,128)(2,1)S(1)}, u32[]{:S(2)}, u32[]{:S(2)}) collective-permute-start(bf16[16,32,256]{2,1,0:T(8,128)(2,1)} %bitcast.113), channel_id=1, source_target_pairs={{0,4},{4,8},{8,12},{12,14},{14,10},{10,6},{6,2},{2,0},{5,1},{9,5},... | collective-permute-start | bytes 786440 | tf_op jit(solution)/shard_map/ppermute | solution.py:64
  6.2 7.3 %collective-permute-start.2 = (bf16[16,32,256]{2,1,0:T(8,128)(2,1)S(1)}, bf16[16,32,256]{2,1,0:T(8,128)(2,1)S(1)}, u32[]{:S(2)}, u32[]{:S(2)}) collective-permute-start(bf16[16,32,256]{2,1,0:T(8,128)(2,1)S(1)} %collective-permute-done.refs_1_), channel_id=1, source_target_pairs={{0,4},{4,8},{8,12},{12,14},{14,10},{10,6},{6,2},{2,0},{5,1},{9,5},... | collective-permute-start | bytes 786440 | tf_op jit(solution)/shard_map/ppermute | solution.py:64
  8.3 7.1 %collective-permute-start.4 = (bf16[16,32,256]{2,1,0:T(8,128)(2,1)S(1)}, bf16[16,32,256]{2,1,0:T(8,128)(2,1)S(1)}, u32[]{:S(2)}, u32[]{:S(2)}) collective-permute-start(bf16[16,32,256]{2,1,0:T(8,128)(2,1)S(1)} %collective-permute-done.1.refs_2_), channel_id=1, source_target_pairs={{0,4},{4,8},{8,12},{12,14},{14,10},{10,6},{6,2},{2,0},{5,1},{9,5},... | collective-permute-start | bytes 786440 | tf_op jit(solution)/shard_map/ppermute | solution.py:64
  13.5 18.6 %copy-start.4 = (f32[2,16]{1,0:T(2,128)S(1)}, f32[2,16]{1,0:T(2,128)}, u32[]{:S(2)}) copy-start(f32[2,16]{1,0:T(2,128)} %param.7) | copy-start | bytes 388
  13.5 6.4 %collective-permute-start.5 = (bf16[16,32,256]{2,1,0:T(8,128)(2,1)S(1)}, bf16[16,32,256]{2,1,0:T(8,128)(2,1)S(1)}, u32[]{:S(2)}, u32[]{:S(2)}) collective-permute-start(bf16[16,32,256]{2,1,0:T(8,128)(2,1)S(1)} %collective-permute-done.2.refs_3_), channel_id=1, source_target_pairs={{0,4},{4,8},{8,12},{12,14},{14,10},{10,6},{6,2},{2,0},{5,1},{9,5},... | collective-permute-start | bytes 786440 | tf_op jit(solution)/shard_map/ppermute | solution.py:64
  15.1 18.2 %copy-start.3 = (bf16[1,16,256,32]{2,3,1,0:T(8,128)(2,1)S(1)}, bf16[1,16,256,32]{2,3,1,0:T(8,128)(2,1)}, u32[]{:S(2)}) copy-start(bf16[1,16,256,32]{2,3,1,0:T(8,128)(2,1)} %param.5) | copy-start | bytes 786436
  15.4 7.3 %collective-permute-start.7 = (bf16[16,32,256]{2,1,0:T(8,128)(2,1)S(1)}, bf16[16,32,256]{2,1,0:T(8,128)(2,1)S(1)}, u32[]{:S(2)}, u32[]{:S(2)}) collective-permute-start(bf16[16,32,256]{2,1,0:T(8,128)(2,1)S(1)} %collective-permute-done.4.refs_6_), channel_id=1, source_target_pairs={{0,4},{4,8},{8,12},{12,14},{14,10},{10,6},{6,2},{2,0},{5,1},{9,5},... | collective-permute-start | bytes 786440 | tf_op jit(solution)/shard_map/ppermute | solution.py:64
  17.0 12.1 %collective-permute-start.3 = (bf16[2,16,32,256]{3,2,1,0:T(8,128)(2,1)S(1)}, bf16[2,16,32,256]{3,2,1,0:T(8,128)(2,1)S(1)}, u32[]{:S(2)}, u32[]{:S(2)}) collective-permute-start(bf16[2,16,32,256]{3,2,1,0:T(8,128)(2,1)S(1)} %pad_maximum_fusion), channel_id=1, source_target_pairs={{0,1},{1,0},{2,3},{3,2},{4,5},{5,4},{6,7},{7,6},{8,9},{9,8},{10,11... | collective-permute-start | bytes 1572872 | tf_op jit(solution)/shard_map/ppermute | solution.py:65
  19.9 6.4 %collective-permute-start.8 = (bf16[16,32,256]{2,1,0:T(8,128)(2,1)S(1)}, bf16[16,32,256]{2,1,0:T(8,128)(2,1)S(1)}, u32[]{:S(2)}, u32[]{:S(2)}) collective-permute-start(bf16[16,32,256]{2,1,0:T(8,128)(2,1)S(1)} %collective-permute-done.5.refs_7_), channel_id=1, source_target_pairs={{0,4},{4,8},{8,12},{12,14},{14,10},{10,6},{6,2},{2,0},{5,1},{9,5},... | collective-permute-start | bytes 786440 | tf_op jit(solution)/shard_map/ppermute | solution.py:64
  22.7 6.4 %collective-permute-start.10 = (bf16[16,32,256]{2,1,0:T(8,128)(2,1)S(1)}, bf16[16,32,256]{2,1,0:T(8,128)(2,1)S(1)}, u32[]{:S(2)}, u32[]{:S(2)}) collective-permute-start(bf16[16,32,256]{2,1,0:T(8,128)(2,1)S(1)} %collective-permute-done.7.refs_10_), channel_id=1, source_target_pairs={{0,4},{4,8},{8,12},{12,14},{14,10},{10,6},{6,2},{2,0},{5,1},{9,5},... | collective-permute-start | bytes 786440 | tf_op jit(solution)/shard_map/ppermute | solution.py:64
  24.3 5.0 %collective-permute-start.6 = (bf16[2,16,32,256]{3,2,1,0:T(8,128)(2,1)S(1)}, bf16[2,16,32,256]{3,2,1,0:T(8,128)(2,1)S(1)}, u32[]{:S(2)}, u32[]{:S(2)}) collective-permute-start(bf16[2,16,32,256]{3,2,1,0:T(8,128)(2,1)S(1)} %pad_maximum_fusion.1), channel_id=1, source_target_pairs={{0,1},{1,0},{2,3},{3,2},{4,5},{5,4},{6,7},{7,6},{8,9},{9,8},{10,11... | collective-permute-start | bytes 1572872 | tf_op jit(solution)/shard_map/ppermute | solution.py:65
  26.3 4.7 %collective-permute-start.9 = (bf16[2,16,32,256]{3,2,1,0:T(8,128)(2,1)S(1)}, bf16[2,16,32,256]{3,2,1,0:T(8,128)(2,1)S(1)}, u32[]{:S(2)}, u32[]{:S(2)}) collective-permute-start(bf16[2,16,32,256]{3,2,1,0:T(8,128)(2,1)S(1)} %pad_maximum_fusion.2), channel_id=1, source_target_pairs={{0,1},{1,0},{2,3},{3,2},{4,5},{5,4},{6,7},{7,6},{8,9},{9,8},{10,11... | collective-permute-start | bytes 1572872 | tf_op jit(solution)/shard_map/ppermute | solution.py:65
  29.1 2.1 %collective-permute-start.11 = (bf16[1,16,32,256]{3,2,1,0:T(8,128)(2,1)S(1)}, bf16[1,16,32,256]{3,2,1,0:T(8,128)(2,1)S(1)}, u32[]{:S(2)}, u32[]{:S(2)}) collective-permute-start(bf16[1,16,32,256]{3,2,1,0:T(8,128)(2,1)S(1)} %bitcast.115), channel_id=1, source_target_pairs={{0,1},{1,0},{2,3},{3,2},{4,5},{5,4},{6,7},{7,6},{8,9},{9,8},{10,11... | collective-permute-start | bytes 786440 | tf_op jit(solution)/shard_map/ppermute | solution.py:65
  29.5 20.6 %collective-permute-start.12 = (bf16[320,256]{1,0:T(8,128)(2,1)S(1)}, bf16[320,256]{1,0:T(8,128)(2,1)S(1)}, u32[]{:S(2)}, u32[]{:S(2)}) collective-permute-start(bf16[320,256]{1,0:T(8,128)(2,1)S(1)} %constant_dynamic-update-slice_fusion), channel_id=1, source_target_pairs={{0,16},{16,0},{1,17},{17,1},{2,18},{18,2},{3,19},{19,3},{4,20},{20... | collective-permute-start | bytes 491528 | tf_op jit(solution)/shard_map/ppermute | solution.py:220
  31.2 18.8 %collective-permute-start.13 = (bf16[192,256]{1,0:T(8,128)(2,1)S(1)}, bf16[192,256]{1,0:T(8,128)(2,1)S(1)}, u32[]{:S(2)}, u32[]{:S(2)}) collective-permute-start(bf16[192,256]{1,0:T(8,128)(2,1)S(1)} %constant_dynamic-update-slice_fusion.10), channel_id=1, source_target_pairs={{0,16},{16,0},{1,17},{17,1},{2,18},{18,2},{3,19},{19,3},{4,20},{20... | collective-permute-start | bytes 294920 | tf_op jit(solution)/shard_map/ppermute | solution.py:221
  38.8 2.2 %copy-start.1 = (bf16[16,512,256]{2,1,0:T(8,128)(2,1)S(1)}, bf16[16,512,256]{2,1,0:T(8,128)(2,1)}, u32[]{:S(2)}) copy-start(bf16[16,512,256]{2,1,0:T(8,128)(2,1)} %fit.1.own_block.blocks) | copy-start | bytes 12582916
  41.0 9.1 %copy-start.2 = (bf16[16,512,256]{2,1,0:T(8,128)(2,1)S(1)}, bf16[16,512,256]{2,1,0:T(8,128)(2,1)}, u32[]{:S(2)}) copy-start(bf16[16,512,256]{2,1,0:T(8,128)(2,1)} %fit.1.own_block.blocks) | copy-start | bytes 12582916
  57.7 1.4 %collective-permute-start.15 = (f32[2,2,2,16,256]{4,3,1,0,2:T(8,128)S(1)}, f32[2,2,2,16,256]{4,3,1,0,2:T(8,128)S(1)}, u32[]{:S(2)}, u32[]{:S(2)}) collective-permute-start(f32[2,2,2,16,256]{4,3,1,0,2:T(8,128)S(1)} %bitcast.120), channel_id=1, source_target_pairs={{0,1},{1,0},{2,3},{3,2},{4,5},{5,4},{6,7},{7,6},{8,9},{9,8},{10,11... | collective-permute-start | bytes 393224 | tf_op jit(solution)/shard_map/ppermute | solution.py:195
  59.1 4.3 %collective-permute-start.16 = (f32[2,2,16,256]{3,2,1,0:T(8,128)S(1)}, f32[2,2,16,256]{3,2,1,0:T(8,128)S(1)}, u32[]{:S(2)}, u32[]{:S(2)}) collective-permute-start(f32[2,2,16,256]{3,2,1,0:T(8,128)S(1)} %dynamic-slice_bitcast_fusion), channel_id=1, source_target_pairs={{0,2},{1,3},{2,0},{3,1},{4,6},{5,7},{6,4},{7,5},{8,10},{9,11},{10,... | collective-permute-start | bytes 196616 | tf_op jit(solution)/shard_map/ppermute | solution.py:195
  63.5 4.0 %collective-permute-start.17 = (f32[2,16,256]{2,1,0:T(8,128)S(1)}, f32[2,16,256]{2,1,0:T(8,128)S(1)}, u32[]{:S(2)}, u32[]{:S(2)}) collective-permute-start(f32[2,16,256]{2,1,0:T(8,128)S(1)} %dynamic-slice_bitcast_fusion.1), channel_id=1, source_target_pairs={{0,4},{1,5},{2,6},{3,7},{4,0},{5,1},{6,2},{7,3},{8,12},{9,13},{10,... | collective-permute-start | bytes 98312 | tf_op jit(solution)/shard_map/ppermute | solution.py:195
  65.1 12.5 %collective-permute-start.14 = (f32[256,512]{1,0:T(8,128)S(1)}, f32[256,512]{1,0:T(8,128)S(1)}, u32[]{:S(2)}, u32[]{:S(2)}) collective-permute-start(f32[256,512]{1,0:T(8,128)S(1)} %get-tuple-element.8), channel_id=1, source_target_pairs={{0,16},{16,0},{1,17},{17,1},{2,18},{18,2},{3,19},{19,3},{4,20},{20... | collective-permute-start | bytes 1572872 | tf_op jit(solution)/shard_map/ppermute | solution.py:233
  67.5 4.7 %collective-permute-start.18 = (f32[16,256]{1,0:T(8,128)S(1)}, f32[16,256]{1,0:T(8,128)S(1)}, u32[]{:S(2)}, u32[]{:S(2)}) collective-permute-start(f32[16,256]{1,0:T(8,128)S(1)} %dynamic-slice_bitcast_fusion.2), channel_id=1, source_target_pairs={{0,8},{1,9},{2,10},{3,11},{4,12},{5,13},{6,14},{7,15},{8,0},{9,1},... | collective-permute-start | bytes 49160 | tf_op jit(solution)/shard_map/ppermute | solution.py:195

commit v2 on v1

--- a/solution.py
+++ b/solution.py
@@ -8,7 +8,8 @@
 from jax.experimental.pallas import tpu as pltpu
 from jax.sharding import PartitionSpec as P
 
-VMEM_LIMIT = 48 * 1024 * 1024
+VMEM_LIMIT = 20 * 1024 * 1024
+GROUP = 4
 NN = (((1,), (0,)), ((), ()))
 NT = (((1,), (1,)), ((), ()))
 TN = (((0,), (0,)), ((), ()))
@@ -63,8 +64,218 @@
             lanes = lanes[:1]
         lanes = [lax.ppermute(lane, "orb", moves) for lane in lanes]
         swapped = lax.ppermute(jnp.stack(lanes), "orb", swap)
-        gathered += lanes + [swapped[n] for n in range(len(lanes))]
+        gathered += lanes + [swapped]
     return gathered
+
+
+def pieces(refs, orbital):
+    for ref in refs:
+        if len(ref.shape) == 3:
+            yield ref[orbital]
+        else:
+            for lane in range(ref.shape[0]):
+                yield ref[lane, orbital]
+
+
+def order_factor(factor_ref, rows, orb_count):
+    own = lax.axis_index("orb")
+    chips, width = orb_count // 2, factor_ref.shape[0] // orb_count
+    chip, core = own // 2, own % 2
+    place = jnp.where(chip % 2 == 0, chip // 2, chips - (chip + 1) // 2)
+
+    def chip_at(distance):
+        there = (place + chips + jnp.where(core == 0, -distance, distance)) % chips
+        return jnp.where(2 * there < chips, 2 * there, 2 * (chips - there) - 1)
+
+    sources = [own, own ^ 1]
+    for step in range(1, chips // 2 + 1):
+        ahead, behind = 2 * chip_at(step), 2 * chip_at(-step)
+        if 2 * step == chips:
+            sources += [ahead + core, behind + 1 - core]
+        else:
+            sources += [ahead + core, ahead + 1 - core, behind + 1 - core, behind + core]
+    for n, source in enumerate(sources):
+        rows[n * width : (n + 1) * width] = factor_ref[pl.ds(pl.multiple_of(source * width, width), width)]
+    return rows[...].T
+
+
+def row_kernel(*refs):
+    *slices, out_ref = refs
+    out_ref[...] = jnp.concatenate(list(pieces(slices, lax.axis_index("orb"))), axis=0)
+
+
+def early_row_kernel(own_hbm, *refs):
+    *slices, out_ref, own_ref, arrived = refs
+    fetch = pltpu.make_async_copy(own_hbm, own_ref, arrived)
+    fetch.start()
+    fetch.wait()
+    out_ref[...] = jnp.concatenate(list(pieces([own_ref] + slices, lax.axis_index("orb"))), axis=0)
+
+
+def stack_kernel(lanes, *refs):
+    for n in range(lanes):
+        refs[-1][n] = refs[n][...]
+
+
+def energy_sums(virt_ref, left_spin, right_spin):
+    nv = virt_ref.shape[1]
+    left = jnp.broadcast_to(virt_ref[pl.ds(left_spin, 1)], (nv, nv)).T
+    return left + virt_ref[pl.ds(right_spin, 1)]
+
+
+def pair_energies(occ_ref, left_spin, right_spin, own):
+    left = occ_ref[pl.ds(left_spin, 1)]
+    chosen = lax.broadcasted_iota(jnp.int32, left.shape, 1) == own
+    return jnp.sum(jnp.where(chosen, left, 0.0), axis=1, keepdims=True) + occ_ref[pl.ds(right_spin, 1)]
+
+
+def amplitudes(coupling, occupied_pair, virtual_pair):
+    return (coupling / (occupied_pair - virtual_pair)).astype(jnp.bfloat16)
+
+
+def fit_same_kernel(orb_count, occ_ref, virt_ref, given_ref, *refs):
+    slices, (factor_ref, fitted_ref, gamma_ref, dens_ref) = refs[:-8], refs[-8:-4]
+    rows, left, sums, amp_ref = refs[-4:]
+    factor_ref[...] = order_factor(given_ref, rows, orb_count)
+    spin, own = lax.axis_index("spin"), lax.axis_index("orb")
+    count, nv = occ_ref.shape[1], virt_ref.shape[1]
+    sums[...] = energy_sums(virt_ref, spin, spin)
+    energies = pair_energies(occ_ref, spin, spin, own)
+    raw = jnp.concatenate(list(pieces(slices, own)), axis=0)
+    left[...] = dot(factor_ref[...], raw, NN).T.astype(left.dtype)
+    total = None
+    for start in range(0, count, GROUP):
+        members = range(start, start + GROUP)
+        raw = [jnp.concatenate(list(pieces(slices, j)), axis=0) for j in members]
+        fitted = dot(factor_ref[...], jnp.concatenate(raw, axis=1), NN).astype(fitted_ref.dtype)
+        columns = slice(start * nv, (start + GROUP) * nv)
+        fitted_ref[:, columns] = fitted
+        couplings = dot(left[...], fitted, NN)
+        amps = []
+        for n, j in enumerate(members):
+            coupling = couplings[:, n * nv : (n + 1) * nv]
+            amps.append(amplitudes(coupling - coupling.T, energies[:, j : j + 1], sums[...]))
+        amps = jnp.concatenate(amps, axis=1)
+        amp_ref[:, columns] = amps
+        term = dot(amps, amps, NT)
+        total = term if total is None else total + term
+    dens_ref[...] = 0.5 * total
+    gamma_ref[...] = dot(amp_ref[...], fitted_ref[...], NT)
+
+
+def opposite_all_kernel(
+    occ_ref, virt_ref, factor_ref, early_ref, late_ref, fitted_ref, dens_in,
+    gamma_ref, kept_ref, sent_ref, left, sums, dens, amp_ref,
+):
+    spin, own = lax.axis_index("spin"), lax.axis_index("orb")
+    count, nv = occ_ref.shape[1], virt_ref.shape[1]
+    sums[...] = energy_sums(virt_ref, 1 - spin, spin)
+    energies = pair_energies(occ_ref, 1 - spin, spin, own)
+    raw = jnp.concatenate([early_ref[...], late_ref[...]], axis=0)
+    left[...] = dot(factor_ref[...], raw, NN).T.astype(left.dtype)
+    total = dens_in[...]
+    for start in range(0, count, GROUP):
+        columns = slice(start * nv, (start + GROUP) * nv)
+        couplings = dot(left[...], fitted_ref[:, columns], NN)
+        amps = []
+        for n in range(GROUP):
+            energy = energies[:, start + n : start + n + 1]
+            amps.append(amplitudes(couplings[:, n * nv : (n + 1) * nv], energy, sums[...]))
+        amp_ref[:, columns] = jnp.concatenate(amps, axis=1)
+        stacked = jnp.concatenate(amps, axis=0)
+        total = total + dot(stacked, stacked, TN)
+    dens[...] = total / count
+    core = own % 2
+    chips, rows, _ = kept_ref.shape
+    for chip in range(chips):
+        for ref, lane in ((kept_ref, core), (sent_ref, 1 - core)):
+            first = pl.multiple_of((2 * chip + lane) * rows, rows)
+            ref[chip] = dens[pl.ds(first, rows)]
+    gamma_ref[...] = dot(amp_ref[...], fitted_ref[...], NT).astype(gamma_ref.dtype)
+
+
+def join_kernel(gamma_in, returned, kept_in, arrived, gamma_ref, kept_ref, sent_ref, total):
+    gamma_ref[...] = gamma_in[...] + returned[...].astype(jnp.float32)
+    total[...] = kept_in[...] + arrived[...]
+    far = lax.axis_index("orb") // (lax.axis_size("orb") // 2)
+    kept_ref[...] = total[far]
+    sent_ref[...] = total[1 - far]
+
+
+def vmem_call(kernel, name, operands, outs, scratch=(), flops=0, in_hbm=0, pin=True):
+    vmem, hbm = pl.BlockSpec(memory_space=pltpu.VMEM), pl.BlockSpec(memory_space=pltpu.HBM)
+    moved = sum(a.size * a.dtype.itemsize for a in operands)
+    if pin:
+        places = [pltpu.HBM] * in_hbm + [pltpu.VMEM] * (len(operands) - in_hbm)
+        operands = [pltpu.with_memory_space_constraint(*pair) for pair in zip(operands, places)]
+    return pl.pallas_call(
+        kernel,
+        in_specs=[hbm] * in_hbm + [vmem] * (len(operands) - in_hbm),
+        out_specs=[vmem] * len(outs),
+        out_shape=[pltpu.VMEM(*out) if pin else jax.ShapeDtypeStruct(*out) for out in outs],
+        scratch_shapes=[pltpu.VMEM(*s) if isinstance(s, tuple) else s for s in scratch],
+        compiler_params=pltpu.CompilerParams(vmem_limit_bytes=VMEM_LIMIT),
+        cost_estimate=pl.CostEstimate(flops=flops, bytes_accessed=moved, transcendentals=0),
+        name=name,
+    )(*operands)
+
+
+def local_in_vmem(integrals, metric_factor, occ_energy, virt_energy, orb_count):
+    across = [(0, 1), (1, 0)]
+    swap = [(d, d ^ 1) for d in range(orb_count)]
+    moves = ring_moves(orb_count)
+    own = jnp.swapaxes(integrals[0], 1, 2)
+    count, width, nv = own.shape
+    naux = metric_factor.shape[0]
+    half, full, arrival = jnp.bfloat16, jnp.float32, pltpu.SemaphoreType.DMA
+    depth = lambda part: width * sum(1 if s.ndim == 3 else s.shape[0] for s in part)
+
+    steps = orb_count // 4
+    lanes = [own, lax.ppermute(own, "orb", swap)]
+    slices, sent, early_row = list(lanes), 0, None
+    for step in range(1, steps + 1):
+        lanes = [lax.ppermute(lane, "orb", moves) for lane in (lanes if step < steps else lanes[:1])]
+        slices += lanes
+        if step == steps-3:
+            sent = len(slices)
+            row, own = vmem_call(
+                early_row_kernel, "early_row", slices, [((depth(slices), nv), half), (own.shape, half)],
+                [arrival], in_hbm=1,
+            )
+            early_row = lax.ppermute(row, "spin", across)
+            slices[0] = own
+        order = [early_row] if step == steps-1 else []
+        (stacked,) = vmem_call(
+            functools.partial(stack_kernel, len(lanes)), "stack", lanes + order,
+            [((len(lanes),) + own.shape, half)],
+        )
+        slices.append(lax.ppermute(stacked, "orb", swap))
+    (row,) = vmem_call(row_kernel, "late_row", slices[sent:], [((depth(slices[sent:]), nv), half)])
+    late_row = lax.ppermute(row, "spin", across)
+    pair = 2 * count * nv * nv
+    factor, fitted, gamma_same, dens_same = vmem_call(
+        functools.partial(fit_same_kernel, orb_count), "fit_same",
+        [occ_energy, virt_energy, metric_factor] + slices,
+        [((naux, naux), half), ((naux, count * nv), half), ((nv, naux), full), ((nv, nv), full)],
+        [((naux, naux), half), ((nv, naux), half), ((nv, nv), full), ((nv, count * nv), half)],
+    )
+    rows = nv // orb_count
+    gamma_other, kept, sent = vmem_call(
+        opposite_all_kernel, "opposite",
+        [occ_energy, virt_energy, factor, early_row, late_row, fitted, dens_same],
+        [((nv, naux), half)] + [((orb_count // 2, rows, nv), full)] * 2,
+        [((nv, naux), half), ((nv, nv), full), ((nv, nv), full), ((nv, count * nv), half)],
+        flops=pair * (2 * naux + nv),
+    )
+    returned = lax.ppermute(gamma_other, "spin", across)
+    kept, arrived = reduce_rows(kept + lax.ppermute(sent, "orb", swap), orb_count, 2)
+    gamma, kept, sent = vmem_call(
+        join_kernel, "join", [gamma_same, returned, kept, arrived],
+        [((nv, naux), full)] + [((rows, nv), full)] * 2, [((2, rows, nv), full)], pin=False,
+    )
+    far = [(d, d ^ (orb_count // 2)) for d in range(orb_count)]
+    density = kept + lax.ppermute(sent, "orb", far)
+    return gamma[None, None], density[None]
 
 
 def fit_kernel(factor_ref, *refs):
@@ -182,21 +393,22 @@
     )(pair_energy, factor, raw, fitted, virt_left[:, None], virt_right[None, :], dens)
 
 
-def reduce_rows(total, orb_count):
+def reduce_rows(total, orb_count, keep):
     index = lax.axis_index("orb")
     bits = orb_count.bit_length() - 1
-    rows = total.reshape((2,) * bits + (total.shape[0] // orb_count, total.shape[1]))
-    for bit in range(bits):
+    rows = total.reshape((2,) * (bits - 1) + total.shape[1:])
+    for bit in range(1, bits + 1 - keep.bit_length()):
         axis = bits - 1 - bit
         mine = (index >> bit) & 1
         moves = [(d, d ^ (1 << bit)) for d in range(orb_count)]
         kept = lax.dynamic_index_in_dim(rows, mine, axis, keepdims=False)
         sent = lax.dynamic_index_in_dim(rows, 1 - mine, axis, keepdims=False)
-        rows = kept + lax.ppermute(sent, "orb", moves)
-    return rows
-
-
-def local(integrals, metric_factor, occ_energy, virt_energy, orb_count):
+        arrived = lax.ppermute(sent, "orb", moves)
+        rows = kept + arrived
+    return kept, arrived
+
+
+def local_streamed(integrals, metric_factor, occ_energy, virt_energy, orb_count):
     spin_index = lax.axis_index("spin")
     orbit_index = lax.axis_index("orb")
     other_spin = 1 - spin_index
@@ -212,7 +424,9 @@
     factor = jnp.take(metric_factor.reshape(orb_count, width, naux), sources, axis=0)
     factor = factor.reshape(naux, naux).T
 
-    slices = gather_slices(own, orb_count)
+    slices = []
+    for part in gather_slices(own, orb_count):
+        slices += [part] if part.ndim == 3 else [part[n] for n in range(part.shape[0])]
     own_row = [pick(s, orbit_index) for s in slices]
     early = len(slices) - 6 if len(slices) > 8 else len(slices) // 2
     raw_row = jnp.concatenate(
@@ -232,8 +446,19 @@
     )
     returned = lax.ppermute(gamma_other, "spin", across)
     gamma = gamma_same + returned
-    density = reduce_rows(dens, orb_count) / occupied
+    split = dens.reshape(orb_count // 2, 2, nv // orb_count, nv) / occupied
+    kept, sent = (lax.dynamic_index_in_dim(split, n, 1, False) for n in (orbit_index % 2, 1 - orbit_index % 2))
+    swap = [(d, d ^ 1) for d in range(orb_count)]
+    kept, arrived = reduce_rows(kept + lax.ppermute(sent, "orb", swap), orb_count, 1)
+    density = kept + arrived
     return gamma[None, None], density[None]
+
+
+def local(integrals, metric_factor, occ_energy, virt_energy, orb_count):
+    _, count, nv, width = integrals.shape
+    fits = count * nv * metric_factor.shape[0] * 2 <= 4 * 1024 * 1024 and width % 16 == 0 and count % GROUP == 0
+    chosen = local_in_vmem if fits else local_streamed
+    return chosen(integrals, metric_factor, occ_energy, virt_energy, orb_count)
 
 
 def solution(mesh):

time: 78.9 us -> 58.2 us (0.74)
  Pallas kernels: 22 us -> 11.6 us
  local copies, waits for them, and re-layouts: 6.82 us -> 0.05 us
  other arithmetic: 4.36 us -> 0.64 us
  starting transfers between devices: 21.9 us -> 23.8 us
  waiting for transfers between devices: 22.5 us -> 21.2 us
    pallas_call x3 -> x9, Pallas kernels: 22 us -> 11.6 us  [vmem_call(): pl.pallas_call(kernel, in_specs=[hbm] * in_hbm + [vmem] * (len(operands)...]
    unnamed x24 -> x6, local copies, waits for them, and re-layouts: 3.05 us -> 0.01 us
    ppermute x19, starting transfers between devices: 21.9 us -> 23.8 us  [the longest x7 14.2 us: local_in_vmem(): lax.ppermute(lane, 'orb', moves)]
    dynamic_slice x1 -> x0, local copies, waits for them, and re-layouts: 1.35 us -> none  [local(): lax.dynamic_index_in_dim(array, n, 0, keepdims=False)]
    ppermute x19, waiting for transfers between devices: 22.5 us -> 21.2 us  [the longest x7 9.97 us: local_in_vmem(): lax.ppermute(lane, 'orb', moves)]
    add x4 -> x2, other arithmetic: 1.25 us -> 0.03 us  [the longest x1 0.02 us: local_in_vmem(): kept + lax.ppermute(sent, 'orb', swap)]
    broadcast_in_dim x5 -> x0, local copies, waits for them, and re-layouts: 1.2 us -> none  [the longest x2 0.9 us: opposite_spin(): virt_left[:, None]]
    broadcast_in_dim x2 -> x1, other arithmetic: 1.48 us -> 0.61 us  [local_in_vmem(): return (gamma[None, None], density[None])]
  transfers between devices with their start and end apart: 19 -> 19, of which waited for: 11 -> 13; matrix products, arithmetic and copies ran while one was open for 10% -> 0% of each run, Pallas kernels for 18% -> 12%
where the time goes in v2:
time: 58.2 us; the launch traced here: 58 us
  starting transfers between devices  23.8 us (41%)
  waiting for transfers between devices  21.2 us (36%)
  Pallas kernels  11.6 us (20%)
  between operations  0.8 us (1%)
  other arithmetic  0.64 us (1%)
    ppermute x7, starting transfers between devices, local_in_vmem(): lax.ppermute(lane, 'orb', moves)  14.2 us
    pallas_call x9, Pallas kernels, vmem_call(): pl.pallas_call(kernel, in_specs=[hbm] * in_hbm + [vmem] * (len(operands)...  11.6 us
    ppermute x7, waiting for transfers between devices, local_in_vmem(): lax.ppermute(lane, 'orb', moves)  9.97 us
    ppermute x2, waiting for transfers between devices, reduce_rows(): arrived = lax.ppermute(sent, 'orb', moves)  4.85 us
    ppermute x1, starting transfers between devices, local_in_vmem(): density = kept + lax.ppermute(sent, 'orb', far)  2.58 us
    ppermute x2, starting transfers between devices, reduce_rows(): arrived = lax.ppermute(sent, 'orb', moves)  2.49 us
    ppermute x1, waiting for transfers between devices, local_in_vmem(): density = kept + lax.ppermute(sent, 'orb', far)  2.05 us
    ppermute x1, starting transfers between devices, local_in_vmem(): early_row = lax.ppermute(row, 'spin', across)  1.56 us
  transfers between devices with their start and end apart: 19, of which 13 were waited for; matrix products, arithmetic and copies ran while one was open for 0% of the time, Pallas kernels for 12%

profile of v2, /device:TPU:0, one launch (start us, length us, event | category | flops | bytes accessed | tf_op | source)
XLA Modules:
  0.0 58.0 jit_solution(9461817351962684838)
XLA Ops:
  0.6 0.0 copy-start.2
  0.6 0.0 copy-start.1
  0.7 0.0 copy-start
  0.7 0.5 collective-permute-start
  1.2 2.6 %collective-permute-start.1 = (bf16[16,32,256]{2,1,0:T(8,128)(2,1)}, bf16[16,32,256]{2,1,0:T(8,128)(2,1)S(1)}, u32[]{:S(2)}, u32[]{:S(2)}) collective-permute-start(bf16[16,32,256]{2,1,0:T(8,128)(2,1)} %bitcast.18), channel_id=1, source_target_pairs={{0,4},{4,8},{8,12},{12,14},{14,10},{10,6},{6,2},{2,0},{5,1},{9,5},... | collective-permute-start | bytes 786440 | tf_op jit(solution)/shard_map/ppermute | solution.py:237
  3.8 0.0 collective-permute-done.refs_0_.refs_1_
  3.8 1.7 %collective-permute-start.2 = (bf16[16,32,256]{2,1,0:T(8,128)(2,1)S(1)}, bf16[16,32,256]{2,1,0:T(8,128)(2,1)S(1)}, u32[]{:S(2)}, u32[]{:S(2)}) collective-permute-start(bf16[16,32,256]{2,1,0:T(8,128)(2,1)S(1)} %collective-permute-done.refs_0_.refs_1_), channel_id=1, source_target_pairs={{0,4},{4,8},{8,12},{12,14},{14,10},{10,6},{6,2},{2,0},{5,1},{9,5},... | collective-permute-start | bytes 786440 | tf_op jit(solution)/shard_map/ppermute | solution.py:237
  5.5 2.8 %collective-permute-done.1.refs_1_.refs_0_.refs_2_ = bf16[16,32,256]{2,1,0:T(8,128)(2,1)S(1)} collective-permute-done((bf16[16,32,256]{2,1,0:T(8,128)(2,1)}, bf16[16,32,256]{2,1,0:T(8,128)(2,1)S(1)}, u32[]{:S(2)}, u32[]{:S(2)}) %collective-permute-start.1) | collective-permute-done | bytes 262176 | tf_op jit(solution)/shard_map/ppermute | solution.py:237
  8.3 2.1 %collective-permute-start.4 = (bf16[16,32,256]{2,1,0:T(8,128)(2,1)S(1)}, bf16[16,32,256]{2,1,0:T(8,128)(2,1)S(1)}, u32[]{:S(2)}, u32[]{:S(2)}) collective-permute-start(bf16[16,32,256]{2,1,0:T(8,128)(2,1)S(1)} %collective-permute-done.1.refs_1_.refs_0_.refs_2_), channel_id=1, source_target_pairs={{0,4},{4,8},{8,12},{12,14},{14,10},{10,6},{6,2},{2,0},{5,1},{9,5},... | collective-permute-start | bytes 786440 | tf_op jit(solution)/shard_map/ppermute | solution.py:237
  10.4 0.7 %collective-permute-done.2.refs_2_.refs_1_.refs_3_ = bf16[16,32,256]{2,1,0:T(8,128)(2,1)S(1)} collective-permute-done((bf16[16,32,256]{2,1,0:T(8,128)(2,1)S(1)}, bf16[16,32,256]{2,1,0:T(8,128)(2,1)S(1)}, u32[]{:S(2)}, u32[]{:S(2)}) %collective-permute-start.2) | collective-permute-done | bytes 262176 | tf_op jit(solution)/shard_map/ppermute | solution.py:237
  11.1 2.1 %collective-permute-start.5 = (bf16[16,32,256]{2,1,0:T(8,128)(2,1)S(1)}, bf16[16,32,256]{2,1,0:T(8,128)(2,1)S(1)}, u32[]{:S(2)}, u32[]{:S(2)}) collective-permute-start(bf16[16,32,256]{2,1,0:T(8,128)(2,1)S(1)} %collective-permute-done.2.refs_2_.refs_1_.refs_3_), channel_id=1, source_target_pairs={{0,4},{4,8},{8,12},{12,14},{14,10},{10,6},{6,2},{2,0},{5,1},{9,5},... | collective-permute-start | bytes 786440 | tf_op jit(solution)/shard_map/ppermute | solution.py:237
  13.2 1.5 %collective-permute-done.4.refs_0_.refs_5_.refs_1_ = bf16[16,32,256]{2,1,0:T(8,128)(2,1)S(1)} collective-permute-done((bf16[16,32,256]{2,1,0:T(8,128)(2,1)S(1)}, bf16[16,32,256]{2,1,0:T(8,128)(2,1)S(1)}, u32[]{:S(2)}, u32[]{:S(2)}) %collective-permute-start.4) | collective-permute-done | bytes 262176 | tf_op jit(solution)/shard_map/ppermute | solution.py:237
  14.7 2.1 %collective-permute-start.7 = (bf16[16,32,256]{2,1,0:T(8,128)(2,1)S(1)}, bf16[16,32,256]{2,1,0:T(8,128)(2,1)S(1)}, u32[]{:S(2)}, u32[]{:S(2)}) collective-permute-start(bf16[16,32,256]{2,1,0:T(8,128)(2,1)S(1)} %collective-permute-done.4.refs_0_.refs_5_.refs_1_), channel_id=1, source_target_pairs={{0,4},{4,8},{8,12},{12,14},{14,10},{10,6},{6,2},{2,0},{5,1},{9,5},... | collective-permute-start | bytes 786440 | tf_op jit(solution)/shard_map/ppermute | solution.py:237
  16.8 0.7 %collective-permute-done.5.refs_1_.refs_6_.refs_2_ = bf16[16,32,256]{2,1,0:T(8,128)(2,1)S(1)} collective-permute-done((bf16[16,32,256]{2,1,0:T(8,128)(2,1)S(1)}, bf16[16,32,256]{2,1,0:T(8,128)(2,1)S(1)}, u32[]{:S(2)}, u32[]{:S(2)}) %collective-permute-start.5) | collective-permute-done | bytes 262176 | tf_op jit(solution)/shard_map/ppermute | solution.py:237
  17.5 2.1 %collective-permute-start.8 = (bf16[16,32,256]{2,1,0:T(8,128)(2,1)S(1)}, bf16[16,32,256]{2,1,0:T(8,128)(2,1)S(1)}, u32[]{:S(2)}, u32[]{:S(2)}) collective-permute-start(bf16[16,32,256]{2,1,0:T(8,128)(2,1)S(1)} %collective-permute-done.5.refs_1_.refs_6_.refs_2_), channel_id=1, source_target_pairs={{0,4},{4,8},{8,12},{12,14},{14,10},{10,6},{6,2},{2,0},{5,1},{9,5},... | collective-permute-start | bytes 786440 | tf_op jit(solution)/shard_map/ppermute | solution.py:237
  19.6 1.0 %early_row.1 = (bf16[128,256]{1,0:T(8,128)(2,1)S(1)}, bf16[16,32,256]{2,1,0:T(8,128)(2,1)S(1)}) custom-call(bf16[16,32,256]{2,1,0:T(8,128)(2,1)} %bitcast.19, bf16[16,32,256]{2,1,0:T(8,128)(2,1)S(1)} %collective-permute-done.refs_0_.refs_1_, bf16[16,32,256]{2,1,0:T(8,128)(2,1)S(1)} %collective-permute-done.1.refs_1_.refs_0_.refs_2_, ...), custom_call_target="tpu_custom_call" | custom-call | bytes 1048576 | tf_op jit(solution)/shard_map/early_row/pallas_call | solution.py:211
  20.5 1.6 %collective-permute-start.9 = (bf16[128,256]{1,0:T(8,128)(2,1)S(1)}, bf16[128,256]{1,0:T(8,128)(2,1)S(1)}, u32[]{:S(2)}, u32[]{:S(2)}) collective-permute-start(bf16[128,256]{1,0:T(8,128)(2,1)S(1)} %get-tuple-element.15), channel_id=1, source_target_pairs={{0,16},{16,0},{1,17},{17,1},{2,18},{18,2},{3,19},{19,3},{4,20},{20... | collective-permute-start | bytes 196616 | tf_op jit(solution)/shard_map/ppermute | solution.py:245
  22.1 0.1 collective-permute-start.3
  22.3 0.6 collective-permute-start.6
  22.8 0.0 collective-permute-done.7.refs_0_.refs_8_.refs_4_
  22.8 1.6 %collective-permute-start.11 = (bf16[16,32,256]{2,1,0:T(8,128)(2,1)S(1)}, bf16[16,32,256]{2,1,0:T(8,128)(2,1)S(1)}, u32[]{:S(2)}, u32[]{:S(2)}) collective-permute-start(bf16[16,32,256]{2,1,0:T(8,128)(2,1)S(1)} %collective-permute-done.7.refs_0_.refs_8_.refs_4_), channel_id=1, source_target_pairs={{0,4},{4,8},{8,12},{12,14},{14,10},{10,6},{6,2},{2,0},{5,1},{9,5},... | collective-permute-start | bytes 786440 | tf_op jit(solution)/shard_map/ppermute | solution.py:237
  24.4 0.5 collective-permute-done.9.refs_2_.early_ref
  24.9 0.0 collective-permute-done.8.refs_1_.refs_9_.refs_5_
  24.9 0.1 collective-permute-start.10
  25.0 4.2 %collective-permute-done.11.refs_0_.refs_11_.refs_7_ = bf16[16,32,256]{2,1,0:T(8,128)(2,1)S(1)} collective-permute-done((bf16[16,32,256]{2,1,0:T(8,128)(2,1)S(1)}, bf16[16,32,256]{2,1,0:T(8,128)(2,1)S(1)}, u32[]{:S(2)}, u32[]{:S(2)}) %collective-permute-start.11) | collective-permute-done | bytes 262176 | tf_op jit(solution)/shard_map/ppermute | solution.py:237
  29.2 0.1 collective-permute-start.12
  29.3 0.0 collective-permute-done.3.refs_4_.refs_0_
  29.3 0.0 collective-permute-done.6.refs_7_.refs_3_
  29.3 1.5 %collective-permute-done.12.refs_12_.refs_8_ = bf16[1,16,32,256]{3,2,1,0:T(8,128)(2,1)S(1)} collective-permute-done((bf16[1,16,32,256]{3,2,1,0:T(8,128)(2,1)S(1)}, bf16[1,16,32,256]{3,2,1,0:T(8,128)(2,1)S(1)}, u32[]{:S(2)}, u32[]{:S(2)}) %collective-permute-start.12) | collective-permute-done | bytes 262176 | tf_op jit(solution)/shard_map/ppermute | solution.py:252
  30.8 0.0 collective-permute-done.10.refs_10_.refs_6_
  30.8 0.6 %collective-permute-start.13 = (bf16[384,256]{1,0:T(8,128)(2,1)S(1)}, bf16[384,256]{1,0:T(8,128)(2,1)S(1)}, u32[]{:S(2)}, u32[]{:S(2)}) collective-permute-start(bf16[384,256]{1,0:T(8,128)(2,1)S(1)} %late_row.1), channel_id=1, source_target_pairs={{0,16},{16,0},{1,17},{17,1},{2,18},{18,2},{3,19},{19,3},{4,20},{20... | collective-permute-start | bytes 589832 | tf_op jit(solution)/shard_map/ppermute | solution.py:254
  31.4 0.0 copy-done.2
  31.4 0.0 copy-done.1
  31.5 0.0 copy-done
  31.5 6.0 %fit_same.1 = (bf16[512,512]{1,0:T(8,128)(2,1)S(1)}, bf16[512,4096]{1,0:T(8,128)(2,1)S(1)}, f32[256,512]{1,0:T(8,128)S(1)}, f32[256,256]{1,0:T(8,128)S(1)}) custom-call(f32[2,16]{1,0:T(2,128)S(1)} %copy-done.2, f32[2,256]{1,0:T(2,128)S(1)} %copy-done.1, bf16[512,512]{1,0:T(8,128)(2,1)S(1)} %copy-done, bf16[16,32,256]{2,1,0:T(8,128)(2,1)S(1)} %get-tuple-element.14.refs_0_, ...), custom_call_target="tpu_custom_call" | custom-call | bytes 4720768 | tf_op jit(solution)/shard_map/fit_same/pallas_call | solution.py:211
  37.4 0.4 collective-permute-done.13.late_ref
  37.9 3.7 %opposite.1 = (bf16[256,512]{1,0:T(8,128)(2,1)S(1)}, f32[8,16,256]{2,1,0:T(8,128)S(1)}, f32[8,16,256]{2,1,0:T(8,128)S(1)}) custom-call(f32[2,16]{1,0:T(2,128)S(1)} %copy-done.2, f32[2,256]{1,0:T(2,128)S(1)} %copy-done.1, bf16[512,512]{1,0:T(8,128)(2,1)S(1)} %get-tuple-element.17.factor_ref, bf16[128,256]{1,0:T(8,128)(2,1)S(1)} %collective-permute-done.9.refs_2_.early_ref, ...), custom_call_target="tpu_custom_call" | custom-call | flops 2684354560 | bytes 5245056 | tf_op jit(solution)/shard_map/opposite/pallas_call | solution.py:211
  41.5 0.1 collective-permute-start.15
  41.6 1.3 %collective-permute-done.15 = f32[8,16,256]{2,1,0:T(8,128)S(1)} collective-permute-done((f32[8,16,256]{2,1,0:T(8,128)S(1)}, f32[8,16,256]{2,1,0:T(8,128)S(1)}, u32[]{:S(2)}, u32[]{:S(2)}) %collective-permute-start.15) | collective-permute-done | bytes 131104 | tf_op jit(solution)/shard_map/ppermute | solution.py:271
  43.0 0.9 %collective-permute-start.16 = (f32[2,2,16,256]{3,2,0,1:T(8,128)S(1)}, f32[2,2,16,256]{3,2,0,1:T(8,128)S(1)}, u32[]{:S(2)}, u32[]{:S(2)}) collective-permute-start(f32[2,2,16,256]{3,2,0,1:T(8,128)S(1)} %bitcast.20), channel_id=1, source_target_pairs={{0,2},{1,3},{2,0},{3,1},{4,6},{5,7},{6,4},{7,5},{8,10},{9,11},{10,... | collective-permute-start | bytes 196616 | tf_op jit(solution)/shard_map/ppermute | solution.py:406
  43.9 1.0 %collective-permute-start.14 = (bf16[256,512]{1,0:T(8,128)(2,1)S(1)}, bf16[256,512]{1,0:T(8,128)(2,1)S(1)}, u32[]{:S(2)}, u32[]{:S(2)}) collective-permute-start(bf16[256,512]{1,0:T(8,128)(2,1)S(1)} %get-tuple-element.20), channel_id=1, source_target_pairs={{0,16},{16,0},{1,17},{17,1},{2,18},{18,2},{3,19},{19,3},{4,20},{20... | collective-permute-start | bytes 786440 | tf_op jit(solution)/shard_map/ppermute | solution.py:270
  44.8 2.5 %collective-permute-done.16 = f32[2,2,16,256]{3,2,0,1:T(8,128)S(1)} collective-permute-done((f32[2,2,16,256]{3,2,0,1:T(8,128)S(1)}, f32[2,2,16,256]{3,2,0,1:T(8,128)S(1)}, u32[]{:S(2)}, u32[]{:S(2)}) %collective-permute-start.16) | collective-permute-done | bytes 65568 | tf_op jit(solution)/shard_map/ppermute | solution.py:406
  47.4 1.6 %collective-permute-start.17 = (f32[2,16,256]{2,1,0:T(8,128)S(1)}, f32[2,16,256]{2,1,0:T(8,128)S(1)}, u32[]{:S(2)}, u32[]{:S(2)}) collective-permute-start(f32[2,16,256]{2,1,0:T(8,128)S(1)} %get-tuple-element.28), channel_id=1, source_target_pairs={{0,4},{1,5},{2,6},{3,7},{4,0},{5,1},{6,2},{7,3},{8,12},{9,13},{10,... | collective-permute-start | bytes 98312 | tf_op jit(solution)/shard_map/ppermute | solution.py:406
  49.0 2.3 %collective-permute-done.17.arrived = f32[2,16,256]{2,1,0:T(8,128)S(1)} collective-permute-done((f32[2,16,256]{2,1,0:T(8,128)S(1)}, f32[2,16,256]{2,1,0:T(8,128)S(1)}, u32[]{:S(2)}, u32[]{:S(2)}) %collective-permute-start.17) | collective-permute-done | bytes 32800 | tf_op jit(solution)/shard_map/ppermute | solution.py:406
  51.4 0.6 %collective-permute-done.14.returned = bf16[256,512]{1,0:T(8,128)(2,1)S(1)} collective-permute-done((bf16[256,512]{1,0:T(8,128)(2,1)S(1)}, bf16[256,512]{1,0:T(8,128)(2,1)S(1)}, u32[]{:S(2)}, u32[]{:S(2)}) %collective-permute-start.14) | collective-permute-done | bytes 262176 | tf_op jit(solution)/shard_map/ppermute | solution.py:270
  51.9 0.8 %join.1 = (f32[256,512]{1,0:T(8,128)}, f32[16,256]{1,0:T(8,128)S(1)}, f32[16,256]{1,0:T(8,128)S(1)}) custom-call(f32[256,512]{1,0:T(8,128)S(1)} %get-tuple-element.16.gamma_in, bf16[256,512]{1,0:T(8,128)(2,1)S(1)} %collective-permute-done.14.returned, f32[2,16,256]{2,1,0:T(8,128)S(1)} %get-tuple-element.29.kept_in, ...), custom_call_target="tpu_custom_call" | custom-call | bytes 851968 | tf_op jit(solution)/shard_map/join/pallas_call | solution.py:211
  52.8 2.6 %collective-permute-start.18 = (f32[16,256]{1,0:T(8,128)S(1)}, f32[16,256]{1,0:T(8,128)S(1)}, u32[]{:S(2)}, u32[]{:S(2)}) collective-permute-start(f32[16,256]{1,0:T(8,128)S(1)} %get-tuple-element.25), channel_id=1, source_target_pairs={{0,8},{1,9},{2,10},{3,11},{4,12},{5,13},{6,14},{7,15},{8,0},{9,1},... | collective-permute-start | bytes 49160 | tf_op jit(solution)/shard_map/ppermute | solution.py:277
  55.4 2.1 %collective-permute-done.18 = f32[16,256]{1,0:T(8,128)S(1)} collective-permute-done((f32[16,256]{1,0:T(8,128)S(1)}, f32[16,256]{1,0:T(8,128)S(1)}, u32[]{:S(2)}, u32[]{:S(2)}) %collective-permute-start.18) | collective-permute-done | bytes 16416 | tf_op jit(solution)/shard_map/ppermute | solution.py:277
  57.4 0.6 %add_bitcast_fusion = f32[1,16,256]{2,1,0:T(8,128)} fusion(f32[16,256]{1,0:T(8,128)S(1)} %get-tuple-element.24, f32[16,256]{1,0:T(8,128)S(1)} %collective-permute-done.18), kind=kLoop, calls=%fused_computation.4 | loop fusion | flops 4096 | bytes 49152 | tf_op jit(solution)/shard_map/broadcast_in_dim | solution.py:278
  (10 shorter events, 0.2 us)
Async XLA Ops:
  0.6 30.8 %copy-start.2 = (f32[2,16]{1,0:T(2,128)S(1)}, f32[2,16]{1,0:T(2,128)}, u32[]{:S(2)}) copy-start(f32[2,16]{1,0:T(2,128)} %occ_ref.3) | copy-start | bytes 388
  0.6 30.8 %copy-start.1 = (f32[2,256]{1,0:T(2,128)S(1)}, f32[2,256]{1,0:T(2,128)}, u32[]{:S(2)}) copy-start(f32[2,256]{1,0:T(2,128)} %virt_ref.3) | copy-start | bytes 6148
  0.7 30.8 %copy-start = (bf16[512,512]{1,0:T(8,128)(2,1)S(1)}, bf16[512,512]{1,0:T(8,128)(2,1)}, u32[]{:S(2)}) copy-start(bf16[512,512]{1,0:T(8,128)(2,1)} %given_ref.1) | copy-start | bytes 1572868
  0.7 3.2 %collective-permute-start = (bf16[16,32,256]{2,1,0:T(8,128)(2,1)}, bf16[16,32,256]{2,1,0:T(8,128)(2,1)S(1)}, u32[]{:S(2)}, u32[]{:S(2)}) collective-permute-start(bf16[16,32,256]{2,1,0:T(8,128)(2,1)} %bitcast.17), channel_id=1, source_target_pairs={{0,1},{1,0},{2,3},{3,2},{4,5},{5,4},{6,7},{7,6},{8,9},{9,8},{10,11... | collective-permute-start | bytes 786440 | tf_op jit(solution)/shard_map/ppermute | solution.py:234
  1.2 7.1 %collective-permute-start.1 = (bf16[16,32,256]{2,1,0:T(8,128)(2,1)}, bf16[16,32,256]{2,1,0:T(8,128)(2,1)S(1)}, u32[]{:S(2)}, u32[]{:S(2)}) collective-permute-start(bf16[16,32,256]{2,1,0:T(8,128)(2,1)} %bitcast.18), channel_id=1, source_target_pairs={{0,4},{4,8},{8,12},{12,14},{14,10},{10,6},{6,2},{2,0},{5,1},{9,5},... | collective-permute-start | bytes 786440 | tf_op jit(solution)/shard_map/ppermute | solution.py:237
  3.8 7.3 %collective-permute-start.2 = (bf16[16,32,256]{2,1,0:T(8,128)(2,1)S(1)}, bf16[16,32,256]{2,1,0:T(8,128)(2,1)S(1)}, u32[]{:S(2)}, u32[]{:S(2)}) collective-permute-start(bf16[16,32,256]{2,1,0:T(8,128)(2,1)S(1)} %collective-permute-done.refs_0_.refs_1_), channel_id=1, source_target_pairs={{0,4},{4,8},{8,12},{12,14},{14,10},{10,6},{6,2},{2,0},{5,1},{9,5},... | collective-permute-start | bytes 786440 | tf_op jit(solution)/shard_map/ppermute | solution.py:237
  8.3 6.4 %collective-permute-start.4 = (bf16[16,32,256]{2,1,0:T(8,128)(2,1)S(1)}, bf16[16,32,256]{2,1,0:T(8,128)(2,1)S(1)}, u32[]{:S(2)}, u32[]{:S(2)}) collective-permute-start(bf16[16,32,256]{2,1,0:T(8,128)(2,1)S(1)} %collective-permute-done.1.refs_1_.refs_0_.refs_2_), channel_id=1, source_target_pairs={{0,4},{4,8},{8,12},{12,14},{14,10},{10,6},{6,2},{2,0},{5,1},{9,5},... | collective-permute-start | bytes 786440 | tf_op jit(solution)/shard_map/ppermute | solution.py:237
  11.1 6.4 %collective-permute-start.5 = (bf16[16,32,256]{2,1,0:T(8,128)(2,1)S(1)}, bf16[16,32,256]{2,1,0:T(8,128)(2,1)S(1)}, u32[]{:S(2)}, u32[]{:S(2)}) collective-permute-start(bf16[16,32,256]{2,1,0:T(8,128)(2,1)S(1)} %collective-permute-done.2.refs_2_.refs_1_.refs_3_), channel_id=1, source_target_pairs={{0,4},{4,8},{8,12},{12,14},{14,10},{10,6},{6,2},{2,0},{5,1},{9,5},... | collective-permute-start | bytes 786440 | tf_op jit(solution)/shard_map/ppermute | solution.py:237
  14.7 8.1 %collective-permute-start.7 = (bf16[16,32,256]{2,1,0:T(8,128)(2,1)S(1)}, bf16[16,32,256]{2,1,0:T(8,128)(2,1)S(1)}, u32[]{:S(2)}, u32[]{:S(2)}) collective-permute-start(bf16[16,32,256]{2,1,0:T(8,128)(2,1)S(1)} %collective-permute-done.4.refs_0_.refs_5_.refs_1_), channel_id=1, source_target_pairs={{0,4},{4,8},{8,12},{12,14},{14,10},{10,6},{6,2},{2,0},{5,1},{9,5},... | collective-permute-start | bytes 786440 | tf_op jit(solution)/shard_map/ppermute | solution.py:237
  17.5 7.4 %collective-permute-start.8 = (bf16[16,32,256]{2,1,0:T(8,128)(2,1)S(1)}, bf16[16,32,256]{2,1,0:T(8,128)(2,1)S(1)}, u32[]{:S(2)}, u32[]{:S(2)}) collective-permute-start(bf16[16,32,256]{2,1,0:T(8,128)(2,1)S(1)} %collective-permute-done.5.refs_1_.refs_6_.refs_2_), channel_id=1, source_target_pairs={{0,4},{4,8},{8,12},{12,14},{14,10},{10,6},{6,2},{2,0},{5,1},{9,5},... | collective-permute-start | bytes 786440 | tf_op jit(solution)/shard_map/ppermute | solution.py:237
  20.5 4.3 %collective-permute-start.9 = (bf16[128,256]{1,0:T(8,128)(2,1)S(1)}, bf16[128,256]{1,0:T(8,128)(2,1)S(1)}, u32[]{:S(2)}, u32[]{:S(2)}) collective-permute-start(bf16[128,256]{1,0:T(8,128)(2,1)S(1)} %get-tuple-element.15), channel_id=1, source_target_pairs={{0,16},{16,0},{1,17},{17,1},{2,18},{18,2},{3,19},{19,3},{4,20},{20... | collective-permute-start | bytes 196616 | tf_op jit(solution)/shard_map/ppermute | solution.py:245
  22.1 7.2 %collective-permute-start.3 = (bf16[2,16,32,256]{3,2,1,0:T(8,128)(2,1)S(1)}, bf16[2,16,32,256]{3,2,1,0:T(8,128)(2,1)S(1)}, u32[]{:S(2)}, u32[]{:S(2)}) collective-permute-start(bf16[2,16,32,256]{3,2,1,0:T(8,128)(2,1)S(1)} %stack.4), channel_id=1, source_target_pairs={{0,1},{1,0},{2,3},{3,2},{4,5},{5,4},{6,7},{7,6},{8,9},{9,8},{10,11... | collective-permute-start | bytes 1572872 | tf_op jit(solution)/shard_map/ppermute | solution.py:252
  22.3 7.0 %collective-permute-start.6 = (bf16[2,16,32,256]{3,2,1,0:T(8,128)(2,1)S(1)}, bf16[2,16,32,256]{3,2,1,0:T(8,128)(2,1)S(1)}, u32[]{:S(2)}, u32[]{:S(2)}) collective-permute-start(bf16[2,16,32,256]{3,2,1,0:T(8,128)(2,1)S(1)} %stack.5), channel_id=1, source_target_pairs={{0,1},{1,0},{2,3},{3,2},{4,5},{5,4},{6,7},{7,6},{8,9},{9,8},{10,11... | collective-permute-start | bytes 1572872 | tf_op jit(solution)/shard_map/ppermute | solution.py:252
  22.8 6.4 %collective-permute-start.11 = (bf16[16,32,256]{2,1,0:T(8,128)(2,1)S(1)}, bf16[16,32,256]{2,1,0:T(8,128)(2,1)S(1)}, u32[]{:S(2)}, u32[]{:S(2)}) collective-permute-start(bf16[16,32,256]{2,1,0:T(8,128)(2,1)S(1)} %collective-permute-done.7.refs_0_.refs_8_.refs_4_), channel_id=1, source_target_pairs={{0,4},{4,8},{8,12},{12,14},{14,10},{10,6},{6,2},{2,0},{5,1},{9,5},... | collective-permute-start | bytes 786440 | tf_op jit(solution)/shard_map/ppermute | solution.py:237
  24.9 5.9 %collective-permute-start.10 = (bf16[2,16,32,256]{3,2,1,0:T(8,128)(2,1)S(1)}, bf16[2,16,32,256]{3,2,1,0:T(8,128)(2,1)S(1)}, u32[]{:S(2)}, u32[]{:S(2)}) collective-permute-start(bf16[2,16,32,256]{3,2,1,0:T(8,128)(2,1)S(1)} %stack.6), channel_id=1, source_target_pairs={{0,1},{1,0},{2,3},{3,2},{4,5},{5,4},{6,7},{7,6},{8,9},{9,8},{10,11... | collective-permute-start | bytes 1572872 | tf_op jit(solution)/shard_map/ppermute | solution.py:252
  29.2 1.6 %collective-permute-start.12 = (bf16[1,16,32,256]{3,2,1,0:T(8,128)(2,1)S(1)}, bf16[1,16,32,256]{3,2,1,0:T(8,128)(2,1)S(1)}, u32[]{:S(2)}, u32[]{:S(2)}) collective-permute-start(bf16[1,16,32,256]{3,2,1,0:T(8,128)(2,1)S(1)} %stack.7), channel_id=1, source_target_pairs={{0,1},{1,0},{2,3},{3,2},{4,5},{5,4},{6,7},{7,6},{8,9},{9,8},{10,11... | collective-permute-start | bytes 786440 | tf_op jit(solution)/shard_map/ppermute | solution.py:252
  30.8 7.0 %collective-permute-start.13 = (bf16[384,256]{1,0:T(8,128)(2,1)S(1)}, bf16[384,256]{1,0:T(8,128)(2,1)S(1)}, u32[]{:S(2)}, u32[]{:S(2)}) collective-permute-start(bf16[384,256]{1,0:T(8,128)(2,1)S(1)} %late_row.1), channel_id=1, source_target_pairs={{0,16},{16,0},{1,17},{17,1},{2,18},{18,2},{3,19},{19,3},{4,20},{20... | collective-permute-start | bytes 589832 | tf_op jit(solution)/shard_map/ppermute | solution.py:254
  41.5 1.4 %collective-permute-start.15 = (f32[8,16,256]{2,1,0:T(8,128)S(1)}, f32[8,16,256]{2,1,0:T(8,128)S(1)}, u32[]{:S(2)}, u32[]{:S(2)}) collective-permute-start(f32[8,16,256]{2,1,0:T(8,128)S(1)} %get-tuple-element.22), channel_id=1, source_target_pairs={{0,1},{1,0},{2,3},{3,2},{4,5},{5,4},{6,7},{7,6},{8,9},{9,8},{10,11... | collective-permute-start | bytes 393224 | tf_op jit(solution)/shard_map/ppermute | solution.py:271
  43.0 4.3 %collective-permute-start.16 = (f32[2,2,16,256]{3,2,0,1:T(8,128)S(1)}, f32[2,2,16,256]{3,2,0,1:T(8,128)S(1)}, u32[]{:S(2)}, u32[]{:S(2)}) collective-permute-start(f32[2,2,16,256]{3,2,0,1:T(8,128)S(1)} %bitcast.20), channel_id=1, source_target_pairs={{0,2},{1,3},{2,0},{3,1},{4,6},{5,7},{6,4},{7,5},{8,10},{9,11},{10,... | collective-permute-start | bytes 196616 | tf_op jit(solution)/shard_map/ppermute | solution.py:406
  43.9 8.1 %collective-permute-start.14 = (bf16[256,512]{1,0:T(8,128)(2,1)S(1)}, bf16[256,512]{1,0:T(8,128)(2,1)S(1)}, u32[]{:S(2)}, u32[]{:S(2)}) collective-permute-start(bf16[256,512]{1,0:T(8,128)(2,1)S(1)} %get-tuple-element.20), channel_id=1, source_target_pairs={{0,16},{16,0},{1,17},{17,1},{2,18},{18,2},{3,19},{19,3},{4,20},{20... | collective-permute-start | bytes 786440 | tf_op jit(solution)/shard_map/ppermute | solution.py:270
  47.4 4.0 %collective-permute-start.17 = (f32[2,16,256]{2,1,0:T(8,128)S(1)}, f32[2,16,256]{2,1,0:T(8,128)S(1)}, u32[]{:S(2)}, u32[]{:S(2)}) collective-permute-start(f32[2,16,256]{2,1,0:T(8,128)S(1)} %get-tuple-element.28), channel_id=1, source_target_pairs={{0,4},{1,5},{2,6},{3,7},{4,0},{5,1},{6,2},{7,3},{8,12},{9,13},{10,... | collective-permute-start | bytes 98312 | tf_op jit(solution)/shard_map/ppermute | solution.py:406
  52.8 4.6 %collective-permute-start.18 = (f32[16,256]{1,0:T(8,128)S(1)}, f32[16,256]{1,0:T(8,128)S(1)}, u32[]{:S(2)}, u32[]{:S(2)}) collective-permute-start(f32[16,256]{1,0:T(8,128)S(1)} %get-tuple-element.25), channel_id=1, source_target_pairs={{0,8},{1,9},{2,10},{3,11},{4,12},{5,13},{6,14},{7,15},{8,0},{9,1},... | collective-permute-start | bytes 49160 | tf_op jit(solution)/shard_map/ppermute | solution.py:277

commit v3 on v2

--- a/solution.py
+++ b/solution.py
@@ -10,6 +10,7 @@
 
 VMEM_LIMIT = 20 * 1024 * 1024
 GROUP = 4
+PIECES = 1
 NN = (((1,), (0,)), ((), ()))
 NT = (((1,), (1,)), ((), ()))
 TN = (((0,), (0,)), ((), ()))
@@ -87,13 +88,18 @@
         there = (place + chips + jnp.where(core == 0, -distance, distance)) % chips
         return jnp.where(2 * there < chips, 2 * there, 2 * (chips - there) - 1)
 
-    sources = [own, own ^ 1]
+    sources, first = [own ^ 1], []
     for step in range(1, chips // 2 + 1):
         ahead, behind = 2 * chip_at(step), 2 * chip_at(-step)
+        back = [own] if step == 1 else []
         if 2 * step == chips:
             sources += [ahead + core, behind + 1 - core]
+        elif step < chips // 2 - 1:
+            sources += [ahead + core, ahead + 1 - core]
+            first += [behind + 1 - core, behind + core] + back
         else:
-            sources += [ahead + core, ahead + 1 - core, behind + 1 - core, behind + core]
+            sources += first + [ahead + core, ahead + 1 - core, behind + 1 - core, behind + core] + back
+            first = []
     for n, source in enumerate(sources):
         rows[n * width : (n + 1) * width] = factor_ref[pl.ds(pl.multiple_of(source * width, width), width)]
     return rows[...].T
@@ -102,14 +108,6 @@
 def row_kernel(*refs):
     *slices, out_ref = refs
     out_ref[...] = jnp.concatenate(list(pieces(slices, lax.axis_index("orb"))), axis=0)
-
-
-def early_row_kernel(own_hbm, *refs):
-    *slices, out_ref, own_ref, arrived = refs
-    fetch = pltpu.make_async_copy(own_hbm, own_ref, arrived)
-    fetch.start()
-    fetch.wait()
-    out_ref[...] = jnp.concatenate(list(pieces([own_ref] + slices, lax.axis_index("orb"))), axis=0)
 
 
 def stack_kernel(lanes, *refs):
@@ -134,8 +132,8 @@
 
 
 def fit_same_kernel(orb_count, occ_ref, virt_ref, given_ref, *refs):
-    slices, (factor_ref, fitted_ref, gamma_ref, dens_ref) = refs[:-8], refs[-8:-4]
-    rows, left, sums, amp_ref = refs[-4:]
+    slices, (factor_ref, fitted_ref, amp_ref, dens_ref) = refs[:-7], refs[-7:-3]
+    rows, left, sums = refs[-3:]
     factor_ref[...] = order_factor(given_ref, rows, orb_count)
     spin, own = lax.axis_index("spin"), lax.axis_index("orb")
     count, nv = occ_ref.shape[1], virt_ref.shape[1]
@@ -160,12 +158,11 @@
         term = dot(amps, amps, NT)
         total = term if total is None else total + term
     dens_ref[...] = 0.5 * total
-    gamma_ref[...] = dot(amp_ref[...], fitted_ref[...], NT)
 
 
 def opposite_all_kernel(
     occ_ref, virt_ref, factor_ref, early_ref, late_ref, fitted_ref, dens_in,
-    gamma_ref, kept_ref, sent_ref, left, sums, dens, amp_ref,
+    amp_ref, kept_ref, sent_ref, left, sums, dens,
 ):
     spin, own = lax.axis_index("spin"), lax.axis_index("orb")
     count, nv = occ_ref.shape[1], virt_ref.shape[1]
@@ -191,15 +188,31 @@
         for ref, lane in ((kept_ref, core), (sent_ref, 1 - core)):
             first = pl.multiple_of((2 * chip + lane) * rows, rows)
             ref[chip] = dens[pl.ds(first, rows)]
-    gamma_ref[...] = dot(amp_ref[...], fitted_ref[...], NT).astype(gamma_ref.dtype)
-
-
-def join_kernel(gamma_in, returned, kept_in, arrived, gamma_ref, kept_ref, sent_ref, total):
-    gamma_ref[...] = gamma_in[...] + returned[...].astype(jnp.float32)
+
+
+def gamma_kernel(amp_ref, fitted_ref, *out_refs):
+    rows = out_refs[0].shape[0]
+    gamma = dot(amp_ref[...], fitted_ref[...], NT)
+    for n, ref in enumerate(out_refs):
+        ref[...] = gamma[n * rows : (n + 1) * rows].astype(ref.dtype)
+
+
+def split_kernel(bit, kept_in, arrived, *refs):
+    kept_ref, sent_ref, total = refs[-3:]
     total[...] = kept_in[...] + arrived[...]
-    far = lax.axis_index("orb") // (lax.axis_size("orb") // 2)
-    kept_ref[...] = total[far]
-    sent_ref[...] = total[1 - far]
+    mine = (lax.axis_index("orb") >> bit) & 1
+    for n in range(kept_ref.shape[0]):
+        kept_ref[n] = total[2 * n + mine]
+        sent_ref[n] = total[2 * n + 1 - mine]
+
+
+def finish_kernel(kept_in, arrived, gamma_in, *refs):
+    *returned, gamma_ref, density_ref = refs
+    rows = returned[0].shape[0]
+    for n, ref in enumerate(returned):
+        part = slice(n * rows, (n + 1) * rows)
+        gamma_ref[part] = gamma_in[part] + ref[...].astype(jnp.float32)
+    density_ref[...] = kept_in[...] + arrived[...]
 
 
 def vmem_call(kernel, name, operands, outs, scratch=(), flops=0, in_hbm=0, pin=True):
@@ -227,55 +240,68 @@
     own = jnp.swapaxes(integrals[0], 1, 2)
     count, width, nv = own.shape
     naux = metric_factor.shape[0]
-    half, full, arrival = jnp.bfloat16, jnp.float32, pltpu.SemaphoreType.DMA
+    half, full = jnp.bfloat16, jnp.float32
     depth = lambda part: width * sum(1 if s.ndim == 3 else s.shape[0] for s in part)
 
     steps = orb_count // 4
     lanes = [own, lax.ppermute(own, "orb", swap)]
-    slices, sent, early_row = list(lanes), 0, None
+    slices, swapped, early_row = lanes[1:], [], None
     for step in range(1, steps + 1):
+        back = lanes[1:] if step == 1 else []
         lanes = [lax.ppermute(lane, "orb", moves) for lane in (lanes if step < steps else lanes[:1])]
         slices += lanes
-        if step == steps-3:
+        if step == steps - 2:
             sent = len(slices)
-            row, own = vmem_call(
-                early_row_kernel, "early_row", slices, [((depth(slices), nv), half), (own.shape, half)],
-                [arrival], in_hbm=1,
-            )
+            (row,) = vmem_call(row_kernel, "early_row", slices, [((depth(slices), nv), half)])
             early_row = lax.ppermute(row, "spin", across)
-            slices[0] = own
-        order = [early_row] if step == steps-1 else []
+        order = [early_row] if step == steps - 1 else []
         (stacked,) = vmem_call(
-            functools.partial(stack_kernel, len(lanes)), "stack", lanes + order,
-            [((len(lanes),) + own.shape, half)],
+            functools.partial(stack_kernel, len(lanes + back)), "stack", lanes + back + order,
+            [((len(lanes + back),) + own.shape, half)],
         )
-        slices.append(lax.ppermute(stacked, "orb", swap))
+        swapped.append(lax.ppermute(stacked, "orb", swap))
+        if step >= steps - 2:
+            slices += swapped
+            swapped = []
     (row,) = vmem_call(row_kernel, "late_row", slices[sent:], [((depth(slices[sent:]), nv), half)])
     late_row = lax.ppermute(row, "spin", across)
     pair = 2 * count * nv * nv
-    factor, fitted, gamma_same, dens_same = vmem_call(
+    factor, fitted, amp_same, dens_same = vmem_call(
         functools.partial(fit_same_kernel, orb_count), "fit_same",
         [occ_energy, virt_energy, metric_factor] + slices,
-        [((naux, naux), half), ((naux, count * nv), half), ((nv, naux), full), ((nv, nv), full)],
-        [((naux, naux), half), ((nv, naux), half), ((nv, nv), full), ((nv, count * nv), half)],
+        [((naux, naux), half), ((naux, count * nv), half), ((nv, count * nv), half), ((nv, nv), full)],
+        [((naux, naux), half), ((nv, naux), half), ((nv, nv), full)],
     )
     rows = nv // orb_count
-    gamma_other, kept, sent = vmem_call(
+    amp_other, kept, sent = vmem_call(
         opposite_all_kernel, "opposite",
         [occ_energy, virt_energy, factor, early_row, late_row, fitted, dens_same],
-        [((nv, naux), half)] + [((orb_count // 2, rows, nv), full)] * 2,
-        [((nv, naux), half), ((nv, nv), full), ((nv, nv), full), ((nv, count * nv), half)],
-        flops=pair * (2 * naux + nv),
-    )
-    returned = lax.ppermute(gamma_other, "spin", across)
-    kept, arrived = reduce_rows(kept + lax.ppermute(sent, "orb", swap), orb_count, 2)
-    gamma, kept, sent = vmem_call(
-        join_kernel, "join", [gamma_same, returned, kept, arrived],
-        [((nv, naux), full)] + [((rows, nv), full)] * 2, [((2, rows, nv), full)], pin=False,
-    )
-    far = [(d, d ^ (orb_count // 2)) for d in range(orb_count)]
-    density = kept + lax.ppermute(sent, "orb", far)
-    return gamma[None, None], density[None]
+        [((nv, count * nv), half)] + [((orb_count // 2, rows, nv), full)] * 2,
+        [((nv, naux), half), ((nv, nv), full), ((nv, nv), full)],
+        flops=pair * (naux + nv),
+    )
+    gamma_other = vmem_call(
+        gamma_kernel, "gamma_other", [amp_other, fitted], [((nv // PIECES, naux), half)] * PIECES,
+        flops=pair * naux,
+    )
+    (gamma_same,) = vmem_call(
+        gamma_kernel, "gamma_same", [amp_same, fitted], [((nv, naux), full)], flops=2*pair*naux
+    )
+    returned = [lax.ppermute(piece, "spin", across) for piece in gamma_other]
+    for bit in range(1, orb_count.bit_length() - 1):
+        arrived = lax.ppermute(sent, "orb", [(d, d ^ (1 << bit - 1)) for d in range(orb_count)])
+        left = orb_count >> bit + 1
+        order = returned[:0] if left == 1 else []
+        kept, sent = vmem_call(
+            functools.partial(split_kernel, bit), "split", [kept, arrived] + order,
+            [((left, rows, nv), full)] * 2, [((2 * left, rows, nv), full)],
+        )
+    arrived = lax.ppermute(sent, "orb", [(d, d ^ (orb_count >> 1)) for d in range(orb_count)])
+    gamma, density = vmem_call(
+        finish_kernel, "finish", [kept, arrived, gamma_same] + returned,
+        [((nv, naux), full), ((1, rows, nv), full)], pin=False,
+    )
+    return gamma[None, None], density
 
 
 def fit_kernel(factor_ref, *refs):

time: 58.2 us -> 54.4 us (0.935)
  waiting for transfers between devices: 21.2 us -> 16.1 us
  starting transfers between devices: 23.8 us -> 26.3 us
  other arithmetic: 0.64 us -> 0 us
  Pallas kernels: 11.6 us -> 11 us
    ppermute x9, waiting for transfers between devices: 10.3 us -> 5.94 us  [the longest x3 3.67 us: local_in_vmem(): lax.ppermute(sent, 'orb', [(d, d ^ 1 << bit - 1) for d in range(orb_count)])]
    ppermute x1, starting transfers between devices: 0.6 us -> 1.83 us  [local_in_vmem(): late_row = lax.ppermute(row, 'spin', across)]
    ppermute x9, starting transfers between devices: 6.88 us -> 7.92 us  [the longest x3 3.49 us: local_in_vmem(): lax.ppermute(sent, 'orb', [(d, d ^ 1 << bit - 1) for d in range(orb_count)])]
    ppermute x7, waiting for transfers between devices: 9.97 us -> 9.23 us  [local_in_vmem(): lax.ppermute(lane, 'orb', moves)]
    broadcast_in_dim x1 -> x0, other arithmetic: 0.61 us -> none  [local_in_vmem(): return (gamma[None, None], density[None])]
    pallas_call x9 -> x14, Pallas kernels: 11.6 us -> 11 us  [vmem_call(): pl.pallas_call(kernel, in_specs=[hbm] * in_hbm + [vmem] * (len(operands)...]
  transfers between devices with their start and end apart: 19 -> 19, of which waited for: 13 -> 10; matrix products, arithmetic and copies ran while one was open for 0% -> 0% of each run, Pallas kernels for 12% -> 14%
where the time goes in v3:
time: 54.4 us; the launch traced here: 54.2 us
  starting transfers between devices  26.3 us (48%)
  waiting for transfers between devices  16.1 us (30%)
  Pallas kernels  11 us (20%)
  between operations  0.79 us (1%)
    ppermute x7, starting transfers between devices, local_in_vmem(): lax.ppermute(lane, 'orb', moves)  14.5 us
    pallas_call x14, Pallas kernels, vmem_call(): pl.pallas_call(kernel, in_specs=[hbm] * in_hbm + [vmem] * (len(operands)...  11 us
    ppermute x7, waiting for transfers between devices, local_in_vmem(): lax.ppermute(lane, 'orb', moves)  9.23 us
    ppermute x3, waiting for transfers between devices, local_in_vmem(): lax.ppermute(sent, 'orb', [(d, d ^ 1 << bit - 1) for d in range(orb_count)])  3.67 us
    ppermute x3, starting transfers between devices, local_in_vmem(): lax.ppermute(sent, 'orb', [(d, d ^ 1 << bit - 1) for d in range(orb_count)])  3.49 us
    ppermute x1, starting transfers between devices, local_in_vmem(): lax.ppermute(sent, 'orb', [(d, d ^ orb_count >> 1) for d in range(orb_cou...  2.66 us
    ppermute x1, starting transfers between devices, local_in_vmem(): late_row = lax.ppermute(row, 'spin', across)  1.83 us
    ppermute x1, starting transfers between devices, local_in_vmem(): returned = [lax.ppermute(piece, 'spin', across) for piece in gamma_other]  1.55 us
  transfers between devices with their start and end apart: 19, of which 10 were waited for; matrix products, arithmetic and copies ran while one was open for 0% of the time, Pallas kernels for 14%

profile of v3, /device:TPU:0, one launch (start us, length us, event | category | flops | bytes accessed | tf_op | source)
XLA Modules:
  0.0 54.2 jit_solution(6282474512064335777)
XLA Ops:
  0.6 0.5 collective-permute-start
  1.1 2.6 %collective-permute-start.1 = (bf16[16,32,256]{2,1,0:T(8,128)(2,1)}, bf16[16,32,256]{2,1,0:T(8,128)(2,1)S(1)}, u32[]{:S(2)}, u32[]{:S(2)}) collective-permute-start(bf16[16,32,256]{2,1,0:T(8,128)(2,1)} %bitcast.6), channel_id=1, source_target_pairs={{0,4},{4,8},{8,12},{12,14},{14,10},{10,6},{6,2},{2,0},{5,1},{9,5},... | collective-permute-start | bytes 786440 | tf_op jit(solution)/shard_map/ppermute | solution.py:251
  3.8 0.0 collective-permute-done.refs_2_.refs_0_
  3.8 1.7 %collective-permute-start.2 = (bf16[16,32,256]{2,1,0:T(8,128)(2,1)S(1)}, bf16[16,32,256]{2,1,0:T(8,128)(2,1)S(1)}, u32[]{:S(2)}, u32[]{:S(2)}) collective-permute-start(bf16[16,32,256]{2,1,0:T(8,128)(2,1)S(1)} %collective-permute-done.refs_2_.refs_0_), channel_id=1, source_target_pairs={{0,4},{4,8},{8,12},{12,14},{14,10},{10,6},{6,2},{2,0},{5,1},{9,5},... | collective-permute-start | bytes 786440 | tf_op jit(solution)/shard_map/ppermute | solution.py:251
  5.5 2.8 %collective-permute-done.1.refs_0_.refs_1_ = bf16[16,32,256]{2,1,0:T(8,128)(2,1)S(1)} collective-permute-done((bf16[16,32,256]{2,1,0:T(8,128)(2,1)}, bf16[16,32,256]{2,1,0:T(8,128)(2,1)S(1)}, u32[]{:S(2)}, u32[]{:S(2)}) %collective-permute-start.1) | collective-permute-done | bytes 262176 | tf_op jit(solution)/shard_map/ppermute | solution.py:251
  8.3 2.1 %collective-permute-start.3 = (bf16[16,32,256]{2,1,0:T(8,128)(2,1)S(1)}, bf16[16,32,256]{2,1,0:T(8,128)(2,1)S(1)}, u32[]{:S(2)}, u32[]{:S(2)}) collective-permute-start(bf16[16,32,256]{2,1,0:T(8,128)(2,1)S(1)} %collective-permute-done.1.refs_0_.refs_1_), channel_id=1, source_target_pairs={{0,4},{4,8},{8,12},{12,14},{14,10},{10,6},{6,2},{2,0},{5,1},{9,5},... | collective-permute-start | bytes 786440 | tf_op jit(solution)/shard_map/ppermute | solution.py:251
  10.4 0.7 %collective-permute-done.2.refs_1_.refs_2_ = bf16[16,32,256]{2,1,0:T(8,128)(2,1)S(1)} collective-permute-done((bf16[16,32,256]{2,1,0:T(8,128)(2,1)S(1)}, bf16[16,32,256]{2,1,0:T(8,128)(2,1)S(1)}, u32[]{:S(2)}, u32[]{:S(2)}) %collective-permute-start.2) | collective-permute-done | bytes 262176 | tf_op jit(solution)/shard_map/ppermute | solution.py:251
  11.1 2.1 %collective-permute-start.4 = (bf16[16,32,256]{2,1,0:T(8,128)(2,1)S(1)}, bf16[16,32,256]{2,1,0:T(8,128)(2,1)S(1)}, u32[]{:S(2)}, u32[]{:S(2)}) collective-permute-start(bf16[16,32,256]{2,1,0:T(8,128)(2,1)S(1)} %collective-permute-done.2.refs_1_.refs_2_), channel_id=1, source_target_pairs={{0,4},{4,8},{8,12},{12,14},{14,10},{10,6},{6,2},{2,0},{5,1},{9,5},... | collective-permute-start | bytes 786440 | tf_op jit(solution)/shard_map/ppermute | solution.py:251
  13.2 0.1 stack.4
  13.2 1.4 %collective-permute-done.3.refs_0_.refs_3_ = bf16[16,32,256]{2,1,0:T(8,128)(2,1)S(1)} collective-permute-done((bf16[16,32,256]{2,1,0:T(8,128)(2,1)S(1)}, bf16[16,32,256]{2,1,0:T(8,128)(2,1)S(1)}, u32[]{:S(2)}, u32[]{:S(2)}) %collective-permute-start.3) | collective-permute-done | bytes 262176 | tf_op jit(solution)/shard_map/ppermute | solution.py:251
  14.7 2.1 %collective-permute-start.7 = (bf16[16,32,256]{2,1,0:T(8,128)(2,1)S(1)}, bf16[16,32,256]{2,1,0:T(8,128)(2,1)S(1)}, u32[]{:S(2)}, u32[]{:S(2)}) collective-permute-start(bf16[16,32,256]{2,1,0:T(8,128)(2,1)S(1)} %collective-permute-done.3.refs_0_.refs_3_), channel_id=1, source_target_pairs={{0,4},{4,8},{8,12},{12,14},{14,10},{10,6},{6,2},{2,0},{5,1},{9,5},... | collective-permute-start | bytes 786440 | tf_op jit(solution)/shard_map/ppermute | solution.py:251
  16.7 0.0 collective-permute-start.5
  16.7 0.7 %collective-permute-done.4.refs_1_.refs_4_ = bf16[16,32,256]{2,1,0:T(8,128)(2,1)S(1)} collective-permute-done((bf16[16,32,256]{2,1,0:T(8,128)(2,1)S(1)}, bf16[16,32,256]{2,1,0:T(8,128)(2,1)S(1)}, u32[]{:S(2)}, u32[]{:S(2)}) %collective-permute-start.4) | collective-permute-done | bytes 262176 | tf_op jit(solution)/shard_map/ppermute | solution.py:251
  17.5 2.1 %collective-permute-start.8 = (bf16[16,32,256]{2,1,0:T(8,128)(2,1)S(1)}, bf16[16,32,256]{2,1,0:T(8,128)(2,1)S(1)}, u32[]{:S(2)}, u32[]{:S(2)}) collective-permute-start(bf16[16,32,256]{2,1,0:T(8,128)(2,1)S(1)} %collective-permute-done.4.refs_1_.refs_4_), channel_id=1, source_target_pairs={{0,4},{4,8},{8,12},{12,14},{14,10},{10,6},{6,2},{2,0},{5,1},{9,5},... | collective-permute-start | bytes 786440 | tf_op jit(solution)/shard_map/ppermute | solution.py:251
  19.6 1.5 %collective-permute-start.9 = (bf16[160,256]{1,0:T(8,128)(2,1)S(1)}, bf16[160,256]{1,0:T(8,128)(2,1)S(1)}, u32[]{:S(2)}, u32[]{:S(2)}) collective-permute-start(bf16[160,256]{1,0:T(8,128)(2,1)S(1)} %early_row.1), channel_id=1, source_target_pairs={{0,16},{16,0},{1,17},{17,1},{2,18},{18,2},{3,19},{19,3},{4,20},{20... | collective-permute-start | bytes 245768 | tf_op jit(solution)/shard_map/ppermute | solution.py:256
  21.1 0.0 copy-start
  21.1 0.0 copy-start.1
  21.1 0.0 copy-start.2
  21.1 0.1 collective-permute-start.6
  21.2 0.0 collective-permute-done.7.refs_0_.refs_7_.refs_2_
  21.2 1.9 %collective-permute-start.11 = (bf16[16,32,256]{2,1,0:T(8,128)(2,1)S(1)}, bf16[16,32,256]{2,1,0:T(8,128)(2,1)S(1)}, u32[]{:S(2)}, u32[]{:S(2)}) collective-permute-start(bf16[16,32,256]{2,1,0:T(8,128)(2,1)S(1)} %collective-permute-done.7.refs_0_.refs_7_.refs_2_), channel_id=1, source_target_pairs={{0,4},{4,8},{8,12},{12,14},{14,10},{10,6},{6,2},{2,0},{5,1},{9,5},... | collective-permute-start | bytes 786440 | tf_op jit(solution)/shard_map/ppermute | solution.py:251
  23.1 0.9 %collective-permute-done.9.refs_2_.early_ref = bf16[160,256]{1,0:T(8,128)(2,1)S(1)} collective-permute-done((bf16[160,256]{1,0:T(8,128)(2,1)S(1)}, bf16[160,256]{1,0:T(8,128)(2,1)S(1)}, u32[]{:S(2)}, u32[]{:S(2)}) %collective-permute-start.9) | collective-permute-done | bytes 81952 | tf_op jit(solution)/shard_map/ppermute | solution.py:256
  24.0 0.0 collective-permute-done.8.refs_1_.refs_8_.refs_3_
  24.0 0.1 collective-permute-start.10
  24.1 3.5 %collective-permute-done.11.refs_0_.refs_10_.refs_5_ = bf16[16,32,256]{2,1,0:T(8,128)(2,1)S(1)} collective-permute-done((bf16[16,32,256]{2,1,0:T(8,128)(2,1)S(1)}, bf16[16,32,256]{2,1,0:T(8,128)(2,1)S(1)}, u32[]{:S(2)}, u32[]{:S(2)}) %collective-permute-start.11) | collective-permute-done | bytes 262176 | tf_op jit(solution)/shard_map/ppermute | solution.py:251
  27.7 0.1 collective-permute-start.12
  27.7 0.0 collective-permute-done.5.refs_5_.refs_0_
  27.7 0.0 collective-permute-done.6.refs_6_.refs_1_
  27.8 1.5 %collective-permute-done.12.refs_11_.refs_6_ = bf16[1,16,32,256]{3,2,1,0:T(8,128)(2,1)S(1)} collective-permute-done((bf16[1,16,32,256]{3,2,1,0:T(8,128)(2,1)S(1)}, bf16[1,16,32,256]{3,2,1,0:T(8,128)(2,1)S(1)}, u32[]{:S(2)}, u32[]{:S(2)}) %collective-permute-start.12) | collective-permute-done | bytes 262176 | tf_op jit(solution)/shard_map/ppermute | solution.py:262
  29.3 0.0 collective-permute-done.10.refs_9_.refs_4_
  29.3 1.8 %collective-permute-start.13 = (bf16[352,256]{1,0:T(8,128)(2,1)S(1)}, bf16[352,256]{1,0:T(8,128)(2,1)S(1)}, u32[]{:S(2)}, u32[]{:S(2)}) collective-permute-start(bf16[352,256]{1,0:T(8,128)(2,1)S(1)} %late_row.1), channel_id=1, source_target_pairs={{0,16},{16,0},{1,17},{17,1},{2,18},{18,2},{3,19},{19,3},{4,20},{20... | collective-permute-start | bytes 540680 | tf_op jit(solution)/shard_map/ppermute | solution.py:267
  31.1 0.0 copy-done
  31.1 0.0 copy-done.1
  31.1 0.0 copy-done.2
  31.1 4.9 %fit_same.1 = (bf16[512,512]{1,0:T(8,128)(2,1)S(1)}, bf16[512,4096]{1,0:T(8,128)(2,1)S(1)}, bf16[256,4096]{1,0:T(8,128)(2,1)S(1)}, f32[256,256]{1,0:T(8,128)S(1)}) custom-call(f32[2,16]{1,0:T(2,128)S(1)} %copy-done.2, f32[2,256]{1,0:T(2,128)S(1)} %copy-done.1, bf16[512,512]{1,0:T(8,128)(2,1)S(1)} %copy-done, ...), custom_call_target="tpu_custom_call" | custom-call | bytes 4720768 | tf_op jit(solution)/shard_map/fit_same/pallas_call | solution.py:224
  36.0 0.0 collective-permute-done.13.late_ref
  36.0 2.6 %opposite.1 = (bf16[256,4096]{1,0:T(8,128)(2,1)S(1)}, f32[8,16,256]{2,1,0:T(8,128)S(1)}, f32[8,16,256]{2,1,0:T(8,128)S(1)}) custom-call(f32[2,16]{1,0:T(2,128)S(1)} %copy-done.2, f32[2,256]{1,0:T(2,128)S(1)} %copy-done.1, bf16[512,512]{1,0:T(8,128)(2,1)S(1)} %get-tuple-element.17.factor_ref, bf16[160,256]{1,0:T(8,128)(2,1)S(1)} %collective-permute-done.9.refs_2_.early_ref, ...), custom_call_target="tpu_custom_call" | custom-call | flops 1610612736 | bytes 5245056 | tf_op jit(solution)/shard_map/opposite/pallas_call | solution.py:224
  38.6 0.1 collective-permute-start.14
  38.7 1.3 %collective-permute-done.14.arrived = f32[8,16,256]{2,1,0:T(8,128)S(1)} collective-permute-done((f32[8,16,256]{2,1,0:T(8,128)S(1)}, f32[8,16,256]{2,1,0:T(8,128)S(1)}, u32[]{:S(2)}, u32[]{:S(2)}) %collective-permute-start.14) | collective-permute-done | bytes 131104 | tf_op jit(solution)/shard_map/ppermute | solution.py:292
  40.0 1.8 %collective-permute-start.15 = (f32[4,16,256]{2,1,0:T(8,128)S(1)}, f32[4,16,256]{2,1,0:T(8,128)S(1)}, u32[]{:S(2)}, u32[]{:S(2)}) collective-permute-start(f32[4,16,256]{2,1,0:T(8,128)S(1)} %get-tuple-element.23), channel_id=1, source_target_pairs={{0,2},{1,3},{2,0},{3,1},{4,6},{5,7},{6,4},{7,5},{8,10},{9,11},{10,... | collective-permute-start | bytes 196616 | tf_op jit(solution)/shard_map/ppermute | solution.py:292
  41.8 1.3 %gamma_other.1 = bf16[256,512]{1,0:T(8,128)(2,1)S(1)} custom-call(bf16[256,4096]{1,0:T(8,128)(2,1)S(1)} %get-tuple-element.29.amp_ref, bf16[512,4096]{1,0:T(8,128)(2,1)S(1)} %get-tuple-element.18.fitted_ref), custom_call_target="tpu_custom_call" | custom-call | flops 1073741824 | bytes 6291456 | tf_op jit(solution)/shard_map/gamma_other/pallas_call | solution.py:224
  43.1 1.5 %collective-permute-start.18 = (bf16[256,512]{1,0:T(8,128)(2,1)S(1)}, bf16[256,512]{1,0:T(8,128)(2,1)S(1)}, u32[]{:S(2)}, u32[]{:S(2)}) collective-permute-start(bf16[256,512]{1,0:T(8,128)(2,1)S(1)} %gamma_other.1), channel_id=1, source_target_pairs={{0,16},{16,0},{1,17},{17,1},{2,18},{18,2},{3,19},{19,3},{4,20},{20... | collective-permute-start | bytes 786440 | tf_op jit(solution)/shard_map/ppermute | solution.py:290
  44.6 0.0 collective-permute-done.15.arrived
  44.7 1.6 %collective-permute-start.16 = (f32[2,16,256]{2,1,0:T(8,128)S(1)}, f32[2,16,256]{2,1,0:T(8,128)S(1)}, u32[]{:S(2)}, u32[]{:S(2)}) collective-permute-start(f32[2,16,256]{2,1,0:T(8,128)S(1)} %get-tuple-element.25), channel_id=1, source_target_pairs={{0,4},{1,5},{2,6},{3,7},{4,0},{5,1},{6,2},{7,3},{8,12},{9,13},{10,... | collective-permute-start | bytes 98312 | tf_op jit(solution)/shard_map/ppermute | solution.py:292
  46.3 2.3 %collective-permute-done.16.arrived = f32[2,16,256]{2,1,0:T(8,128)S(1)} collective-permute-done((f32[2,16,256]{2,1,0:T(8,128)S(1)}, f32[2,16,256]{2,1,0:T(8,128)S(1)}, u32[]{:S(2)}, u32[]{:S(2)}) %collective-permute-start.16) | collective-permute-done | bytes 32800 | tf_op jit(solution)/shard_map/ppermute | solution.py:292
  48.7 2.7 %collective-permute-start.17 = (f32[1,16,256]{2,1,0:T(8,128)S(1)}, f32[1,16,256]{2,1,0:T(8,128)S(1)}, u32[]{:S(2)}, u32[]{:S(2)}) collective-permute-start(f32[1,16,256]{2,1,0:T(8,128)S(1)} %get-tuple-element.27), channel_id=1, source_target_pairs={{0,8},{1,9},{2,10},{3,11},{4,12},{5,13},{6,14},{7,15},{8,0},{9,1},... | collective-permute-start | bytes 49160 | tf_op jit(solution)/shard_map/ppermute | solution.py:299
  51.3 1.3 %gamma_same.1.gamma_in = f32[256,512]{1,0:T(8,128)S(1)} custom-call(bf16[256,4096]{1,0:T(8,128)(2,1)S(1)} %get-tuple-element.28.amp_ref, bf16[512,4096]{1,0:T(8,128)(2,1)S(1)} %get-tuple-element.18.fitted_ref), custom_call_target="tpu_custom_call" | custom-call | flops 2147483648 | bytes 6291456 | tf_op jit(solution)/shard_map/gamma_same/pallas_call | solution.py:224
  52.6 0.8 %collective-permute-done.17.arrived = f32[1,16,256]{2,1,0:T(8,128)S(1)} collective-permute-done((f32[1,16,256]{2,1,0:T(8,128)S(1)}, f32[1,16,256]{2,1,0:T(8,128)S(1)}, u32[]{:S(2)}, u32[]{:S(2)}) %collective-permute-start.17) | collective-permute-done | bytes 16416 | tf_op jit(solution)/shard_map/ppermute | solution.py:299
  53.4 0.0 collective-permute-done.18.refs_0_
  53.4 0.8 %finish.1 = (f32[256,512]{1,0:T(8,128)}, f32[1,16,256]{2,1,0:T(8,128)}) custom-call(f32[1,16,256]{2,1,0:T(8,128)S(1)} %get-tuple-element.26.kept_in, f32[1,16,256]{2,1,0:T(8,128)S(1)} %collective-permute-done.17.arrived, f32[256,512]{1,0:T(8,128)S(1)} %gamma_same.1.gamma_in, bf16[256,512]{1,0:T(8,128)(2,1)S(1)} %collective-permute-done.18.refs_0_), custom_call_target="tpu_custom_call" | custom-call | bytes 819200 | tf_op jit(solution)/shard_map/finish/pallas_call | solution.py:224
  (8 shorter events, 0.2 us)
Async XLA Ops:
  0.6 3.2 %collective-permute-start = (bf16[16,32,256]{2,1,0:T(8,128)(2,1)}, bf16[16,32,256]{2,1,0:T(8,128)(2,1)S(1)}, u32[]{:S(2)}, u32[]{:S(2)}) collective-permute-start(bf16[16,32,256]{2,1,0:T(8,128)(2,1)} %bitcast.5), channel_id=1, source_target_pairs={{0,1},{1,0},{2,3},{3,2},{4,5},{5,4},{6,7},{7,6},{8,9},{9,8},{10,11... | collective-permute-start | bytes 786440 | tf_op jit(solution)/shard_map/ppermute | solution.py:247
  1.1 7.1 %collective-permute-start.1 = (bf16[16,32,256]{2,1,0:T(8,128)(2,1)}, bf16[16,32,256]{2,1,0:T(8,128)(2,1)S(1)}, u32[]{:S(2)}, u32[]{:S(2)}) collective-permute-start(bf16[16,32,256]{2,1,0:T(8,128)(2,1)} %bitcast.6), channel_id=1, source_target_pairs={{0,4},{4,8},{8,12},{12,14},{14,10},{10,6},{6,2},{2,0},{5,1},{9,5},... | collective-permute-start | bytes 786440 | tf_op jit(solution)/shard_map/ppermute | solution.py:251
  3.8 7.3 %collective-permute-start.2 = (bf16[16,32,256]{2,1,0:T(8,128)(2,1)S(1)}, bf16[16,32,256]{2,1,0:T(8,128)(2,1)S(1)}, u32[]{:S(2)}, u32[]{:S(2)}) collective-permute-start(bf16[16,32,256]{2,1,0:T(8,128)(2,1)S(1)} %collective-permute-done.refs_2_.refs_0_), channel_id=1, source_target_pairs={{0,4},{4,8},{8,12},{12,14},{14,10},{10,6},{6,2},{2,0},{5,1},{9,5},... | collective-permute-start | bytes 786440 | tf_op jit(solution)/shard_map/ppermute | solution.py:251
  8.3 6.4 %collective-permute-start.3 = (bf16[16,32,256]{2,1,0:T(8,128)(2,1)S(1)}, bf16[16,32,256]{2,1,0:T(8,128)(2,1)S(1)}, u32[]{:S(2)}, u32[]{:S(2)}) collective-permute-start(bf16[16,32,256]{2,1,0:T(8,128)(2,1)S(1)} %collective-permute-done.1.refs_0_.refs_1_), channel_id=1, source_target_pairs={{0,4},{4,8},{8,12},{12,14},{14,10},{10,6},{6,2},{2,0},{5,1},{9,5},... | collective-permute-start | bytes 786440 | tf_op jit(solution)/shard_map/ppermute | solution.py:251
  11.1 6.4 %collective-permute-start.4 = (bf16[16,32,256]{2,1,0:T(8,128)(2,1)S(1)}, bf16[16,32,256]{2,1,0:T(8,128)(2,1)S(1)}, u32[]{:S(2)}, u32[]{:S(2)}) collective-permute-start(bf16[16,32,256]{2,1,0:T(8,128)(2,1)S(1)} %collective-permute-done.2.refs_1_.refs_2_), channel_id=1, source_target_pairs={{0,4},{4,8},{8,12},{12,14},{14,10},{10,6},{6,2},{2,0},{5,1},{9,5},... | collective-permute-start | bytes 786440 | tf_op jit(solution)/shard_map/ppermute | solution.py:251
  14.7 6.5 %collective-permute-start.7 = (bf16[16,32,256]{2,1,0:T(8,128)(2,1)S(1)}, bf16[16,32,256]{2,1,0:T(8,128)(2,1)S(1)}, u32[]{:S(2)}, u32[]{:S(2)}) collective-permute-start(bf16[16,32,256]{2,1,0:T(8,128)(2,1)S(1)} %collective-permute-done.3.refs_0_.refs_3_), channel_id=1, source_target_pairs={{0,4},{4,8},{8,12},{12,14},{14,10},{10,6},{6,2},{2,0},{5,1},{9,5},... | collective-permute-start | bytes 786440 | tf_op jit(solution)/shard_map/ppermute | solution.py:251
  16.7 11.0 %collective-permute-start.5 = (bf16[3,16,32,256]{3,2,1,0:T(8,128)(2,1)S(1)}, bf16[3,16,32,256]{3,2,1,0:T(8,128)(2,1)S(1)}, u32[]{:S(2)}, u32[]{:S(2)}) collective-permute-start(bf16[3,16,32,256]{3,2,1,0:T(8,128)(2,1)S(1)} %stack.4), channel_id=1, source_target_pairs={{0,1},{1,0},{2,3},{3,2},{4,5},{5,4},{6,7},{7,6},{8,9},{9,8},{10,11... | collective-permute-start | bytes 2359304 | tf_op jit(solution)/shard_map/ppermute | solution.py:262
  17.5 6.5 %collective-permute-start.8 = (bf16[16,32,256]{2,1,0:T(8,128)(2,1)S(1)}, bf16[16,32,256]{2,1,0:T(8,128)(2,1)S(1)}, u32[]{:S(2)}, u32[]{:S(2)}) collective-permute-start(bf16[16,32,256]{2,1,0:T(8,128)(2,1)S(1)} %collective-permute-done.4.refs_1_.refs_4_), channel_id=1, source_target_pairs={{0,4},{4,8},{8,12},{12,14},{14,10},{10,6},{6,2},{2,0},{5,1},{9,5},... | collective-permute-start | bytes 786440 | tf_op jit(solution)/shard_map/ppermute | solution.py:251
  19.6 4.4 %collective-permute-start.9 = (bf16[160,256]{1,0:T(8,128)(2,1)S(1)}, bf16[160,256]{1,0:T(8,128)(2,1)S(1)}, u32[]{:S(2)}, u32[]{:S(2)}) collective-permute-start(bf16[160,256]{1,0:T(8,128)(2,1)S(1)} %early_row.1), channel_id=1, source_target_pairs={{0,16},{16,0},{1,17},{17,1},{2,18},{18,2},{3,19},{19,3},{4,20},{20... | collective-permute-start | bytes 245768 | tf_op jit(solution)/shard_map/ppermute | solution.py:256
  21.1 10.0 %copy-start = (bf16[512,512]{1,0:T(8,128)(2,1)S(1)}, bf16[512,512]{1,0:T(8,128)(2,1)}, u32[]{:S(2)}) copy-start(bf16[512,512]{1,0:T(8,128)(2,1)} %given_ref.1) | copy-start | bytes 1572868
  21.1 10.0 %copy-start.1 = (f32[2,256]{1,0:T(2,128)S(1)}, f32[2,256]{1,0:T(2,128)}, u32[]{:S(2)}) copy-start(f32[2,256]{1,0:T(2,128)} %virt_ref.3) | copy-start | bytes 6148
  21.1 10.0 %copy-start.2 = (f32[2,16]{1,0:T(2,128)S(1)}, f32[2,16]{1,0:T(2,128)}, u32[]{:S(2)}) copy-start(f32[2,16]{1,0:T(2,128)} %occ_ref.3) | copy-start | bytes 388
  21.1 6.6 %collective-permute-start.6 = (bf16[2,16,32,256]{3,2,1,0:T(8,128)(2,1)S(1)}, bf16[2,16,32,256]{3,2,1,0:T(8,128)(2,1)S(1)}, u32[]{:S(2)}, u32[]{:S(2)}) collective-permute-start(bf16[2,16,32,256]{3,2,1,0:T(8,128)(2,1)S(1)} %stack.5), channel_id=1, source_target_pairs={{0,1},{1,0},{2,3},{3,2},{4,5},{5,4},{6,7},{7,6},{8,9},{9,8},{10,11... | collective-permute-start | bytes 1572872 | tf_op jit(solution)/shard_map/ppermute | solution.py:262
  21.2 6.4 %collective-permute-start.11 = (bf16[16,32,256]{2,1,0:T(8,128)(2,1)S(1)}, bf16[16,32,256]{2,1,0:T(8,128)(2,1)S(1)}, u32[]{:S(2)}, u32[]{:S(2)}) collective-permute-start(bf16[16,32,256]{2,1,0:T(8,128)(2,1)S(1)} %collective-permute-done.7.refs_0_.refs_7_.refs_2_), channel_id=1, source_target_pairs={{0,4},{4,8},{8,12},{12,14},{14,10},{10,6},{6,2},{2,0},{5,1},{9,5},... | collective-permute-start | bytes 786440 | tf_op jit(solution)/shard_map/ppermute | solution.py:251
  24.0 5.2 %collective-permute-start.10 = (bf16[2,16,32,256]{3,2,1,0:T(8,128)(2,1)S(1)}, bf16[2,16,32,256]{3,2,1,0:T(8,128)(2,1)S(1)}, u32[]{:S(2)}, u32[]{:S(2)}) collective-permute-start(bf16[2,16,32,256]{3,2,1,0:T(8,128)(2,1)S(1)} %stack.6), channel_id=1, source_target_pairs={{0,1},{1,0},{2,3},{3,2},{4,5},{5,4},{6,7},{7,6},{8,9},{9,8},{10,11... | collective-permute-start | bytes 1572872 | tf_op jit(solution)/shard_map/ppermute | solution.py:262
  27.7 1.6 %collective-permute-start.12 = (bf16[1,16,32,256]{3,2,1,0:T(8,128)(2,1)S(1)}, bf16[1,16,32,256]{3,2,1,0:T(8,128)(2,1)S(1)}, u32[]{:S(2)}, u32[]{:S(2)}) collective-permute-start(bf16[1,16,32,256]{3,2,1,0:T(8,128)(2,1)S(1)} %stack.7), channel_id=1, source_target_pairs={{0,1},{1,0},{2,3},{3,2},{4,5},{5,4},{6,7},{7,6},{8,9},{9,8},{10,11... | collective-permute-start | bytes 786440 | tf_op jit(solution)/shard_map/ppermute | solution.py:262
  29.3 6.7 %collective-permute-start.13 = (bf16[352,256]{1,0:T(8,128)(2,1)S(1)}, bf16[352,256]{1,0:T(8,128)(2,1)S(1)}, u32[]{:S(2)}, u32[]{:S(2)}) collective-permute-start(bf16[352,256]{1,0:T(8,128)(2,1)S(1)} %late_row.1), channel_id=1, source_target_pairs={{0,16},{16,0},{1,17},{17,1},{2,18},{18,2},{3,19},{19,3},{4,20},{20... | collective-permute-start | bytes 540680 | tf_op jit(solution)/shard_map/ppermute | solution.py:267
  38.6 1.4 %collective-permute-start.14 = (f32[8,16,256]{2,1,0:T(8,128)S(1)}, f32[8,16,256]{2,1,0:T(8,128)S(1)}, u32[]{:S(2)}, u32[]{:S(2)}) collective-permute-start(f32[8,16,256]{2,1,0:T(8,128)S(1)} %get-tuple-element.21), channel_id=1, source_target_pairs={{0,1},{1,0},{2,3},{3,2},{4,5},{5,4},{6,7},{7,6},{8,9},{9,8},{10,11... | collective-permute-start | bytes 393224 | tf_op jit(solution)/shard_map/ppermute | solution.py:292
  40.0 4.6 %collective-permute-start.15 = (f32[4,16,256]{2,1,0:T(8,128)S(1)}, f32[4,16,256]{2,1,0:T(8,128)S(1)}, u32[]{:S(2)}, u32[]{:S(2)}) collective-permute-start(f32[4,16,256]{2,1,0:T(8,128)S(1)} %get-tuple-element.23), channel_id=1, source_target_pairs={{0,2},{1,3},{2,0},{3,1},{4,6},{5,7},{6,4},{7,5},{8,10},{9,11},{10,... | collective-permute-start | bytes 196616 | tf_op jit(solution)/shard_map/ppermute | solution.py:292
  43.1 10.3 %collective-permute-start.18 = (bf16[256,512]{1,0:T(8,128)(2,1)S(1)}, bf16[256,512]{1,0:T(8,128)(2,1)S(1)}, u32[]{:S(2)}, u32[]{:S(2)}) collective-permute-start(bf16[256,512]{1,0:T(8,128)(2,1)S(1)} %gamma_other.1), channel_id=1, source_target_pairs={{0,16},{16,0},{1,17},{17,1},{2,18},{18,2},{3,19},{19,3},{4,20},{20... | collective-permute-start | bytes 786440 | tf_op jit(solution)/shard_map/ppermute | solution.py:290
  44.7 4.0 %collective-permute-start.16 = (f32[2,16,256]{2,1,0:T(8,128)S(1)}, f32[2,16,256]{2,1,0:T(8,128)S(1)}, u32[]{:S(2)}, u32[]{:S(2)}) collective-permute-start(f32[2,16,256]{2,1,0:T(8,128)S(1)} %get-tuple-element.25), channel_id=1, source_target_pairs={{0,4},{1,5},{2,6},{3,7},{4,0},{5,1},{6,2},{7,3},{8,12},{9,13},{10,... | collective-permute-start | bytes 98312 | tf_op jit(solution)/shard_map/ppermute | solution.py:292
  48.7 4.7 %collective-permute-start.17 = (f32[1,16,256]{2,1,0:T(8,128)S(1)}, f32[1,16,256]{2,1,0:T(8,128)S(1)}, u32[]{:S(2)}, u32[]{:S(2)}) collective-permute-start(f32[1,16,256]{2,1,0:T(8,128)S(1)} %get-tuple-element.27), channel_id=1, source_target_pairs={{0,8},{1,9},{2,10},{3,11},{4,12},{5,13},{6,14},{7,15},{8,0},{9,1},... | collective-permute-start | bytes 49160 | tf_op jit(solution)/shard_map/ppermute | solution.py:299

commit v4 on v3

--- a/solution.py
+++ b/solution.py
@@ -131,22 +131,38 @@
     return (coupling / (occupied_pair - virtual_pair)).astype(jnp.bfloat16)
 
 
-def fit_same_kernel(orb_count, occ_ref, virt_ref, given_ref, *refs):
-    slices, (factor_ref, fitted_ref, amp_ref, dens_ref) = refs[:-7], refs[-7:-3]
-    rows, left, sums = refs[-3:]
+def early_fit_kernel(orb_count, given_ref, *refs):
+    *slices, factor_ref, early_ref, rows = refs
     factor_ref[...] = order_factor(given_ref, rows, orb_count)
+    nv = early_ref.shape[1] // orb_count
+    depth = early_depth(slices)
+    for start in range(0, orb_count, GROUP):
+        raw = [jnp.concatenate(list(pieces(slices, j)), axis=0) for j in range(start, start + GROUP)]
+        columns = slice(start * nv, (start + GROUP) * nv)
+        early_ref[:, columns] = dot(factor_ref[:, :depth], jnp.concatenate(raw, axis=1), NN)
+
+
+def early_depth(slices):
+    return sum(s.shape[-2] * (1 if len(s.shape) == 3 else s.shape[0]) for s in slices)
+
+
+def fit_same_kernel(occ_ref, virt_ref, factor_ref, early_ref, *refs):
+    slices, (fitted_ref, amp_ref, dens_ref, left, sums) = refs[:-5], refs[-5:]
+    first = factor_ref.shape[0] - early_depth(slices)
     spin, own = lax.axis_index("spin"), lax.axis_index("orb")
     count, nv = occ_ref.shape[1], virt_ref.shape[1]
     sums[...] = energy_sums(virt_ref, spin, spin)
     energies = pair_energies(occ_ref, spin, spin, own)
     raw = jnp.concatenate(list(pieces(slices, own)), axis=0)
-    left[...] = dot(factor_ref[...], raw, NN).T.astype(left.dtype)
+    early = early_ref[:, pl.ds(pl.multiple_of(own * nv, nv), nv)]
+    left[...] = (early + dot(factor_ref[:, first:], raw, NN)).T.astype(left.dtype)
     total = None
     for start in range(0, count, GROUP):
         members = range(start, start + GROUP)
         raw = [jnp.concatenate(list(pieces(slices, j)), axis=0) for j in members]
-        fitted = dot(factor_ref[...], jnp.concatenate(raw, axis=1), NN).astype(fitted_ref.dtype)
         columns = slice(start * nv, (start + GROUP) * nv)
+        late = dot(factor_ref[:, first:], jnp.concatenate(raw, axis=1), NN)
+        fitted = (early_ref[:, columns] + late).astype(fitted_ref.dtype)
         fitted_ref[:, columns] = fitted
         couplings = dot(left[...], fitted, NN)
         amps = []
@@ -161,14 +177,14 @@
 
 
 def opposite_all_kernel(
-    occ_ref, virt_ref, factor_ref, early_ref, late_ref, fitted_ref, dens_in,
+    occ_ref, virt_ref, factor_ref, early_ref, late_ref, last_ref, fitted_ref, dens_in,
     amp_ref, kept_ref, sent_ref, left, sums, dens,
 ):
     spin, own = lax.axis_index("spin"), lax.axis_index("orb")
     count, nv = occ_ref.shape[1], virt_ref.shape[1]
     sums[...] = energy_sums(virt_ref, 1 - spin, spin)
     energies = pair_energies(occ_ref, 1 - spin, spin, own)
-    raw = jnp.concatenate([early_ref[...], late_ref[...]], axis=0)
+    raw = jnp.concatenate([early_ref[...], late_ref[...], last_ref[...]], axis=0)
     left[...] = dot(factor_ref[...], raw, NN).T.astype(left.dtype)
     total = dens_in[...]
     for start in range(0, count, GROUP):
@@ -217,7 +233,7 @@
 
 def vmem_call(kernel, name, operands, outs, scratch=(), flops=0, in_hbm=0, pin=True):
     vmem, hbm = pl.BlockSpec(memory_space=pltpu.VMEM), pl.BlockSpec(memory_space=pltpu.HBM)
-    moved = sum(a.size * a.dtype.itemsize for a in operands)
+    moved = sum(a.size * a.dtype.itemsize for a in operands) if flops else 0
     if pin:
         places = [pltpu.HBM] * in_hbm + [pltpu.VMEM] * (len(operands) - in_hbm)
         operands = [pltpu.with_memory_space_constraint(*pair) for pair in zip(operands, places)]
@@ -243,6 +259,7 @@
     half, full = jnp.bfloat16, jnp.float32
     depth = lambda part: width * sum(1 if s.ndim == 3 else s.shape[0] for s in part)
 
+    pair = 2 * count * nv * nv
     steps = orb_count // 4
     lanes = [own, lax.ppermute(own, "orb", swap)]
     slices, swapped, early_row = lanes[1:], [], None
@@ -254,7 +271,12 @@
             sent = len(slices)
             (row,) = vmem_call(row_kernel, "early_row", slices, [((depth(slices), nv), half)])
             early_row = lax.ppermute(row, "spin", across)
-        order = [early_row] if step == steps - 1 else []
+        if step == steps - 1:
+            factor, early = vmem_call(
+                functools.partial(early_fit_kernel, orb_count), "early_fit", [metric_factor] + slices[: sent + 1],
+                [((naux, naux), half), ((naux, count * nv), full)], [((naux, naux), half)], flops=0,
+            )
+        order = [early_row] if step == steps - 1 else [early] if step == steps else []
         (stacked,) = vmem_call(
             functools.partial(stack_kernel, len(lanes + back)), "stack", lanes + back + order,
             [((len(lanes + back),) + own.shape, half)],
@@ -263,19 +285,19 @@
         if step >= steps - 2:
             slices += swapped
             swapped = []
-    (row,) = vmem_call(row_kernel, "late_row", slices[sent:], [((depth(slices[sent:]), nv), half)])
-    late_row = lax.ppermute(row, "spin", across)
-    pair = 2 * count * nv * nv
-    factor, fitted, amp_same, dens_same = vmem_call(
-        functools.partial(fit_same_kernel, orb_count), "fit_same",
-        [occ_energy, virt_energy, metric_factor] + slices,
-        [((naux, naux), half), ((naux, count * nv), half), ((nv, count * nv), half), ((nv, nv), full)],
-        [((naux, naux), half), ((nv, naux), half), ((nv, nv), full)],
+    rows_sent, cut = [early_row], sent+4
+    for part in (slices[sent:cut], slices[cut:]):
+        (row,) = vmem_call(row_kernel, "late_row", part, [((depth(part), nv), half)])
+        rows_sent.append(lax.ppermute(row, "spin", across))
+    fitted, amp_same, dens_same = vmem_call(
+        fit_same_kernel, "fit_same", [occ_energy, virt_energy, factor, early] + slices[sent + 1 :],
+        [((naux, count * nv), half), ((nv, count * nv), half), ((nv, nv), full)],
+        [((nv, naux), half), ((nv, nv), full)],
     )
     rows = nv // orb_count
     amp_other, kept, sent = vmem_call(
         opposite_all_kernel, "opposite",
-        [occ_energy, virt_energy, factor, early_row, late_row, fitted, dens_same],
+        [occ_energy, virt_energy, factor] + rows_sent + [fitted, dens_same],
         [((nv, count * nv), half)] + [((orb_count // 2, rows, nv), full)] * 2,
         [((nv, naux), half), ((nv, nv), full), ((nv, nv), full)],
         flops=pair * (naux + nv),

time: 54.4 us -> 53.2 us (0.978)
  waiting for transfers between devices: 16.1 us -> 13.5 us
  starting transfers between devices: 26.3 us -> 27.4 us
    ppermute x4, waiting for transfers between devices: 1.51 us -> 0.01 us  [local_in_vmem(): swapped.append(lax.ppermute(stacked, 'orb', swap))]
    ppermute x7, waiting for transfers between devices: 9.23 us -> 7.9 us  [local_in_vmem(): lax.ppermute(lane, 'orb', moves)]
    ppermute x1 -> x2, starting transfers between devices: 1.83 us -> 3.09 us  [local_in_vmem(): rows_sent.append(lax.ppermute(row, 'spin', across))]
    pallas_call x14 -> x16, Pallas kernels: 11 us -> 11.3 us  [vmem_call(): pl.pallas_call(kernel, in_specs=[hbm] * in_hbm + [vmem] * (len(operands)...]
  transfers between devices with their start and end apart: 19 -> 20, of which waited for: 10 -> 10; matrix products, arithmetic and copies ran while one was open for 0% -> 0% of each run, Pallas kernels for 14% -> 15%
where the time goes in v4:
time: 53.2 us; the launch traced here: 53.1 us
  starting transfers between devices  27.4 us (52%)
  waiting for transfers between devices  13.5 us (25%)
  Pallas kernels  11.3 us (21%)
  between operations  0.8 us (2%)
    ppermute x7, starting transfers between devices, local_in_vmem(): lax.ppermute(lane, 'orb', moves)  14.4 us
    pallas_call x16, Pallas kernels, vmem_call(): pl.pallas_call(kernel, in_specs=[hbm] * in_hbm + [vmem] * (len(operands)...  11.3 us
    ppermute x7, waiting for transfers between devices, local_in_vmem(): lax.ppermute(lane, 'orb', moves)  7.9 us
    ppermute x3, waiting for transfers between devices, local_in_vmem(): lax.ppermute(sent, 'orb', [(d, d ^ 1 << bit - 1) for d in range(orb_count)])  3.68 us
    ppermute x3, starting transfers between devices, local_in_vmem(): lax.ppermute(sent, 'orb', [(d, d ^ 1 << bit - 1) for d in range(orb_count)])  3.42 us
    ppermute x2, starting transfers between devices, local_in_vmem(): rows_sent.append(lax.ppermute(row, 'spin', across))  3.09 us
    ppermute x1, starting transfers between devices, local_in_vmem(): lax.ppermute(sent, 'orb', [(d, d ^ orb_count >> 1) for d in range(orb_cou...  2.65 us
    ppermute x1, starting transfers between devices, local_in_vmem(): returned = [lax.ppermute(piece, 'spin', across) for piece in gamma_other]  1.56 us
  transfers between devices with their start and end apart: 20, of which 10 were waited for; matrix products, arithmetic and copies ran while one was open for 0% of the time, Pallas kernels for 15%

profile of v4, /device:TPU:0, one launch (start us, length us, event | category | flops | bytes accessed | tf_op | source)
XLA Modules:
  0.0 53.1 jit_solution(10341211846071824204)
XLA Ops:
  0.6 0.0 copy-start
  0.6 0.5 collective-permute-start
  1.2 2.6 %collective-permute-start.1 = (bf16[16,32,256]{2,1,0:T(8,128)(2,1)}, bf16[16,32,256]{2,1,0:T(8,128)(2,1)S(1)}, u32[]{:S(2)}, u32[]{:S(2)}) collective-permute-start(bf16[16,32,256]{2,1,0:T(8,128)(2,1)} %bitcast.6), channel_id=1, source_target_pairs={{0,4},{4,8},{8,12},{12,14},{14,10},{10,6},{6,2},{2,0},{5,1},{9,5},... | collective-permute-start | bytes 786440 | tf_op jit(solution)/shard_map/ppermute | solution.py:268
  3.8 0.0 collective-permute-done.refs_2_.refs_0_
  3.8 1.7 %collective-permute-start.2 = (bf16[16,32,256]{2,1,0:T(8,128)(2,1)S(1)}, bf16[16,32,256]{2,1,0:T(8,128)(2,1)S(1)}, u32[]{:S(2)}, u32[]{:S(2)}) collective-permute-start(bf16[16,32,256]{2,1,0:T(8,128)(2,1)S(1)} %collective-permute-done.refs_2_.refs_0_), channel_id=1, source_target_pairs={{0,4},{4,8},{8,12},{12,14},{14,10},{10,6},{6,2},{2,0},{5,1},{9,5},... | collective-permute-start | bytes 786440 | tf_op jit(solution)/shard_map/ppermute | solution.py:268
  5.5 2.8 %collective-permute-done.1.refs_0_.refs_1_ = bf16[16,32,256]{2,1,0:T(8,128)(2,1)S(1)} collective-permute-done((bf16[16,32,256]{2,1,0:T(8,128)(2,1)}, bf16[16,32,256]{2,1,0:T(8,128)(2,1)S(1)}, u32[]{:S(2)}, u32[]{:S(2)}) %collective-permute-start.1) | collective-permute-done | bytes 262176 | tf_op jit(solution)/shard_map/ppermute | solution.py:268
  8.3 2.1 %collective-permute-start.3 = (bf16[16,32,256]{2,1,0:T(8,128)(2,1)S(1)}, bf16[16,32,256]{2,1,0:T(8,128)(2,1)S(1)}, u32[]{:S(2)}, u32[]{:S(2)}) collective-permute-start(bf16[16,32,256]{2,1,0:T(8,128)(2,1)S(1)} %collective-permute-done.1.refs_0_.refs_1_), channel_id=1, source_target_pairs={{0,4},{4,8},{8,12},{12,14},{14,10},{10,6},{6,2},{2,0},{5,1},{9,5},... | collective-permute-start | bytes 786440 | tf_op jit(solution)/shard_map/ppermute | solution.py:268
  10.4 0.7 %collective-permute-done.2.refs_1_.refs_2_ = bf16[16,32,256]{2,1,0:T(8,128)(2,1)S(1)} collective-permute-done((bf16[16,32,256]{2,1,0:T(8,128)(2,1)S(1)}, bf16[16,32,256]{2,1,0:T(8,128)(2,1)S(1)}, u32[]{:S(2)}, u32[]{:S(2)}) %collective-permute-start.2) | collective-permute-done | bytes 262176 | tf_op jit(solution)/shard_map/ppermute | solution.py:268
  11.1 0.1 stack.4
  11.2 0.1 collective-permute-start.5
  11.2 2.1 %collective-permute-start.4 = (bf16[16,32,256]{2,1,0:T(8,128)(2,1)S(1)}, bf16[16,32,256]{2,1,0:T(8,128)(2,1)S(1)}, u32[]{:S(2)}, u32[]{:S(2)}) collective-permute-start(bf16[16,32,256]{2,1,0:T(8,128)(2,1)S(1)} %collective-permute-done.2.refs_1_.refs_2_), channel_id=1, source_target_pairs={{0,4},{4,8},{8,12},{12,14},{14,10},{10,6},{6,2},{2,0},{5,1},{9,5},... | collective-permute-start | bytes 786440 | tf_op jit(solution)/shard_map/ppermute | solution.py:268
  13.4 1.3 %collective-permute-done.3.refs_3_.refs_0_ = bf16[16,32,256]{2,1,0:T(8,128)(2,1)S(1)} collective-permute-done((bf16[16,32,256]{2,1,0:T(8,128)(2,1)S(1)}, bf16[16,32,256]{2,1,0:T(8,128)(2,1)S(1)}, u32[]{:S(2)}, u32[]{:S(2)}) %collective-permute-start.3) | collective-permute-done | bytes 262176 | tf_op jit(solution)/shard_map/ppermute | solution.py:268
  14.7 2.1 %collective-permute-start.8 = (bf16[16,32,256]{2,1,0:T(8,128)(2,1)S(1)}, bf16[16,32,256]{2,1,0:T(8,128)(2,1)S(1)}, u32[]{:S(2)}, u32[]{:S(2)}) collective-permute-start(bf16[16,32,256]{2,1,0:T(8,128)(2,1)S(1)} %collective-permute-done.3.refs_3_.refs_0_), channel_id=1, source_target_pairs={{0,4},{4,8},{8,12},{12,14},{14,10},{10,6},{6,2},{2,0},{5,1},{9,5},... | collective-permute-start | bytes 786440 | tf_op jit(solution)/shard_map/ppermute | solution.py:268
  16.7 0.9 %collective-permute-done.4.refs_4_.refs_1_ = bf16[16,32,256]{2,1,0:T(8,128)(2,1)S(1)} collective-permute-done((bf16[16,32,256]{2,1,0:T(8,128)(2,1)S(1)}, bf16[16,32,256]{2,1,0:T(8,128)(2,1)S(1)}, u32[]{:S(2)}, u32[]{:S(2)}) %collective-permute-start.4) | collective-permute-done | bytes 262176 | tf_op jit(solution)/shard_map/ppermute | solution.py:268
  17.7 2.1 %collective-permute-start.9 = (bf16[16,32,256]{2,1,0:T(8,128)(2,1)S(1)}, bf16[16,32,256]{2,1,0:T(8,128)(2,1)S(1)}, u32[]{:S(2)}, u32[]{:S(2)}) collective-permute-start(bf16[16,32,256]{2,1,0:T(8,128)(2,1)S(1)} %collective-permute-done.4.refs_4_.refs_1_), channel_id=1, source_target_pairs={{0,4},{4,8},{8,12},{12,14},{14,10},{10,6},{6,2},{2,0},{5,1},{9,5},... | collective-permute-start | bytes 786440 | tf_op jit(solution)/shard_map/ppermute | solution.py:268
  19.8 1.5 %collective-permute-start.6 = (bf16[160,256]{1,0:T(8,128)(2,1)S(1)}, bf16[160,256]{1,0:T(8,128)(2,1)S(1)}, u32[]{:S(2)}, u32[]{:S(2)}) collective-permute-start(bf16[160,256]{1,0:T(8,128)(2,1)S(1)} %early_row.1), channel_id=1, source_target_pairs={{0,16},{16,0},{1,17},{17,1},{2,18},{18,2},{3,19},{19,3},{4,20},{20... | collective-permute-start | bytes 245768 | tf_op jit(solution)/shard_map/ppermute | solution.py:273
  21.3 0.1 collective-permute-start.7
  21.4 0.0 collective-permute-done.8.refs_2_.refs_0_.refs_1_
  21.4 1.8 %collective-permute-start.12 = (bf16[16,32,256]{2,1,0:T(8,128)(2,1)S(1)}, bf16[16,32,256]{2,1,0:T(8,128)(2,1)S(1)}, u32[]{:S(2)}, u32[]{:S(2)}) collective-permute-start(bf16[16,32,256]{2,1,0:T(8,128)(2,1)S(1)} %collective-permute-done.8.refs_2_.refs_0_.refs_1_), channel_id=1, source_target_pairs={{0,4},{4,8},{8,12},{12,14},{14,10},{10,6},{6,2},{2,0},{5,1},{9,5},... | collective-permute-start | bytes 786440 | tf_op jit(solution)/shard_map/ppermute | solution.py:268
  23.1 1.1 %collective-permute-done.6.refs_2_.early_ref = bf16[160,256]{1,0:T(8,128)(2,1)S(1)} collective-permute-done((bf16[160,256]{1,0:T(8,128)(2,1)S(1)}, bf16[160,256]{1,0:T(8,128)(2,1)S(1)}, u32[]{:S(2)}, u32[]{:S(2)}) %collective-permute-start.6) | collective-permute-done | bytes 81952 | tf_op jit(solution)/shard_map/ppermute | solution.py:273
  24.2 0.0 collective-permute-done.9.refs_3_.refs_1_.refs_2_
  24.2 0.1 collective-permute-start.11
  24.3 0.0 collective-permute-done.5.refs_5_.refs_0_
  24.3 0.0 copy-done
  24.3 1.3 %early_fit.1 = (bf16[512,512]{1,0:T(8,128)(2,1)S(1)}, f32[512,4096]{1,0:T(8,128)S(1)}) custom-call(bf16[512,512]{1,0:T(8,128)(2,1)S(1)} %copy-done, bf16[16,32,256]{2,1,0:T(8,128)(2,1)S(1)} %collective-permute-done.refs_2_.refs_0_, bf16[16,32,256]{2,1,0:T(8,128)(2,1)S(1)} %collective-permute-done.1.refs_0_.refs_1_, ...), custom_call_target="tpu_custom_call" | custom-call | tf_op jit(solution)/shard_map/early_fit/pallas_call | solution.py:240
  25.7 2.1 %collective-permute-done.12.refs_0_.refs_1_.refs_4_ = bf16[16,32,256]{2,1,0:T(8,128)(2,1)S(1)} collective-permute-done((bf16[16,32,256]{2,1,0:T(8,128)(2,1)S(1)}, bf16[16,32,256]{2,1,0:T(8,128)(2,1)S(1)}, u32[]{:S(2)}, u32[]{:S(2)}) %collective-permute-start.12) | collective-permute-done | bytes 262176 | tf_op jit(solution)/shard_map/ppermute | solution.py:268
  27.8 0.0 copy-start.1
  27.8 0.0 copy-start.2
  27.8 0.1 collective-permute-start.13
  27.9 0.0 collective-permute-done.7.refs_1_.refs_0_
  27.9 1.7 %collective-permute-start.10 = (bf16[224,256]{1,0:T(8,128)(2,1)S(1)}, bf16[224,256]{1,0:T(8,128)(2,1)S(1)}, u32[]{:S(2)}, u32[]{:S(2)}) collective-permute-start(bf16[224,256]{1,0:T(8,128)(2,1)S(1)} %late_row.2), channel_id=1, source_target_pairs={{0,16},{16,0},{1,17},{17,1},{2,18},{18,2},{3,19},{19,3},{4,20},{20... | collective-permute-start | bytes 344072 | tf_op jit(solution)/shard_map/ppermute | solution.py:291
  29.6 0.0 collective-permute-done.11.refs_0_.refs_3_
  29.6 0.0 collective-permute-done.13.refs_2_.refs_5_
  29.6 1.4 %collective-permute-start.14 = (bf16[128,256]{1,0:T(8,128)(2,1)S(1)}, bf16[128,256]{1,0:T(8,128)(2,1)S(1)}, u32[]{:S(2)}, u32[]{:S(2)}) collective-permute-start(bf16[128,256]{1,0:T(8,128)(2,1)S(1)} %late_row.3), channel_id=1, source_target_pairs={{0,16},{16,0},{1,17},{17,1},{2,18},{18,2},{3,19},{19,3},{4,20},{20... | collective-permute-start | bytes 196616 | tf_op jit(solution)/shard_map/ppermute | solution.py:291
  31.0 0.0 copy-done.1
  31.0 0.0 copy-done.2
  31.0 3.8 %fit_same.1 = (bf16[512,4096]{1,0:T(8,128)(2,1)S(1)}, bf16[256,4096]{1,0:T(8,128)(2,1)S(1)}, f32[256,256]{1,0:T(8,128)S(1)}) custom-call(f32[2,16]{1,0:T(2,128)S(1)} %copy-done.2, f32[2,256]{1,0:T(2,128)S(1)} %copy-done.1, bf16[512,512]{1,0:T(8,128)(2,1)S(1)} %get-tuple-element.18.factor_ref, f32[512,4096]{1,0:T(8,128)S(1)} %get-tuple-element.19.refs_1_.early_ref, ...), custom_call_target="tpu_custom_call" | custom-call | tf_op jit(solution)/shard_map/fit_same/pallas_call | solution.py:240
  34.9 0.0 collective-permute-done.10.late_ref
  34.9 0.1 collective-permute-done.14.last_ref
  34.9 2.6 %opposite.1 = (bf16[256,4096]{1,0:T(8,128)(2,1)S(1)}, f32[8,16,256]{2,1,0:T(8,128)S(1)}, f32[8,16,256]{2,1,0:T(8,128)S(1)}) custom-call(f32[2,16]{1,0:T(2,128)S(1)} %copy-done.2, f32[2,256]{1,0:T(2,128)S(1)} %copy-done.1, bf16[512,512]{1,0:T(8,128)(2,1)S(1)} %get-tuple-element.18.factor_ref, bf16[160,256]{1,0:T(8,128)(2,1)S(1)} %collective-permute-done.6.refs_2_.early_ref, ...), custom_call_target="tpu_custom_call" | custom-call | flops 1610612736 | bytes 5245056 | tf_op jit(solution)/shard_map/opposite/pallas_call | solution.py:240
  37.5 0.1 collective-permute-start.15
  37.6 1.3 %collective-permute-done.15.arrived = f32[8,16,256]{2,1,0:T(8,128)S(1)} collective-permute-done((f32[8,16,256]{2,1,0:T(8,128)S(1)}, f32[8,16,256]{2,1,0:T(8,128)S(1)}, u32[]{:S(2)}, u32[]{:S(2)}) %collective-permute-start.15) | collective-permute-done | bytes 131104 | tf_op jit(solution)/shard_map/ppermute | solution.py:314
  39.0 1.7 %collective-permute-start.16 = (f32[4,16,256]{2,1,0:T(8,128)S(1)}, f32[4,16,256]{2,1,0:T(8,128)S(1)}, u32[]{:S(2)}, u32[]{:S(2)}) collective-permute-start(f32[4,16,256]{2,1,0:T(8,128)S(1)} %get-tuple-element.25), channel_id=1, source_target_pairs={{0,2},{1,3},{2,0},{3,1},{4,6},{5,7},{6,4},{7,5},{8,10},{9,11},{10,... | collective-permute-start | bytes 196616 | tf_op jit(solution)/shard_map/ppermute | solution.py:314
  40.7 1.3 %gamma_other.1 = bf16[256,512]{1,0:T(8,128)(2,1)S(1)} custom-call(bf16[256,4096]{1,0:T(8,128)(2,1)S(1)} %get-tuple-element.31.amp_ref, bf16[512,4096]{1,0:T(8,128)(2,1)S(1)} %get-tuple-element.20.fitted_ref), custom_call_target="tpu_custom_call" | custom-call | flops 1073741824 | bytes 6291456 | tf_op jit(solution)/shard_map/gamma_other/pallas_call | solution.py:240
  41.9 1.6 %collective-permute-start.19 = (bf16[256,512]{1,0:T(8,128)(2,1)S(1)}, bf16[256,512]{1,0:T(8,128)(2,1)S(1)}, u32[]{:S(2)}, u32[]{:S(2)}) collective-permute-start(bf16[256,512]{1,0:T(8,128)(2,1)S(1)} %gamma_other.1), channel_id=1, source_target_pairs={{0,16},{16,0},{1,17},{17,1},{2,18},{18,2},{3,19},{19,3},{4,20},{20... | collective-permute-start | bytes 786440 | tf_op jit(solution)/shard_map/ppermute | solution.py:312
  43.5 0.0 collective-permute-done.16.arrived
  43.5 1.6 %collective-permute-start.17 = (f32[2,16,256]{2,1,0:T(8,128)S(1)}, f32[2,16,256]{2,1,0:T(8,128)S(1)}, u32[]{:S(2)}, u32[]{:S(2)}) collective-permute-start(f32[2,16,256]{2,1,0:T(8,128)S(1)} %get-tuple-element.27), channel_id=1, source_target_pairs={{0,4},{1,5},{2,6},{3,7},{4,0},{5,1},{6,2},{7,3},{8,12},{9,13},{10,... | collective-permute-start | bytes 98312 | tf_op jit(solution)/shard_map/ppermute | solution.py:314
  45.2 2.3 %collective-permute-done.17.arrived = f32[2,16,256]{2,1,0:T(8,128)S(1)} collective-permute-done((f32[2,16,256]{2,1,0:T(8,128)S(1)}, f32[2,16,256]{2,1,0:T(8,128)S(1)}, u32[]{:S(2)}, u32[]{:S(2)}) %collective-permute-start.17) | collective-permute-done | bytes 32800 | tf_op jit(solution)/shard_map/ppermute | solution.py:314
  47.5 2.7 %collective-permute-start.18 = (f32[1,16,256]{2,1,0:T(8,128)S(1)}, f32[1,16,256]{2,1,0:T(8,128)S(1)}, u32[]{:S(2)}, u32[]{:S(2)}) collective-permute-start(f32[1,16,256]{2,1,0:T(8,128)S(1)} %get-tuple-element.29), channel_id=1, source_target_pairs={{0,8},{1,9},{2,10},{3,11},{4,12},{5,13},{6,14},{7,15},{8,0},{9,1},... | collective-permute-start | bytes 49160 | tf_op jit(solution)/shard_map/ppermute | solution.py:321
  50.2 1.3 %gamma_same.1.gamma_in = f32[256,512]{1,0:T(8,128)S(1)} custom-call(bf16[256,4096]{1,0:T(8,128)(2,1)S(1)} %get-tuple-element.30.amp_ref, bf16[512,4096]{1,0:T(8,128)(2,1)S(1)} %get-tuple-element.20.fitted_ref), custom_call_target="tpu_custom_call" | custom-call | flops 2147483648 | bytes 6291456 | tf_op jit(solution)/shard_map/gamma_same/pallas_call | solution.py:240
  51.5 0.8 %collective-permute-done.18.arrived = f32[1,16,256]{2,1,0:T(8,128)S(1)} collective-permute-done((f32[1,16,256]{2,1,0:T(8,128)S(1)}, f32[1,16,256]{2,1,0:T(8,128)S(1)}, u32[]{:S(2)}, u32[]{:S(2)}) %collective-permute-start.18) | collective-permute-done | bytes 16416 | tf_op jit(solution)/shard_map/ppermute | solution.py:321
  52.2 0.0 collective-permute-done.19.refs_0_
  52.2 0.8 %finish.1 = (f32[256,512]{1,0:T(8,128)}, f32[1,16,256]{2,1,0:T(8,128)}) custom-call(f32[1,16,256]{2,1,0:T(8,128)S(1)} %get-tuple-element.28.kept_in, f32[1,16,256]{2,1,0:T(8,128)S(1)} %collective-permute-done.18.arrived, f32[256,512]{1,0:T(8,128)S(1)} %gamma_same.1.gamma_in, bf16[256,512]{1,0:T(8,128)(2,1)S(1)} %collective-permute-done.19.refs_0_), custom_call_target="tpu_custom_call" | custom-call | tf_op jit(solution)/shard_map/finish/pallas_call | solution.py:240
  (9 shorter events, 0.2 us)
Async XLA Ops:
  0.6 23.7 %copy-start = (bf16[512,512]{1,0:T(8,128)(2,1)S(1)}, bf16[512,512]{1,0:T(8,128)(2,1)}, u32[]{:S(2)}) copy-start(bf16[512,512]{1,0:T(8,128)(2,1)} %given_ref.1) | copy-start | bytes 1572868
  0.6 3.2 %collective-permute-start = (bf16[16,32,256]{2,1,0:T(8,128)(2,1)}, bf16[16,32,256]{2,1,0:T(8,128)(2,1)S(1)}, u32[]{:S(2)}, u32[]{:S(2)}) collective-permute-start(bf16[16,32,256]{2,1,0:T(8,128)(2,1)} %bitcast.5), channel_id=1, source_target_pairs={{0,1},{1,0},{2,3},{3,2},{4,5},{5,4},{6,7},{7,6},{8,9},{9,8},{10,11... | collective-permute-start | bytes 786440 | tf_op jit(solution)/shard_map/ppermute | solution.py:264
  1.2 7.1 %collective-permute-start.1 = (bf16[16,32,256]{2,1,0:T(8,128)(2,1)}, bf16[16,32,256]{2,1,0:T(8,128)(2,1)S(1)}, u32[]{:S(2)}, u32[]{:S(2)}) collective-permute-start(bf16[16,32,256]{2,1,0:T(8,128)(2,1)} %bitcast.6), channel_id=1, source_target_pairs={{0,4},{4,8},{8,12},{12,14},{14,10},{10,6},{6,2},{2,0},{5,1},{9,5},... | collective-permute-start | bytes 786440 | tf_op jit(solution)/shard_map/ppermute | solution.py:268
  3.8 7.3 %collective-permute-start.2 = (bf16[16,32,256]{2,1,0:T(8,128)(2,1)S(1)}, bf16[16,32,256]{2,1,0:T(8,128)(2,1)S(1)}, u32[]{:S(2)}, u32[]{:S(2)}) collective-permute-start(bf16[16,32,256]{2,1,0:T(8,128)(2,1)S(1)} %collective-permute-done.refs_2_.refs_0_), channel_id=1, source_target_pairs={{0,4},{4,8},{8,12},{12,14},{14,10},{10,6},{6,2},{2,0},{5,1},{9,5},... | collective-permute-start | bytes 786440 | tf_op jit(solution)/shard_map/ppermute | solution.py:268
  8.3 6.4 %collective-permute-start.3 = (bf16[16,32,256]{2,1,0:T(8,128)(2,1)S(1)}, bf16[16,32,256]{2,1,0:T(8,128)(2,1)S(1)}, u32[]{:S(2)}, u32[]{:S(2)}) collective-permute-start(bf16[16,32,256]{2,1,0:T(8,128)(2,1)S(1)} %collective-permute-done.1.refs_0_.refs_1_), channel_id=1, source_target_pairs={{0,4},{4,8},{8,12},{12,14},{14,10},{10,6},{6,2},{2,0},{5,1},{9,5},... | collective-permute-start | bytes 786440 | tf_op jit(solution)/shard_map/ppermute | solution.py:268
  11.2 13.2 %collective-permute-start.5 = (bf16[3,16,32,256]{3,2,1,0:T(8,128)(2,1)S(1)}, bf16[3,16,32,256]{3,2,1,0:T(8,128)(2,1)S(1)}, u32[]{:S(2)}, u32[]{:S(2)}) collective-permute-start(bf16[3,16,32,256]{3,2,1,0:T(8,128)(2,1)S(1)} %stack.4), channel_id=1, source_target_pairs={{0,1},{1,0},{2,3},{3,2},{4,5},{5,4},{6,7},{7,6},{8,9},{9,8},{10,11... | collective-permute-start | bytes 2359304 | tf_op jit(solution)/shard_map/ppermute | solution.py:284
  11.2 6.4 %collective-permute-start.4 = (bf16[16,32,256]{2,1,0:T(8,128)(2,1)S(1)}, bf16[16,32,256]{2,1,0:T(8,128)(2,1)S(1)}, u32[]{:S(2)}, u32[]{:S(2)}) collective-permute-start(bf16[16,32,256]{2,1,0:T(8,128)(2,1)S(1)} %collective-permute-done.2.refs_1_.refs_2_), channel_id=1, source_target_pairs={{0,4},{4,8},{8,12},{12,14},{14,10},{10,6},{6,2},{2,0},{5,1},{9,5},... | collective-permute-start | bytes 786440 | tf_op jit(solution)/shard_map/ppermute | solution.py:268
  14.7 6.7 %collective-permute-start.8 = (bf16[16,32,256]{2,1,0:T(8,128)(2,1)S(1)}, bf16[16,32,256]{2,1,0:T(8,128)(2,1)S(1)}, u32[]{:S(2)}, u32[]{:S(2)}) collective-permute-start(bf16[16,32,256]{2,1,0:T(8,128)(2,1)S(1)} %collective-permute-done.3.refs_3_.refs_0_), channel_id=1, source_target_pairs={{0,4},{4,8},{8,12},{12,14},{14,10},{10,6},{6,2},{2,0},{5,1},{9,5},... | collective-permute-start | bytes 786440 | tf_op jit(solution)/shard_map/ppermute | solution.py:268
  17.7 6.5 %collective-permute-start.9 = (bf16[16,32,256]{2,1,0:T(8,128)(2,1)S(1)}, bf16[16,32,256]{2,1,0:T(8,128)(2,1)S(1)}, u32[]{:S(2)}, u32[]{:S(2)}) collective-permute-start(bf16[16,32,256]{2,1,0:T(8,128)(2,1)S(1)} %collective-permute-done.4.refs_4_.refs_1_), channel_id=1, source_target_pairs={{0,4},{4,8},{8,12},{12,14},{14,10},{10,6},{6,2},{2,0},{5,1},{9,5},... | collective-permute-start | bytes 786440 | tf_op jit(solution)/shard_map/ppermute | solution.py:268
  19.8 4.4 %collective-permute-start.6 = (bf16[160,256]{1,0:T(8,128)(2,1)S(1)}, bf16[160,256]{1,0:T(8,128)(2,1)S(1)}, u32[]{:S(2)}, u32[]{:S(2)}) collective-permute-start(bf16[160,256]{1,0:T(8,128)(2,1)S(1)} %early_row.1), channel_id=1, source_target_pairs={{0,16},{16,0},{1,17},{17,1},{2,18},{18,2},{3,19},{19,3},{4,20},{20... | collective-permute-start | bytes 245768 | tf_op jit(solution)/shard_map/ppermute | solution.py:273
  21.3 6.6 %collective-permute-start.7 = (bf16[2,16,32,256]{3,2,1,0:T(8,128)(2,1)S(1)}, bf16[2,16,32,256]{3,2,1,0:T(8,128)(2,1)S(1)}, u32[]{:S(2)}, u32[]{:S(2)}) collective-permute-start(bf16[2,16,32,256]{3,2,1,0:T(8,128)(2,1)S(1)} %stack.5), channel_id=1, source_target_pairs={{0,1},{1,0},{2,3},{3,2},{4,5},{5,4},{6,7},{7,6},{8,9},{9,8},{10,11... | collective-permute-start | bytes 1572872 | tf_op jit(solution)/shard_map/ppermute | solution.py:284
  21.4 6.4 %collective-permute-start.12 = (bf16[16,32,256]{2,1,0:T(8,128)(2,1)S(1)}, bf16[16,32,256]{2,1,0:T(8,128)(2,1)S(1)}, u32[]{:S(2)}, u32[]{:S(2)}) collective-permute-start(bf16[16,32,256]{2,1,0:T(8,128)(2,1)S(1)} %collective-permute-done.8.refs_2_.refs_0_.refs_1_), channel_id=1, source_target_pairs={{0,4},{4,8},{8,12},{12,14},{14,10},{10,6},{6,2},{2,0},{5,1},{9,5},... | collective-permute-start | bytes 786440 | tf_op jit(solution)/shard_map/ppermute | solution.py:268
  24.2 5.4 %collective-permute-start.11 = (bf16[2,16,32,256]{3,2,1,0:T(8,128)(2,1)S(1)}, bf16[2,16,32,256]{3,2,1,0:T(8,128)(2,1)S(1)}, u32[]{:S(2)}, u32[]{:S(2)}) collective-permute-start(bf16[2,16,32,256]{3,2,1,0:T(8,128)(2,1)S(1)} %stack.6), channel_id=1, source_target_pairs={{0,1},{1,0},{2,3},{3,2},{4,5},{5,4},{6,7},{7,6},{8,9},{9,8},{10,11... | collective-permute-start | bytes 1572872 | tf_op jit(solution)/shard_map/ppermute | solution.py:284
  27.8 3.2 %copy-start.1 = (f32[2,256]{1,0:T(2,128)S(1)}, f32[2,256]{1,0:T(2,128)}, u32[]{:S(2)}) copy-start(f32[2,256]{1,0:T(2,128)} %virt_ref.3) | copy-start | bytes 6148
  27.8 3.2 %copy-start.2 = (f32[2,16]{1,0:T(2,128)S(1)}, f32[2,16]{1,0:T(2,128)}, u32[]{:S(2)}) copy-start(f32[2,16]{1,0:T(2,128)} %occ_ref.3) | copy-start | bytes 388
  27.8 1.8 %collective-permute-start.13 = (bf16[1,16,32,256]{3,2,1,0:T(8,128)(2,1)S(1)}, bf16[1,16,32,256]{3,2,1,0:T(8,128)(2,1)S(1)}, u32[]{:S(2)}, u32[]{:S(2)}) collective-permute-start(bf16[1,16,32,256]{3,2,1,0:T(8,128)(2,1)S(1)} %stack.7), channel_id=1, source_target_pairs={{0,1},{1,0},{2,3},{3,2},{4,5},{5,4},{6,7},{7,6},{8,9},{9,8},{10,11... | collective-permute-start | bytes 786440 | tf_op jit(solution)/shard_map/ppermute | solution.py:284
  27.9 6.9 %collective-permute-start.10 = (bf16[224,256]{1,0:T(8,128)(2,1)S(1)}, bf16[224,256]{1,0:T(8,128)(2,1)S(1)}, u32[]{:S(2)}, u32[]{:S(2)}) collective-permute-start(bf16[224,256]{1,0:T(8,128)(2,1)S(1)} %late_row.2), channel_id=1, source_target_pairs={{0,16},{16,0},{1,17},{17,1},{2,18},{18,2},{3,19},{19,3},{4,20},{20... | collective-permute-start | bytes 344072 | tf_op jit(solution)/shard_map/ppermute | solution.py:291
  29.6 5.3 %collective-permute-start.14 = (bf16[128,256]{1,0:T(8,128)(2,1)S(1)}, bf16[128,256]{1,0:T(8,128)(2,1)S(1)}, u32[]{:S(2)}, u32[]{:S(2)}) collective-permute-start(bf16[128,256]{1,0:T(8,128)(2,1)S(1)} %late_row.3), channel_id=1, source_target_pairs={{0,16},{16,0},{1,17},{17,1},{2,18},{18,2},{3,19},{19,3},{4,20},{20... | collective-permute-start | bytes 196616 | tf_op jit(solution)/shard_map/ppermute | solution.py:291
  37.5 1.4 %collective-permute-start.15 = (f32[8,16,256]{2,1,0:T(8,128)S(1)}, f32[8,16,256]{2,1,0:T(8,128)S(1)}, u32[]{:S(2)}, u32[]{:S(2)}) collective-permute-start(f32[8,16,256]{2,1,0:T(8,128)S(1)} %get-tuple-element.23), channel_id=1, source_target_pairs={{0,1},{1,0},{2,3},{3,2},{4,5},{5,4},{6,7},{7,6},{8,9},{9,8},{10,11... | collective-permute-start | bytes 393224 | tf_op jit(solution)/shard_map/ppermute | solution.py:314
  39.0 4.5 %collective-permute-start.16 = (f32[4,16,256]{2,1,0:T(8,128)S(1)}, f32[4,16,256]{2,1,0:T(8,128)S(1)}, u32[]{:S(2)}, u32[]{:S(2)}) collective-permute-start(f32[4,16,256]{2,1,0:T(8,128)S(1)} %get-tuple-element.25), channel_id=1, source_target_pairs={{0,2},{1,3},{2,0},{3,1},{4,6},{5,7},{6,4},{7,5},{8,10},{9,11},{10,... | collective-permute-start | bytes 196616 | tf_op jit(solution)/shard_map/ppermute | solution.py:314
  41.9 10.3 %collective-permute-start.19 = (bf16[256,512]{1,0:T(8,128)(2,1)S(1)}, bf16[256,512]{1,0:T(8,128)(2,1)S(1)}, u32[]{:S(2)}, u32[]{:S(2)}) collective-permute-start(bf16[256,512]{1,0:T(8,128)(2,1)S(1)} %gamma_other.1), channel_id=1, source_target_pairs={{0,16},{16,0},{1,17},{17,1},{2,18},{18,2},{3,19},{19,3},{4,20},{20... | collective-permute-start | bytes 786440 | tf_op jit(solution)/shard_map/ppermute | solution.py:312
  43.5 4.0 %collective-permute-start.17 = (f32[2,16,256]{2,1,0:T(8,128)S(1)}, f32[2,16,256]{2,1,0:T(8,128)S(1)}, u32[]{:S(2)}, u32[]{:S(2)}) collective-permute-start(f32[2,16,256]{2,1,0:T(8,128)S(1)} %get-tuple-element.27), channel_id=1, source_target_pairs={{0,4},{1,5},{2,6},{3,7},{4,0},{5,1},{6,2},{7,3},{8,12},{9,13},{10,... | collective-permute-start | bytes 98312 | tf_op jit(solution)/shard_map/ppermute | solution.py:314
  47.5 4.7 %collective-permute-start.18 = (f32[1,16,256]{2,1,0:T(8,128)S(1)}, f32[1,16,256]{2,1,0:T(8,128)S(1)}, u32[]{:S(2)}, u32[]{:S(2)}) collective-permute-start(f32[1,16,256]{2,1,0:T(8,128)S(1)} %get-tuple-element.29), channel_id=1, source_target_pairs={{0,8},{1,9},{2,10},{3,11},{4,12},{5,13},{6,14},{7,15},{8,0},{9,1},... | collective-permute-start | bytes 49160 | tf_op jit(solution)/shard_map/ppermute | solution.py:321

commit v5 on v4

--- a/solution.py
+++ b/solution.py
@@ -155,7 +155,7 @@
     energies = pair_energies(occ_ref, spin, spin, own)
     raw = jnp.concatenate(list(pieces(slices, own)), axis=0)
     early = early_ref[:, pl.ds(pl.multiple_of(own * nv, nv), nv)]
-    left[...] = (early + dot(factor_ref[:, first:], raw, NN)).T.astype(left.dtype)
+    left[...] = (early + dot(factor_ref[:, first:], raw, NN)).astype(left.dtype).T
     total = None
     for start in range(0, count, GROUP):
         members = range(start, start + GROUP)
@@ -185,7 +185,7 @@
     sums[...] = energy_sums(virt_ref, 1 - spin, spin)
     energies = pair_energies(occ_ref, 1 - spin, spin, own)
     raw = jnp.concatenate([early_ref[...], late_ref[...], last_ref[...]], axis=0)
-    left[...] = dot(factor_ref[...], raw, NN).T.astype(left.dtype)
+    left[...] = dot(factor_ref[...], raw, NN).astype(left.dtype).T
     total = dens_in[...]
     for start in range(0, count, GROUP):
         columns = slice(start * nv, (start + GROUP) * nv)
@@ -198,12 +198,13 @@
         stacked = jnp.concatenate(amps, axis=0)
         total = total + dot(stacked, stacked, TN)
     dens[...] = total / count
-    core = own % 2
-    chips, rows, _ = kept_ref.shape
-    for chip in range(chips):
-        for ref, lane in ((kept_ref, core), (sent_ref, 1 - core)):
-            first = pl.multiple_of((2 * chip + lane) * rows, rows)
-            ref[chip] = dens[pl.ds(first, rows)]
+    chip, core = own // 2, own % 2
+    near, far, rows, _ = kept_ref.shape
+    for ref, lane in ((kept_ref, core), (sent_ref, 1 - core)):
+        for m in range(near):
+            for n in range(far):
+                there = ((chip ^ (near * lane + m)) & (2 * near - 1)) + 2 * near * n
+                ref[m, n] = dens[pl.ds(pl.multiple_of(there * rows, rows), rows)]
 
 
 def gamma_kernel(amp_ref, fitted_ref, *out_refs):
@@ -213,13 +214,28 @@
         ref[...] = gamma[n * rows : (n + 1) * rows].astype(ref.dtype)
 
 
-def split_kernel(bit, kept_in, arrived, *refs):
+def near_kernel(kept_in, arrived, *refs):
+    one_ref, two_ref, total = refs[-3:]
+    total[...] = kept_in[...] + arrived[...]
+    core = lax.axis_index("orb") % 2
+    one_ref[...] = total[1 - core]
+    two_ref[...] = total[core]
+
+
+def far_split_kernel(one_in, two_in, *refs):
+    kept_ref, sent_ref, total = refs[-3:]
+    total[...] = one_in[...] + two_in[...]
+    mine = lax.axis_index("orb") // 8
+    kept_ref[...] = total[mine]
+    sent_ref[...] = total[1 - mine]
+
+
+def core_split_kernel(kept_in, arrived, *refs):
     kept_ref, sent_ref, total = refs[-3:]
     total[...] = kept_in[...] + arrived[...]
-    mine = (lax.axis_index("orb") >> bit) & 1
-    for n in range(kept_ref.shape[0]):
-        kept_ref[n] = total[2 * n + mine]
-        sent_ref[n] = total[2 * n + 1 - mine]
+    core, rows = lax.axis_index("orb") % 2, kept_ref.shape[0]
+    kept_ref[...] = total[pl.ds(pl.multiple_of(core * rows, rows), rows)]
+    sent_ref[...] = total[pl.ds(pl.multiple_of((1 - core) * rows, rows), rows)]
 
 
 def finish_kernel(kept_in, arrived, gamma_in, *refs):
@@ -228,7 +244,7 @@
     for n, ref in enumerate(returned):
         part = slice(n * rows, (n + 1) * rows)
         gamma_ref[part] = gamma_in[part] + ref[...].astype(jnp.float32)
-    density_ref[...] = kept_in[...] + arrived[...]
+    density_ref[0] = kept_in[...] + arrived[...]
 
 
 def vmem_call(kernel, name, operands, outs, scratch=(), flops=0, in_hbm=0, pin=True):
@@ -294,11 +310,12 @@
         [((naux, count * nv), half), ((nv, count * nv), half), ((nv, nv), full)],
         [((nv, naux), half), ((nv, nv), full)],
     )
-    rows = nv // orb_count
+    rows = 2 * nv // orb_count
+    share = (2, 2, rows, nv)
     amp_other, kept, sent = vmem_call(
         opposite_all_kernel, "opposite",
         [occ_energy, virt_energy, factor] + rows_sent + [fitted, dens_same],
-        [((nv, count * nv), half)] + [((orb_count // 2, rows, nv), full)] * 2,
+        [((nv, count * nv), half)] + [(share, full)] * 2,
         [((nv, naux), half), ((nv, nv), full), ((nv, nv), full)],
         flops=pair * (naux + nv),
     )
@@ -310,18 +327,24 @@
         gamma_kernel, "gamma_same", [amp_same, fitted], [((nv, naux), full)], flops=2*pair*naux
     )
     returned = [lax.ppermute(piece, "spin", across) for piece in gamma_other]
-    for bit in range(1, orb_count.bit_length() - 1):
-        arrived = lax.ppermute(sent, "orb", [(d, d ^ (1 << bit - 1)) for d in range(orb_count)])
-        left = orb_count >> bit + 1
-        order = returned[:0] if left == 1 else []
-        kept, sent = vmem_call(
-            functools.partial(split_kernel, bit), "split", [kept, arrived] + order,
-            [((left, rows, nv), full)] * 2, [((2 * left, rows, nv), full)],
-        )
-    arrived = lax.ppermute(sent, "orb", [(d, d ^ (orb_count >> 1)) for d in range(orb_count)])
+    arrived = lax.ppermute(sent, "orb", swap)
+    one, two = vmem_call(near_kernel, "near", [kept, arrived], [(share[1:], full)] * 2, [(share, full)])
+    chip_moves = lambda first, second: [
+        (d, 2 * (d // 2 ^ (second if d % 2 else first)) + d % 2) for d in range(orb_count)
+    ]
+    one = lax.ppermute(one, "orb", chip_moves(1, 2))
+    two = lax.ppermute(two, "orb", chip_moves(0, 3))
+    kept, sent = vmem_call(
+        far_split_kernel, "far_split", [one, two], [(share[2:], full)] * 2, [(share[1:], full)]
+    )
+    arrived = lax.ppermute(sent, "orb", chip_moves(4, 4))
+    kept, sent = vmem_call(
+        core_split_kernel, "core_split", [kept, arrived, gamma_same], [((rows // 2, nv), full)] * 2, [(share[2:], full)]
+    )
+    arrived = lax.ppermute(sent, "orb", swap)
     gamma, density = vmem_call(
         finish_kernel, "finish", [kept, arrived, gamma_same] + returned,
-        [((nv, naux), full), ((1, rows, nv), full)], pin=False,
+        [((nv, naux), full), ((1, rows // 2, nv), full)], pin=False,
     )
     return gamma[None, None], density
 
@@ -504,7 +527,7 @@
 
 def local(integrals, metric_factor, occ_energy, virt_energy, orb_count):
     _, count, nv, width = integrals.shape
-    fits = count * nv * metric_factor.shape[0] * 2 <= 4 * 1024 * 1024 and width % 16 == 0 and count % GROUP == 0
+    fits = orb_count == 16 and count * nv * metric_factor.shape[0] * 2 <= 4 * 1024 * 1024 and width % 16 == 0 and count % GROUP == 0
     chosen = local_in_vmem if fits else local_streamed
     return chosen(integrals, metric_factor, occ_energy, virt_energy, orb_count)
 

time: 53.2 us -> 52.2 us (0.981)
  waiting for transfers between devices: 13.5 us -> 12.2 us
    ppermute x4 -> x5, waiting for transfers between devices: 4.44 us -> 3.13 us  [the longest x2 2.17 us: local_in_vmem(): arrived = lax.ppermute(sent, 'orb', swap)]
    ppermute x4 -> x5, starting transfers between devices: 6.07 us -> 6.33 us  [the longest x1 2.65 us: local_in_vmem(): arrived = lax.ppermute(sent, 'orb', chip_moves(4, 4))]
  transfers between devices with their start and end apart: 20 -> 21, of which waited for: 10 -> 10; matrix products, arithmetic and copies ran while one was open for 0% -> 0% of each run, Pallas kernels for 15% -> 15%
where the time goes in v5:
time: 52.2 us; the launch traced here: 52 us
  starting transfers between devices  27.7 us (53%)
  waiting for transfers between devices  12.2 us (23%)
  Pallas kernels  11.2 us (21%)
  between operations  0.81 us (2%)
    ppermute x7, starting transfers between devices, local_in_vmem(): lax.ppermute(lane, 'orb', moves)  14.4 us
    pallas_call x16, Pallas kernels, vmem_call(): pl.pallas_call(kernel, in_specs=[hbm] * in_hbm + [vmem] * (len(operands)...  11.2 us
    ppermute x7, waiting for transfers between devices, local_in_vmem(): lax.ppermute(lane, 'orb', moves)  7.9 us
    ppermute x2, starting transfers between devices, local_in_vmem(): rows_sent.append(lax.ppermute(row, 'spin', across))  3.09 us
    ppermute x1, starting transfers between devices, local_in_vmem(): arrived = lax.ppermute(sent, 'orb', chip_moves(4, 4))  2.65 us
    ppermute x2, waiting for transfers between devices, local_in_vmem(): arrived = lax.ppermute(sent, 'orb', swap)  2.17 us
    ppermute x1, starting transfers between devices, local_in_vmem(): one = lax.ppermute(one, 'orb', chip_moves(1, 2))  1.7 us
    ppermute x1, starting transfers between devices, local_in_vmem(): returned = [lax.ppermute(piece, 'spin', across) for piece in gamma_other]  1.56 us
  transfers between devices with their start and end apart: 21, of which 10 were waited for; matrix products, arithmetic and copies ran while one was open for 0% of the time, Pallas kernels for 15%

profile of v5, /device:TPU:0, one launch (start us, length us, event | category | flops | bytes accessed | tf_op | source)
XLA Modules:
  0.0 52.0 jit_solution(10026121515646093110)
XLA Ops:
  0.6 0.0 copy-start
  0.6 0.5 collective-permute-start
  1.2 2.6 %collective-permute-start.1 = (bf16[16,32,256]{2,1,0:T(8,128)(2,1)}, bf16[16,32,256]{2,1,0:T(8,128)(2,1)S(1)}, u32[]{:S(2)}, u32[]{:S(2)}) collective-permute-start(bf16[16,32,256]{2,1,0:T(8,128)(2,1)} %bitcast.6), channel_id=1, source_target_pairs={{0,4},{4,8},{8,12},{12,14},{14,10},{10,6},{6,2},{2,0},{5,1},{9,5},... | collective-permute-start | bytes 786440 | tf_op jit(solution)/shard_map/ppermute | solution.py:284
  3.8 0.0 collective-permute-done.refs_2_.refs_0_
  3.8 1.7 %collective-permute-start.2 = (bf16[16,32,256]{2,1,0:T(8,128)(2,1)S(1)}, bf16[16,32,256]{2,1,0:T(8,128)(2,1)S(1)}, u32[]{:S(2)}, u32[]{:S(2)}) collective-permute-start(bf16[16,32,256]{2,1,0:T(8,128)(2,1)S(1)} %collective-permute-done.refs_2_.refs_0_), channel_id=1, source_target_pairs={{0,4},{4,8},{8,12},{12,14},{14,10},{10,6},{6,2},{2,0},{5,1},{9,5},... | collective-permute-start | bytes 786440 | tf_op jit(solution)/shard_map/ppermute | solution.py:284
  5.5 2.8 %collective-permute-done.1.refs_0_.refs_1_ = bf16[16,32,256]{2,1,0:T(8,128)(2,1)S(1)} collective-permute-done((bf16[16,32,256]{2,1,0:T(8,128)(2,1)}, bf16[16,32,256]{2,1,0:T(8,128)(2,1)S(1)}, u32[]{:S(2)}, u32[]{:S(2)}) %collective-permute-start.1) | collective-permute-done | bytes 262176 | tf_op jit(solution)/shard_map/ppermute | solution.py:284
  8.3 2.1 %collective-permute-start.3 = (bf16[16,32,256]{2,1,0:T(8,128)(2,1)S(1)}, bf16[16,32,256]{2,1,0:T(8,128)(2,1)S(1)}, u32[]{:S(2)}, u32[]{:S(2)}) collective-permute-start(bf16[16,32,256]{2,1,0:T(8,128)(2,1)S(1)} %collective-permute-done.1.refs_0_.refs_1_), channel_id=1, source_target_pairs={{0,4},{4,8},{8,12},{12,14},{14,10},{10,6},{6,2},{2,0},{5,1},{9,5},... | collective-permute-start | bytes 786440 | tf_op jit(solution)/shard_map/ppermute | solution.py:284
  10.4 0.7 %collective-permute-done.2.refs_1_.refs_2_ = bf16[16,32,256]{2,1,0:T(8,128)(2,1)S(1)} collective-permute-done((bf16[16,32,256]{2,1,0:T(8,128)(2,1)S(1)}, bf16[16,32,256]{2,1,0:T(8,128)(2,1)S(1)}, u32[]{:S(2)}, u32[]{:S(2)}) %collective-permute-start.2) | collective-permute-done | bytes 262176 | tf_op jit(solution)/shard_map/ppermute | solution.py:284
  11.1 0.1 stack.4
  11.2 0.1 collective-permute-start.5
  11.2 2.1 %collective-permute-start.4 = (bf16[16,32,256]{2,1,0:T(8,128)(2,1)S(1)}, bf16[16,32,256]{2,1,0:T(8,128)(2,1)S(1)}, u32[]{:S(2)}, u32[]{:S(2)}) collective-permute-start(bf16[16,32,256]{2,1,0:T(8,128)(2,1)S(1)} %collective-permute-done.2.refs_1_.refs_2_), channel_id=1, source_target_pairs={{0,4},{4,8},{8,12},{12,14},{14,10},{10,6},{6,2},{2,0},{5,1},{9,5},... | collective-permute-start | bytes 786440 | tf_op jit(solution)/shard_map/ppermute | solution.py:284
  13.4 1.3 %collective-permute-done.3.refs_3_.refs_0_ = bf16[16,32,256]{2,1,0:T(8,128)(2,1)S(1)} collective-permute-done((bf16[16,32,256]{2,1,0:T(8,128)(2,1)S(1)}, bf16[16,32,256]{2,1,0:T(8,128)(2,1)S(1)}, u32[]{:S(2)}, u32[]{:S(2)}) %collective-permute-start.3) | collective-permute-done | bytes 262176 | tf_op jit(solution)/shard_map/ppermute | solution.py:284
  14.7 2.1 %collective-permute-start.8 = (bf16[16,32,256]{2,1,0:T(8,128)(2,1)S(1)}, bf16[16,32,256]{2,1,0:T(8,128)(2,1)S(1)}, u32[]{:S(2)}, u32[]{:S(2)}) collective-permute-start(bf16[16,32,256]{2,1,0:T(8,128)(2,1)S(1)} %collective-permute-done.3.refs_3_.refs_0_), channel_id=1, source_target_pairs={{0,4},{4,8},{8,12},{12,14},{14,10},{10,6},{6,2},{2,0},{5,1},{9,5},... | collective-permute-start | bytes 786440 | tf_op jit(solution)/shard_map/ppermute | solution.py:284
  16.7 0.9 %collective-permute-done.4.refs_4_.refs_1_ = bf16[16,32,256]{2,1,0:T(8,128)(2,1)S(1)} collective-permute-done((bf16[16,32,256]{2,1,0:T(8,128)(2,1)S(1)}, bf16[16,32,256]{2,1,0:T(8,128)(2,1)S(1)}, u32[]{:S(2)}, u32[]{:S(2)}) %collective-permute-start.4) | collective-permute-done | bytes 262176 | tf_op jit(solution)/shard_map/ppermute | solution.py:284
  17.7 2.1 %collective-permute-start.9 = (bf16[16,32,256]{2,1,0:T(8,128)(2,1)S(1)}, bf16[16,32,256]{2,1,0:T(8,128)(2,1)S(1)}, u32[]{:S(2)}, u32[]{:S(2)}) collective-permute-start(bf16[16,32,256]{2,1,0:T(8,128)(2,1)S(1)} %collective-permute-done.4.refs_4_.refs_1_), channel_id=1, source_target_pairs={{0,4},{4,8},{8,12},{12,14},{14,10},{10,6},{6,2},{2,0},{5,1},{9,5},... | collective-permute-start | bytes 786440 | tf_op jit(solution)/shard_map/ppermute | solution.py:284
  19.8 1.5 %collective-permute-start.6 = (bf16[160,256]{1,0:T(8,128)(2,1)S(1)}, bf16[160,256]{1,0:T(8,128)(2,1)S(1)}, u32[]{:S(2)}, u32[]{:S(2)}) collective-permute-start(bf16[160,256]{1,0:T(8,128)(2,1)S(1)} %early_row.1), channel_id=1, source_target_pairs={{0,16},{16,0},{1,17},{17,1},{2,18},{18,2},{3,19},{19,3},{4,20},{20... | collective-permute-start | bytes 245768 | tf_op jit(solution)/shard_map/ppermute | solution.py:289
  21.3 0.1 collective-permute-start.7
  21.4 0.0 collective-permute-done.8.refs_2_.refs_0_.refs_1_
  21.4 1.8 %collective-permute-start.12 = (bf16[16,32,256]{2,1,0:T(8,128)(2,1)S(1)}, bf16[16,32,256]{2,1,0:T(8,128)(2,1)S(1)}, u32[]{:S(2)}, u32[]{:S(2)}) collective-permute-start(bf16[16,32,256]{2,1,0:T(8,128)(2,1)S(1)} %collective-permute-done.8.refs_2_.refs_0_.refs_1_), channel_id=1, source_target_pairs={{0,4},{4,8},{8,12},{12,14},{14,10},{10,6},{6,2},{2,0},{5,1},{9,5},... | collective-permute-start | bytes 786440 | tf_op jit(solution)/shard_map/ppermute | solution.py:284
  23.1 1.1 %collective-permute-done.6.refs_2_.early_ref = bf16[160,256]{1,0:T(8,128)(2,1)S(1)} collective-permute-done((bf16[160,256]{1,0:T(8,128)(2,1)S(1)}, bf16[160,256]{1,0:T(8,128)(2,1)S(1)}, u32[]{:S(2)}, u32[]{:S(2)}) %collective-permute-start.6) | collective-permute-done | bytes 81952 | tf_op jit(solution)/shard_map/ppermute | solution.py:289
  24.2 0.0 collective-permute-done.9.refs_3_.refs_1_.refs_2_
  24.2 0.1 collective-permute-start.11
  24.3 0.0 collective-permute-done.5.refs_5_.refs_0_
  24.3 0.0 copy-done
  24.3 1.3 %early_fit.1 = (bf16[512,512]{1,0:T(8,128)(2,1)S(1)}, f32[512,4096]{1,0:T(8,128)S(1)}) custom-call(bf16[512,512]{1,0:T(8,128)(2,1)S(1)} %copy-done, bf16[16,32,256]{2,1,0:T(8,128)(2,1)S(1)} %collective-permute-done.refs_2_.refs_0_, bf16[16,32,256]{2,1,0:T(8,128)(2,1)S(1)} %collective-permute-done.1.refs_0_.refs_1_, ...), custom_call_target="tpu_custom_call" | custom-call | tf_op jit(solution)/shard_map/early_fit/pallas_call | solution.py:256
  25.7 2.1 %collective-permute-done.12.refs_0_.refs_1_.refs_4_ = bf16[16,32,256]{2,1,0:T(8,128)(2,1)S(1)} collective-permute-done((bf16[16,32,256]{2,1,0:T(8,128)(2,1)S(1)}, bf16[16,32,256]{2,1,0:T(8,128)(2,1)S(1)}, u32[]{:S(2)}, u32[]{:S(2)}) %collective-permute-start.12) | collective-permute-done | bytes 262176 | tf_op jit(solution)/shard_map/ppermute | solution.py:284
  27.8 0.0 copy-start.1
  27.8 0.0 copy-start.2
  27.8 0.1 collective-permute-start.13
  27.9 0.0 collective-permute-done.7.refs_1_.refs_0_
  27.9 1.7 %collective-permute-start.10 = (bf16[224,256]{1,0:T(8,128)(2,1)S(1)}, bf16[224,256]{1,0:T(8,128)(2,1)S(1)}, u32[]{:S(2)}, u32[]{:S(2)}) collective-permute-start(bf16[224,256]{1,0:T(8,128)(2,1)S(1)} %late_row.2), channel_id=1, source_target_pairs={{0,16},{16,0},{1,17},{17,1},{2,18},{18,2},{3,19},{19,3},{4,20},{20... | collective-permute-start | bytes 344072 | tf_op jit(solution)/shard_map/ppermute | solution.py:307
  29.6 0.0 collective-permute-done.11.refs_0_.refs_3_
  29.6 0.0 collective-permute-done.13.refs_2_.refs_5_
  29.6 1.4 %collective-permute-start.14 = (bf16[128,256]{1,0:T(8,128)(2,1)S(1)}, bf16[128,256]{1,0:T(8,128)(2,1)S(1)}, u32[]{:S(2)}, u32[]{:S(2)}) collective-permute-start(bf16[128,256]{1,0:T(8,128)(2,1)S(1)} %late_row.3), channel_id=1, source_target_pairs={{0,16},{16,0},{1,17},{17,1},{2,18},{18,2},{3,19},{19,3},{4,20},{20... | collective-permute-start | bytes 196616 | tf_op jit(solution)/shard_map/ppermute | solution.py:307
  31.0 0.0 copy-done.1
  31.0 0.0 copy-done.2
  31.0 3.8 %fit_same.1 = (bf16[512,4096]{1,0:T(8,128)(2,1)S(1)}, bf16[256,4096]{1,0:T(8,128)(2,1)S(1)}, f32[256,256]{1,0:T(8,128)S(1)}) custom-call(f32[2,16]{1,0:T(2,128)S(1)} %copy-done.2, f32[2,256]{1,0:T(2,128)S(1)} %copy-done.1, bf16[512,512]{1,0:T(8,128)(2,1)S(1)} %get-tuple-element.18.factor_ref, f32[512,4096]{1,0:T(8,128)S(1)} %get-tuple-element.19.refs_1_.early_ref, ...), custom_call_target="tpu_custom_call" | custom-call | tf_op jit(solution)/shard_map/fit_same/pallas_call | solution.py:256
  34.8 0.0 collective-permute-done.10.late_ref
  34.8 0.1 collective-permute-done.14.last_ref
  34.9 2.5 %opposite.1 = (bf16[256,4096]{1,0:T(8,128)(2,1)S(1)}, f32[2,2,32,256]{3,2,1,0:T(8,128)S(1)}, f32[2,2,32,256]{3,2,1,0:T(8,128)S(1)}) custom-call(f32[2,16]{1,0:T(2,128)S(1)} %copy-done.2, f32[2,256]{1,0:T(2,128)S(1)} %copy-done.1, bf16[512,512]{1,0:T(8,128)(2,1)S(1)} %get-tuple-element.18.factor_ref, ...), custom_call_target="tpu_custom_call" | custom-call | flops 1610612736 | bytes 5245056 | tf_op jit(solution)/shard_map/opposite/pallas_call | solution.py:256
  37.5 0.1 collective-permute-start.15
  37.5 1.3 %collective-permute-done.15.arrived = f32[2,2,32,256]{3,2,1,0:T(8,128)S(1)} collective-permute-done((f32[2,2,32,256]{3,2,1,0:T(8,128)S(1)}, f32[2,2,32,256]{3,2,1,0:T(8,128)S(1)}, u32[]{:S(2)}, u32[]{:S(2)}) %collective-permute-start.15) | collective-permute-done | bytes 131104 | tf_op jit(solution)/shard_map/ppermute | solution.py:330
  38.9 1.7 %collective-permute-start.16 = (f32[2,32,256]{2,1,0:T(8,128)S(1)}, f32[2,32,256]{2,1,0:T(8,128)S(1)}, u32[]{:S(2)}, u32[]{:S(2)}) collective-permute-start(f32[2,32,256]{2,1,0:T(8,128)S(1)} %get-tuple-element.24), channel_id=1, source_target_pairs={{0,2},{1,5},{2,0},{3,7},{4,6},{5,1},{6,4},{7,3},{8,10},{9,13},{10,... | collective-permute-start | bytes 196616 | tf_op jit(solution)/shard_map/ppermute | solution.py:335
  40.6 0.7 %collective-permute-start.17 = (f32[2,32,256]{2,1,0:T(8,128)S(1)}, f32[2,32,256]{2,1,0:T(8,128)S(1)}, u32[]{:S(2)}, u32[]{:S(2)}) collective-permute-start(f32[2,32,256]{2,1,0:T(8,128)S(1)} %get-tuple-element.25), channel_id=1, source_target_pairs={{0,0},{1,7},{2,2},{3,5},{4,4},{5,3},{6,6},{7,1},{8,8},{9,15},{10,1... | collective-permute-start | bytes 196616 | tf_op jit(solution)/shard_map/ppermute | solution.py:336
  41.3 1.3 %gamma_other.1 = bf16[256,512]{1,0:T(8,128)(2,1)S(1)} custom-call(bf16[256,4096]{1,0:T(8,128)(2,1)S(1)} %get-tuple-element.31.amp_ref, bf16[512,4096]{1,0:T(8,128)(2,1)S(1)} %get-tuple-element.20.fitted_ref), custom_call_target="tpu_custom_call" | custom-call | flops 1073741824 | bytes 6291456 | tf_op jit(solution)/shard_map/gamma_other/pallas_call | solution.py:256
  42.6 1.6 %collective-permute-start.20 = (bf16[256,512]{1,0:T(8,128)(2,1)S(1)}, bf16[256,512]{1,0:T(8,128)(2,1)S(1)}, u32[]{:S(2)}, u32[]{:S(2)}) collective-permute-start(bf16[256,512]{1,0:T(8,128)(2,1)S(1)} %gamma_other.1), channel_id=1, source_target_pairs={{0,16},{16,0},{1,17},{17,1},{2,18},{18,2},{3,19},{19,3},{4,20},{20... | collective-permute-start | bytes 786440 | tf_op jit(solution)/shard_map/ppermute | solution.py:329
  44.1 0.0 collective-permute-done.16.one_in
  44.1 0.0 collective-permute-done.17.two_in
  44.2 2.7 %collective-permute-start.18 = (f32[32,256]{1,0:T(8,128)S(1)}, f32[32,256]{1,0:T(8,128)S(1)}, u32[]{:S(2)}, u32[]{:S(2)}) collective-permute-start(f32[32,256]{1,0:T(8,128)S(1)} %get-tuple-element.27), channel_id=1, source_target_pairs={{0,8},{1,9},{2,10},{3,11},{4,12},{5,13},{6,14},{7,15},{8,0},{9,1},... | collective-permute-start | bytes 98312 | tf_op jit(solution)/shard_map/ppermute | solution.py:340
  46.8 1.3 %gamma_same.1.refs_0_.gamma_in = f32[256,512]{1,0:T(8,128)S(1)} custom-call(bf16[256,4096]{1,0:T(8,128)(2,1)S(1)} %get-tuple-element.28.amp_ref, bf16[512,4096]{1,0:T(8,128)(2,1)S(1)} %get-tuple-element.20.fitted_ref), custom_call_target="tpu_custom_call" | custom-call | flops 2147483648 | bytes 6291456 | tf_op jit(solution)/shard_map/gamma_same/pallas_call | solution.py:256
  48.1 0.9 %collective-permute-done.18.arrived = f32[32,256]{1,0:T(8,128)S(1)} collective-permute-done((f32[32,256]{1,0:T(8,128)S(1)}, f32[32,256]{1,0:T(8,128)S(1)}, u32[]{:S(2)}, u32[]{:S(2)}) %collective-permute-start.18) | collective-permute-done | bytes 32800 | tf_op jit(solution)/shard_map/ppermute | solution.py:340
  49.0 1.3 %collective-permute-start.19 = (f32[16,256]{1,0:T(8,128)S(1)}, f32[16,256]{1,0:T(8,128)S(1)}, u32[]{:S(2)}, u32[]{:S(2)}) collective-permute-start(f32[16,256]{1,0:T(8,128)S(1)} %get-tuple-element.30), channel_id=1, source_target_pairs={{0,1},{1,0},{2,3},{3,2},{4,5},{5,4},{6,7},{7,6},{8,9},{9,8},{10,11... | collective-permute-start | bytes 49160 | tf_op jit(solution)/shard_map/ppermute | solution.py:344
  50.3 0.8 %collective-permute-done.19.arrived = f32[16,256]{1,0:T(8,128)S(1)} collective-permute-done((f32[16,256]{1,0:T(8,128)S(1)}, f32[16,256]{1,0:T(8,128)S(1)}, u32[]{:S(2)}, u32[]{:S(2)}) %collective-permute-start.19) | collective-permute-done | bytes 16416 | tf_op jit(solution)/shard_map/ppermute | solution.py:344
  51.1 0.0 collective-permute-done.20.refs_0_
  51.1 0.8 %finish.1 = (f32[256,512]{1,0:T(8,128)}, f32[1,16,256]{2,1,0:T(8,128)}) custom-call(f32[16,256]{1,0:T(8,128)S(1)} %get-tuple-element.29.kept_in, f32[16,256]{1,0:T(8,128)S(1)} %collective-permute-done.19.arrived, f32[256,512]{1,0:T(8,128)S(1)} %gamma_same.1.refs_0_.gamma_in, bf16[256,512]{1,0:T(8,128)(2,1)S(1)} %collective-permute-done.20.refs_0_), custom_call_target="tpu_custom_call" | custom-call | tf_op jit(solution)/shard_map/finish/pallas_call | solution.py:256
  (9 shorter events, 0.2 us)
Async XLA Ops:
  0.6 23.7 %copy-start = (bf16[512,512]{1,0:T(8,128)(2,1)S(1)}, bf16[512,512]{1,0:T(8,128)(2,1)}, u32[]{:S(2)}) copy-start(bf16[512,512]{1,0:T(8,128)(2,1)} %given_ref.1) | copy-start | bytes 1572868
  0.6 3.2 %collective-permute-start = (bf16[16,32,256]{2,1,0:T(8,128)(2,1)}, bf16[16,32,256]{2,1,0:T(8,128)(2,1)S(1)}, u32[]{:S(2)}, u32[]{:S(2)}) collective-permute-start(bf16[16,32,256]{2,1,0:T(8,128)(2,1)} %bitcast.5), channel_id=1, source_target_pairs={{0,1},{1,0},{2,3},{3,2},{4,5},{5,4},{6,7},{7,6},{8,9},{9,8},{10,11... | collective-permute-start | bytes 786440 | tf_op jit(solution)/shard_map/ppermute | solution.py:280
  1.2 7.1 %collective-permute-start.1 = (bf16[16,32,256]{2,1,0:T(8,128)(2,1)}, bf16[16,32,256]{2,1,0:T(8,128)(2,1)S(1)}, u32[]{:S(2)}, u32[]{:S(2)}) collective-permute-start(bf16[16,32,256]{2,1,0:T(8,128)(2,1)} %bitcast.6), channel_id=1, source_target_pairs={{0,4},{4,8},{8,12},{12,14},{14,10},{10,6},{6,2},{2,0},{5,1},{9,5},... | collective-permute-start | bytes 786440 | tf_op jit(solution)/shard_map/ppermute | solution.py:284
  3.8 7.3 %collective-permute-start.2 = (bf16[16,32,256]{2,1,0:T(8,128)(2,1)S(1)}, bf16[16,32,256]{2,1,0:T(8,128)(2,1)S(1)}, u32[]{:S(2)}, u32[]{:S(2)}) collective-permute-start(bf16[16,32,256]{2,1,0:T(8,128)(2,1)S(1)} %collective-permute-done.refs_2_.refs_0_), channel_id=1, source_target_pairs={{0,4},{4,8},{8,12},{12,14},{14,10},{10,6},{6,2},{2,0},{5,1},{9,5},... | collective-permute-start | bytes 786440 | tf_op jit(solution)/shard_map/ppermute | solution.py:284
  8.3 6.4 %collective-permute-start.3 = (bf16[16,32,256]{2,1,0:T(8,128)(2,1)S(1)}, bf16[16,32,256]{2,1,0:T(8,128)(2,1)S(1)}, u32[]{:S(2)}, u32[]{:S(2)}) collective-permute-start(bf16[16,32,256]{2,1,0:T(8,128)(2,1)S(1)} %collective-permute-done.1.refs_0_.refs_1_), channel_id=1, source_target_pairs={{0,4},{4,8},{8,12},{12,14},{14,10},{10,6},{6,2},{2,0},{5,1},{9,5},... | collective-permute-start | bytes 786440 | tf_op jit(solution)/shard_map/ppermute | solution.py:284
  11.2 13.2 %collective-permute-start.5 = (bf16[3,16,32,256]{3,2,1,0:T(8,128)(2,1)S(1)}, bf16[3,16,32,256]{3,2,1,0:T(8,128)(2,1)S(1)}, u32[]{:S(2)}, u32[]{:S(2)}) collective-permute-start(bf16[3,16,32,256]{3,2,1,0:T(8,128)(2,1)S(1)} %stack.4), channel_id=1, source_target_pairs={{0,1},{1,0},{2,3},{3,2},{4,5},{5,4},{6,7},{7,6},{8,9},{9,8},{10,11... | collective-permute-start | bytes 2359304 | tf_op jit(solution)/shard_map/ppermute | solution.py:300
  11.2 6.4 %collective-permute-start.4 = (bf16[16,32,256]{2,1,0:T(8,128)(2,1)S(1)}, bf16[16,32,256]{2,1,0:T(8,128)(2,1)S(1)}, u32[]{:S(2)}, u32[]{:S(2)}) collective-permute-start(bf16[16,32,256]{2,1,0:T(8,128)(2,1)S(1)} %collective-permute-done.2.refs_1_.refs_2_), channel_id=1, source_target_pairs={{0,4},{4,8},{8,12},{12,14},{14,10},{10,6},{6,2},{2,0},{5,1},{9,5},... | collective-permute-start | bytes 786440 | tf_op jit(solution)/shard_map/ppermute | solution.py:284
  14.7 6.7 %collective-permute-start.8 = (bf16[16,32,256]{2,1,0:T(8,128)(2,1)S(1)}, bf16[16,32,256]{2,1,0:T(8,128)(2,1)S(1)}, u32[]{:S(2)}, u32[]{:S(2)}) collective-permute-start(bf16[16,32,256]{2,1,0:T(8,128)(2,1)S(1)} %collective-permute-done.3.refs_3_.refs_0_), channel_id=1, source_target_pairs={{0,4},{4,8},{8,12},{12,14},{14,10},{10,6},{6,2},{2,0},{5,1},{9,5},... | collective-permute-start | bytes 786440 | tf_op jit(solution)/shard_map/ppermute | solution.py:284
  17.7 6.5 %collective-permute-start.9 = (bf16[16,32,256]{2,1,0:T(8,128)(2,1)S(1)}, bf16[16,32,256]{2,1,0:T(8,128)(2,1)S(1)}, u32[]{:S(2)}, u32[]{:S(2)}) collective-permute-start(bf16[16,32,256]{2,1,0:T(8,128)(2,1)S(1)} %collective-permute-done.4.refs_4_.refs_1_), channel_id=1, source_target_pairs={{0,4},{4,8},{8,12},{12,14},{14,10},{10,6},{6,2},{2,0},{5,1},{9,5},... | collective-permute-start | bytes 786440 | tf_op jit(solution)/shard_map/ppermute | solution.py:284
  19.8 4.4 %collective-permute-start.6 = (bf16[160,256]{1,0:T(8,128)(2,1)S(1)}, bf16[160,256]{1,0:T(8,128)(2,1)S(1)}, u32[]{:S(2)}, u32[]{:S(2)}) collective-permute-start(bf16[160,256]{1,0:T(8,128)(2,1)S(1)} %early_row.1), channel_id=1, source_target_pairs={{0,16},{16,0},{1,17},{17,1},{2,18},{18,2},{3,19},{19,3},{4,20},{20... | collective-permute-start | bytes 245768 | tf_op jit(solution)/shard_map/ppermute | solution.py:289
  21.3 6.6 %collective-permute-start.7 = (bf16[2,16,32,256]{3,2,1,0:T(8,128)(2,1)S(1)}, bf16[2,16,32,256]{3,2,1,0:T(8,128)(2,1)S(1)}, u32[]{:S(2)}, u32[]{:S(2)}) collective-permute-start(bf16[2,16,32,256]{3,2,1,0:T(8,128)(2,1)S(1)} %stack.5), channel_id=1, source_target_pairs={{0,1},{1,0},{2,3},{3,2},{4,5},{5,4},{6,7},{7,6},{8,9},{9,8},{10,11... | collective-permute-start | bytes 1572872 | tf_op jit(solution)/shard_map/ppermute | solution.py:300
  21.4 6.4 %collective-permute-start.12 = (bf16[16,32,256]{2,1,0:T(8,128)(2,1)S(1)}, bf16[16,32,256]{2,1,0:T(8,128)(2,1)S(1)}, u32[]{:S(2)}, u32[]{:S(2)}) collective-permute-start(bf16[16,32,256]{2,1,0:T(8,128)(2,1)S(1)} %collective-permute-done.8.refs_2_.refs_0_.refs_1_), channel_id=1, source_target_pairs={{0,4},{4,8},{8,12},{12,14},{14,10},{10,6},{6,2},{2,0},{5,1},{9,5},... | collective-permute-start | bytes 786440 | tf_op jit(solution)/shard_map/ppermute | solution.py:284
  24.2 5.4 %collective-permute-start.11 = (bf16[2,16,32,256]{3,2,1,0:T(8,128)(2,1)S(1)}, bf16[2,16,32,256]{3,2,1,0:T(8,128)(2,1)S(1)}, u32[]{:S(2)}, u32[]{:S(2)}) collective-permute-start(bf16[2,16,32,256]{3,2,1,0:T(8,128)(2,1)S(1)} %stack.6), channel_id=1, source_target_pairs={{0,1},{1,0},{2,3},{3,2},{4,5},{5,4},{6,7},{7,6},{8,9},{9,8},{10,11... | collective-permute-start | bytes 1572872 | tf_op jit(solution)/shard_map/ppermute | solution.py:300
  27.8 3.2 %copy-start.1 = (f32[2,256]{1,0:T(2,128)S(1)}, f32[2,256]{1,0:T(2,128)}, u32[]{:S(2)}) copy-start(f32[2,256]{1,0:T(2,128)} %virt_ref.3) | copy-start | bytes 6148
  27.8 3.2 %copy-start.2 = (f32[2,16]{1,0:T(2,128)S(1)}, f32[2,16]{1,0:T(2,128)}, u32[]{:S(2)}) copy-start(f32[2,16]{1,0:T(2,128)} %occ_ref.3) | copy-start | bytes 388
  27.8 1.8 %collective-permute-start.13 = (bf16[1,16,32,256]{3,2,1,0:T(8,128)(2,1)S(1)}, bf16[1,16,32,256]{3,2,1,0:T(8,128)(2,1)S(1)}, u32[]{:S(2)}, u32[]{:S(2)}) collective-permute-start(bf16[1,16,32,256]{3,2,1,0:T(8,128)(2,1)S(1)} %stack.7), channel_id=1, source_target_pairs={{0,1},{1,0},{2,3},{3,2},{4,5},{5,4},{6,7},{7,6},{8,9},{9,8},{10,11... | collective-permute-start | bytes 786440 | tf_op jit(solution)/shard_map/ppermute | solution.py:300
  27.9 6.9 %collective-permute-start.10 = (bf16[224,256]{1,0:T(8,128)(2,1)S(1)}, bf16[224,256]{1,0:T(8,128)(2,1)S(1)}, u32[]{:S(2)}, u32[]{:S(2)}) collective-permute-start(bf16[224,256]{1,0:T(8,128)(2,1)S(1)} %late_row.2), channel_id=1, source_target_pairs={{0,16},{16,0},{1,17},{17,1},{2,18},{18,2},{3,19},{19,3},{4,20},{20... | collective-permute-start | bytes 344072 | tf_op jit(solution)/shard_map/ppermute | solution.py:307
  29.6 5.3 %collective-permute-start.14 = (bf16[128,256]{1,0:T(8,128)(2,1)S(1)}, bf16[128,256]{1,0:T(8,128)(2,1)S(1)}, u32[]{:S(2)}, u32[]{:S(2)}) collective-permute-start(bf16[128,256]{1,0:T(8,128)(2,1)S(1)} %late_row.3), channel_id=1, source_target_pairs={{0,16},{16,0},{1,17},{17,1},{2,18},{18,2},{3,19},{19,3},{4,20},{20... | collective-permute-start | bytes 196616 | tf_op jit(solution)/shard_map/ppermute | solution.py:307
  37.5 1.4 %collective-permute-start.15 = (f32[2,2,32,256]{3,2,1,0:T(8,128)S(1)}, f32[2,2,32,256]{3,2,1,0:T(8,128)S(1)}, u32[]{:S(2)}, u32[]{:S(2)}) collective-permute-start(f32[2,2,32,256]{3,2,1,0:T(8,128)S(1)} %get-tuple-element.23), channel_id=1, source_target_pairs={{0,1},{1,0},{2,3},{3,2},{4,5},{5,4},{6,7},{7,6},{8,9},{9,8},{10,11... | collective-permute-start | bytes 393224 | tf_op jit(solution)/shard_map/ppermute | solution.py:330
  38.9 5.2 %collective-permute-start.16 = (f32[2,32,256]{2,1,0:T(8,128)S(1)}, f32[2,32,256]{2,1,0:T(8,128)S(1)}, u32[]{:S(2)}, u32[]{:S(2)}) collective-permute-start(f32[2,32,256]{2,1,0:T(8,128)S(1)} %get-tuple-element.24), channel_id=1, source_target_pairs={{0,2},{1,5},{2,0},{3,7},{4,6},{5,1},{6,4},{7,3},{8,10},{9,13},{10,... | collective-permute-start | bytes 196616 | tf_op jit(solution)/shard_map/ppermute | solution.py:335
  40.6 3.5 %collective-permute-start.17 = (f32[2,32,256]{2,1,0:T(8,128)S(1)}, f32[2,32,256]{2,1,0:T(8,128)S(1)}, u32[]{:S(2)}, u32[]{:S(2)}) collective-permute-start(f32[2,32,256]{2,1,0:T(8,128)S(1)} %get-tuple-element.25), channel_id=1, source_target_pairs={{0,0},{1,7},{2,2},{3,5},{4,4},{5,3},{6,6},{7,1},{8,8},{9,15},{10,1... | collective-permute-start | bytes 196616 | tf_op jit(solution)/shard_map/ppermute | solution.py:336
  42.6 8.6 %collective-permute-start.20 = (bf16[256,512]{1,0:T(8,128)(2,1)S(1)}, bf16[256,512]{1,0:T(8,128)(2,1)S(1)}, u32[]{:S(2)}, u32[]{:S(2)}) collective-permute-start(bf16[256,512]{1,0:T(8,128)(2,1)S(1)} %gamma_other.1), channel_id=1, source_target_pairs={{0,16},{16,0},{1,17},{17,1},{2,18},{18,2},{3,19},{19,3},{4,20},{20... | collective-permute-start | bytes 786440 | tf_op jit(solution)/shard_map/ppermute | solution.py:329
  44.2 4.9 %collective-permute-start.18 = (f32[32,256]{1,0:T(8,128)S(1)}, f32[32,256]{1,0:T(8,128)S(1)}, u32[]{:S(2)}, u32[]{:S(2)}) collective-permute-start(f32[32,256]{1,0:T(8,128)S(1)} %get-tuple-element.27), channel_id=1, source_target_pairs={{0,8},{1,9},{2,10},{3,11},{4,12},{5,13},{6,14},{7,15},{8,0},{9,1},... | collective-permute-start | bytes 98312 | tf_op jit(solution)/shard_map/ppermute | solution.py:340
  49.0 2.1 %collective-permute-start.19 = (f32[16,256]{1,0:T(8,128)S(1)}, f32[16,256]{1,0:T(8,128)S(1)}, u32[]{:S(2)}, u32[]{:S(2)}) collective-permute-start(f32[16,256]{1,0:T(8,128)S(1)} %get-tuple-element.30), channel_id=1, source_target_pairs={{0,1},{1,0},{2,3},{3,2},{4,5},{5,4},{6,7},{7,6},{8,9},{9,8},{10,11... | collective-permute-start | bytes 49160 | tf_op jit(solution)/shard_map/ppermute | solution.py:344

commit v6 on v5

--- a/solution.py
+++ b/solution.py
@@ -156,18 +156,19 @@
     raw = jnp.concatenate(list(pieces(slices, own)), axis=0)
     early = early_ref[:, pl.ds(pl.multiple_of(own * nv, nv), nv)]
     left[...] = (early + dot(factor_ref[:, first:], raw, NN)).astype(left.dtype).T
+    for start in range(0, count, GROUP):
+        raw = [jnp.concatenate(list(pieces(slices, j)), axis=0) for j in range(start, start + GROUP)]
+        columns = slice(start * nv, (start + GROUP) * nv)
+        late = dot(factor_ref[:, first:], jnp.concatenate(raw, axis=1), NN)
+        fitted_ref[:, columns] = (early_ref[:, columns] + late).astype(fitted_ref.dtype)
     total = None
     for start in range(0, count, GROUP):
-        members = range(start, start + GROUP)
-        raw = [jnp.concatenate(list(pieces(slices, j)), axis=0) for j in members]
         columns = slice(start * nv, (start + GROUP) * nv)
-        late = dot(factor_ref[:, first:], jnp.concatenate(raw, axis=1), NN)
-        fitted = (early_ref[:, columns] + late).astype(fitted_ref.dtype)
-        fitted_ref[:, columns] = fitted
-        couplings = dot(left[...], fitted, NN)
+        couplings = dot(left[...], fitted_ref[:, columns], NN)
         amps = []
-        for n, j in enumerate(members):
+        for n in range(GROUP):
             coupling = couplings[:, n * nv : (n + 1) * nv]
+            j = start + n
             amps.append(amplitudes(coupling - coupling.T, energies[:, j : j + 1], sums[...]))
         amps = jnp.concatenate(amps, axis=1)
         amp_ref[:, columns] = amps
@@ -203,7 +204,8 @@
     for ref, lane in ((kept_ref, core), (sent_ref, 1 - core)):
         for m in range(near):
             for n in range(far):
-                there = ((chip ^ (near * lane + m)) & (2 * near - 1)) + 2 * near * n
+                offset = lane + m * (3 - 2 * lane)
+                there = ((chip ^ offset) & (2 * near - 1)) + 2 * near * n
                 ref[m, n] = dens[pl.ds(pl.multiple_of(there * rows, rows), rows)]
 
 
@@ -225,7 +227,7 @@
 def far_split_kernel(one_in, two_in, *refs):
     kept_ref, sent_ref, total = refs[-3:]
     total[...] = one_in[...] + two_in[...]
-    mine = lax.axis_index("orb") // 8
+    mine = lax.axis_index("orb") // (lax.axis_size("orb") // 2)
     kept_ref[...] = total[mine]
     sent_ref[...] = total[1 - mine]
 
@@ -301,7 +303,7 @@
         if step >= steps - 2:
             slices += swapped
             swapped = []
-    rows_sent, cut = [early_row], sent+4
+    rows_sent, cut = [early_row], sent + 4
     for part in (slices[sent:cut], slices[cut:]):
         (row,) = vmem_call(row_kernel, "late_row", part, [((depth(part), nv), half)])
         rows_sent.append(lax.ppermute(row, "spin", across))
@@ -324,20 +326,20 @@
         flops=pair * naux,
     )
     (gamma_same,) = vmem_call(
-        gamma_kernel, "gamma_same", [amp_same, fitted], [((nv, naux), full)], flops=2*pair*naux
+        gamma_kernel, "gamma_same", [amp_same, fitted], [((nv, naux), full)], flops=2 * pair * naux
     )
     returned = [lax.ppermute(piece, "spin", across) for piece in gamma_other]
     arrived = lax.ppermute(sent, "orb", swap)
-    one, two = vmem_call(near_kernel, "near", [kept, arrived], [(share[1:], full)] * 2, [(share, full)])
+    one, two = vmem_call(near_kernel, "near", [kept, arrived] + list(gamma_other), [(share[1:], full)] * 2, [(share, full)])
     chip_moves = lambda first, second: [
         (d, 2 * (d // 2 ^ (second if d % 2 else first)) + d % 2) for d in range(orb_count)
     ]
-    one = lax.ppermute(one, "orb", chip_moves(1, 2))
-    two = lax.ppermute(two, "orb", chip_moves(0, 3))
+    one = lax.ppermute(one, "orb", chip_moves(3, 1))
+    two = lax.ppermute(two, "orb", chip_moves(0, 2))
     kept, sent = vmem_call(
         far_split_kernel, "far_split", [one, two], [(share[2:], full)] * 2, [(share[1:], full)]
     )
-    arrived = lax.ppermute(sent, "orb", chip_moves(4, 4))
+    arrived = lax.ppermute(sent, "orb", chip_moves(orb_count // 4, orb_count // 4))
     kept, sent = vmem_call(
         core_split_kernel, "core_split", [kept, arrived, gamma_same], [((rows // 2, nv), full)] * 2, [(share[2:], full)]
     )
@@ -527,7 +529,7 @@
 
 def local(integrals, metric_factor, occ_energy, virt_energy, orb_count):
     _, count, nv, width = integrals.shape
-    fits = orb_count == 16 and count * nv * metric_factor.shape[0] * 2 <= 4 * 1024 * 1024 and width % 16 == 0 and count % GROUP == 0
+    fits = orb_count // 2 == 4 * 2 and count * nv * metric_factor.shape[0] * 2 <= 4 * 1024 * 1024 and width % 16 == 0 and count % GROUP == 0
     chosen = local_in_vmem if fits else local_streamed
     return chosen(integrals, metric_factor, occ_energy, virt_energy, orb_count)
 

time: 52.2 us -> 52.1 us (level)
  starting transfers between devices: 27.7 us -> 28.8 us
  waiting for transfers between devices: 12.2 us -> 11.2 us
    ppermute x2, waiting for transfers between devices: 2.17 us -> 0.89 us  [local_in_vmem(): arrived = lax.ppermute(sent, 'orb', swap)]
    ppermute x3, starting transfers between devices: 5.01 us -> 6.16 us  [the longest x1 2.78 us: local_in_vmem(): lax.ppermute(sent, 'orb', chip_moves(orb_count // 4, orb_count // 4))]
  transfers between devices with their start and end apart: 21 -> 21, of which waited for: 10 -> 11; matrix products, arithmetic and copies ran while one was open for 0% -> 0% of each run, Pallas kernels for 15% -> 15%
where the time goes in v6:
time: 52.1 us; the launch traced here: 52 us
  starting transfers between devices  28.8 us (55%)
  waiting for transfers between devices  11.2 us (21%)
  Pallas kernels  11.1 us (21%)
  between operations  0.81 us (2%)
    ppermute x7, starting transfers between devices, local_in_vmem(): lax.ppermute(lane, 'orb', moves)  14.4 us
    pallas_call x16, Pallas kernels, vmem_call(): pl.pallas_call(kernel, in_specs=[hbm] * in_hbm + [vmem] * (len(operands)...  11.1 us
    ppermute x7, waiting for transfers between devices, local_in_vmem(): lax.ppermute(lane, 'orb', moves)  7.9 us
    ppermute x2, starting transfers between devices, local_in_vmem(): rows_sent.append(lax.ppermute(row, 'spin', across))  3.09 us
    ppermute x1, starting transfers between devices, local_in_vmem(): lax.ppermute(sent, 'orb', chip_moves(orb_count // 4, orb_count // 4))  2.78 us
    ppermute x1, starting transfers between devices, local_in_vmem(): one = lax.ppermute(one, 'orb', chip_moves(3, 1))  2.72 us
    ppermute x1, starting transfers between devices, local_in_vmem(): returned = [lax.ppermute(piece, 'spin', across) for piece in gamma_other]  1.55 us
    ppermute x1, starting transfers between devices, local_in_vmem(): early_row = lax.ppermute(row, 'spin', across)  1.49 us
  transfers between devices with their start and end apart: 21, of which 11 were waited for; matrix products, arithmetic and copies ran while one was open for 0% of the time, Pallas kernels for 15%

profile of v6, /device:TPU:0, one launch (start us, length us, event | category | flops | bytes accessed | tf_op | source)
XLA Modules:
  0.0 52.0 jit_solution(10562073840902024284)
XLA Ops:
  0.6 0.0 copy-start
  0.6 0.5 collective-permute-start
  1.2 2.6 %collective-permute-start.1 = (bf16[16,32,256]{2,1,0:T(8,128)(2,1)}, bf16[16,32,256]{2,1,0:T(8,128)(2,1)S(1)}, u32[]{:S(2)}, u32[]{:S(2)}) collective-permute-start(bf16[16,32,256]{2,1,0:T(8,128)(2,1)} %bitcast.6), channel_id=1, source_target_pairs={{0,4},{4,8},{8,12},{12,14},{14,10},{10,6},{6,2},{2,0},{5,1},{9,5},... | collective-permute-start | bytes 786440 | tf_op jit(solution)/shard_map/ppermute | solution.py:286
  3.8 0.0 collective-permute-done.refs_2_.refs_0_
  3.8 1.7 %collective-permute-start.2 = (bf16[16,32,256]{2,1,0:T(8,128)(2,1)S(1)}, bf16[16,32,256]{2,1,0:T(8,128)(2,1)S(1)}, u32[]{:S(2)}, u32[]{:S(2)}) collective-permute-start(bf16[16,32,256]{2,1,0:T(8,128)(2,1)S(1)} %collective-permute-done.refs_2_.refs_0_), channel_id=1, source_target_pairs={{0,4},{4,8},{8,12},{12,14},{14,10},{10,6},{6,2},{2,0},{5,1},{9,5},... | collective-permute-start | bytes 786440 | tf_op jit(solution)/shard_map/ppermute | solution.py:286
  5.5 2.8 %collective-permute-done.1.refs_0_.refs_1_ = bf16[16,32,256]{2,1,0:T(8,128)(2,1)S(1)} collective-permute-done((bf16[16,32,256]{2,1,0:T(8,128)(2,1)}, bf16[16,32,256]{2,1,0:T(8,128)(2,1)S(1)}, u32[]{:S(2)}, u32[]{:S(2)}) %collective-permute-start.1) | collective-permute-done | bytes 262176 | tf_op jit(solution)/shard_map/ppermute | solution.py:286
  8.3 2.1 %collective-permute-start.3 = (bf16[16,32,256]{2,1,0:T(8,128)(2,1)S(1)}, bf16[16,32,256]{2,1,0:T(8,128)(2,1)S(1)}, u32[]{:S(2)}, u32[]{:S(2)}) collective-permute-start(bf16[16,32,256]{2,1,0:T(8,128)(2,1)S(1)} %collective-permute-done.1.refs_0_.refs_1_), channel_id=1, source_target_pairs={{0,4},{4,8},{8,12},{12,14},{14,10},{10,6},{6,2},{2,0},{5,1},{9,5},... | collective-permute-start | bytes 786440 | tf_op jit(solution)/shard_map/ppermute | solution.py:286
  10.4 0.7 %collective-permute-done.2.refs_1_.refs_2_ = bf16[16,32,256]{2,1,0:T(8,128)(2,1)S(1)} collective-permute-done((bf16[16,32,256]{2,1,0:T(8,128)(2,1)S(1)}, bf16[16,32,256]{2,1,0:T(8,128)(2,1)S(1)}, u32[]{:S(2)}, u32[]{:S(2)}) %collective-permute-start.2) | collective-permute-done | bytes 262176 | tf_op jit(solution)/shard_map/ppermute | solution.py:286
  11.1 0.1 stack.4
  11.2 0.1 collective-permute-start.5
  11.2 2.1 %collective-permute-start.4 = (bf16[16,32,256]{2,1,0:T(8,128)(2,1)S(1)}, bf16[16,32,256]{2,1,0:T(8,128)(2,1)S(1)}, u32[]{:S(2)}, u32[]{:S(2)}) collective-permute-start(bf16[16,32,256]{2,1,0:T(8,128)(2,1)S(1)} %collective-permute-done.2.refs_1_.refs_2_), channel_id=1, source_target_pairs={{0,4},{4,8},{8,12},{12,14},{14,10},{10,6},{6,2},{2,0},{5,1},{9,5},... | collective-permute-start | bytes 786440 | tf_op jit(solution)/shard_map/ppermute | solution.py:286
  13.4 1.3 %collective-permute-done.3.refs_3_.refs_0_ = bf16[16,32,256]{2,1,0:T(8,128)(2,1)S(1)} collective-permute-done((bf16[16,32,256]{2,1,0:T(8,128)(2,1)S(1)}, bf16[16,32,256]{2,1,0:T(8,128)(2,1)S(1)}, u32[]{:S(2)}, u32[]{:S(2)}) %collective-permute-start.3) | collective-permute-done | bytes 262176 | tf_op jit(solution)/shard_map/ppermute | solution.py:286
  14.7 2.1 %collective-permute-start.8 = (bf16[16,32,256]{2,1,0:T(8,128)(2,1)S(1)}, bf16[16,32,256]{2,1,0:T(8,128)(2,1)S(1)}, u32[]{:S(2)}, u32[]{:S(2)}) collective-permute-start(bf16[16,32,256]{2,1,0:T(8,128)(2,1)S(1)} %collective-permute-done.3.refs_3_.refs_0_), channel_id=1, source_target_pairs={{0,4},{4,8},{8,12},{12,14},{14,10},{10,6},{6,2},{2,0},{5,1},{9,5},... | collective-permute-start | bytes 786440 | tf_op jit(solution)/shard_map/ppermute | solution.py:286
  16.7 0.9 %collective-permute-done.4.refs_4_.refs_1_ = bf16[16,32,256]{2,1,0:T(8,128)(2,1)S(1)} collective-permute-done((bf16[16,32,256]{2,1,0:T(8,128)(2,1)S(1)}, bf16[16,32,256]{2,1,0:T(8,128)(2,1)S(1)}, u32[]{:S(2)}, u32[]{:S(2)}) %collective-permute-start.4) | collective-permute-done | bytes 262176 | tf_op jit(solution)/shard_map/ppermute | solution.py:286
  17.7 2.1 %collective-permute-start.9 = (bf16[16,32,256]{2,1,0:T(8,128)(2,1)S(1)}, bf16[16,32,256]{2,1,0:T(8,128)(2,1)S(1)}, u32[]{:S(2)}, u32[]{:S(2)}) collective-permute-start(bf16[16,32,256]{2,1,0:T(8,128)(2,1)S(1)} %collective-permute-done.4.refs_4_.refs_1_), channel_id=1, source_target_pairs={{0,4},{4,8},{8,12},{12,14},{14,10},{10,6},{6,2},{2,0},{5,1},{9,5},... | collective-permute-start | bytes 786440 | tf_op jit(solution)/shard_map/ppermute | solution.py:286
  19.8 1.5 %collective-permute-start.6 = (bf16[160,256]{1,0:T(8,128)(2,1)S(1)}, bf16[160,256]{1,0:T(8,128)(2,1)S(1)}, u32[]{:S(2)}, u32[]{:S(2)}) collective-permute-start(bf16[160,256]{1,0:T(8,128)(2,1)S(1)} %early_row.1), channel_id=1, source_target_pairs={{0,16},{16,0},{1,17},{17,1},{2,18},{18,2},{3,19},{19,3},{4,20},{20... | collective-permute-start | bytes 245768 | tf_op jit(solution)/shard_map/ppermute | solution.py:291
  21.3 0.1 collective-permute-start.7
  21.4 0.0 collective-permute-done.8.refs_2_.refs_0_.refs_1_
  21.4 1.8 %collective-permute-start.12 = (bf16[16,32,256]{2,1,0:T(8,128)(2,1)S(1)}, bf16[16,32,256]{2,1,0:T(8,128)(2,1)S(1)}, u32[]{:S(2)}, u32[]{:S(2)}) collective-permute-start(bf16[16,32,256]{2,1,0:T(8,128)(2,1)S(1)} %collective-permute-done.8.refs_2_.refs_0_.refs_1_), channel_id=1, source_target_pairs={{0,4},{4,8},{8,12},{12,14},{14,10},{10,6},{6,2},{2,0},{5,1},{9,5},... | collective-permute-start | bytes 786440 | tf_op jit(solution)/shard_map/ppermute | solution.py:286
  23.1 1.1 %collective-permute-done.6.refs_2_.early_ref = bf16[160,256]{1,0:T(8,128)(2,1)S(1)} collective-permute-done((bf16[160,256]{1,0:T(8,128)(2,1)S(1)}, bf16[160,256]{1,0:T(8,128)(2,1)S(1)}, u32[]{:S(2)}, u32[]{:S(2)}) %collective-permute-start.6) | collective-permute-done | bytes 81952 | tf_op jit(solution)/shard_map/ppermute | solution.py:291
  24.2 0.0 collective-permute-done.9.refs_3_.refs_1_.refs_2_
  24.2 0.1 collective-permute-start.11
  24.3 0.0 collective-permute-done.5.refs_5_.refs_0_
  24.3 0.0 copy-done
  24.3 1.3 %early_fit.1 = (bf16[512,512]{1,0:T(8,128)(2,1)S(1)}, f32[512,4096]{1,0:T(8,128)S(1)}) custom-call(bf16[512,512]{1,0:T(8,128)(2,1)S(1)} %copy-done, bf16[16,32,256]{2,1,0:T(8,128)(2,1)S(1)} %collective-permute-done.refs_2_.refs_0_, bf16[16,32,256]{2,1,0:T(8,128)(2,1)S(1)} %collective-permute-done.1.refs_0_.refs_1_, ...), custom_call_target="tpu_custom_call" | custom-call | tf_op jit(solution)/shard_map/early_fit/pallas_call | solution.py:258
  25.7 2.1 %collective-permute-done.12.refs_0_.refs_1_.refs_4_ = bf16[16,32,256]{2,1,0:T(8,128)(2,1)S(1)} collective-permute-done((bf16[16,32,256]{2,1,0:T(8,128)(2,1)S(1)}, bf16[16,32,256]{2,1,0:T(8,128)(2,1)S(1)}, u32[]{:S(2)}, u32[]{:S(2)}) %collective-permute-start.12) | collective-permute-done | bytes 262176 | tf_op jit(solution)/shard_map/ppermute | solution.py:286
  27.8 0.0 copy-start.1
  27.8 0.0 copy-start.2
  27.8 0.1 collective-permute-start.13
  27.9 0.0 collective-permute-done.7.refs_1_.refs_0_
  27.9 1.7 %collective-permute-start.10 = (bf16[224,256]{1,0:T(8,128)(2,1)S(1)}, bf16[224,256]{1,0:T(8,128)(2,1)S(1)}, u32[]{:S(2)}, u32[]{:S(2)}) collective-permute-start(bf16[224,256]{1,0:T(8,128)(2,1)S(1)} %late_row.2), channel_id=1, source_target_pairs={{0,16},{16,0},{1,17},{17,1},{2,18},{18,2},{3,19},{19,3},{4,20},{20... | collective-permute-start | bytes 344072 | tf_op jit(solution)/shard_map/ppermute | solution.py:309
  29.6 0.0 collective-permute-done.11.refs_0_.refs_3_
  29.6 0.0 collective-permute-done.13.refs_2_.refs_5_
  29.6 1.4 %collective-permute-start.14 = (bf16[128,256]{1,0:T(8,128)(2,1)S(1)}, bf16[128,256]{1,0:T(8,128)(2,1)S(1)}, u32[]{:S(2)}, u32[]{:S(2)}) collective-permute-start(bf16[128,256]{1,0:T(8,128)(2,1)S(1)} %late_row.3), channel_id=1, source_target_pairs={{0,16},{16,0},{1,17},{17,1},{2,18},{18,2},{3,19},{19,3},{4,20},{20... | collective-permute-start | bytes 196616 | tf_op jit(solution)/shard_map/ppermute | solution.py:309
  31.0 0.0 copy-done.1
  31.0 0.0 copy-done.2
  31.0 3.6 %fit_same.1 = (bf16[512,4096]{1,0:T(8,128)(2,1)S(1)}, bf16[256,4096]{1,0:T(8,128)(2,1)S(1)}, f32[256,256]{1,0:T(8,128)S(1)}) custom-call(f32[2,16]{1,0:T(2,128)S(1)} %copy-done.2, f32[2,256]{1,0:T(2,128)S(1)} %copy-done.1, bf16[512,512]{1,0:T(8,128)(2,1)S(1)} %get-tuple-element.18.factor_ref, f32[512,4096]{1,0:T(8,128)S(1)} %get-tuple-element.19.refs_1_.early_ref, ...), custom_call_target="tpu_custom_call" | custom-call | tf_op jit(solution)/shard_map/fit_same/pallas_call | solution.py:258
  34.7 0.0 collective-permute-done.10.late_ref
  34.7 0.2 collective-permute-done.14.last_ref
  34.9 2.5 %opposite.1 = (bf16[256,4096]{1,0:T(8,128)(2,1)S(1)}, f32[2,2,32,256]{3,2,1,0:T(8,128)S(1)}, f32[2,2,32,256]{3,2,1,0:T(8,128)S(1)}) custom-call(f32[2,16]{1,0:T(2,128)S(1)} %copy-done.2, f32[2,256]{1,0:T(2,128)S(1)} %copy-done.1, bf16[512,512]{1,0:T(8,128)(2,1)S(1)} %get-tuple-element.18.factor_ref, ...), custom_call_target="tpu_custom_call" | custom-call | flops 1610612736 | bytes 5245056 | tf_op jit(solution)/shard_map/opposite/pallas_call | solution.py:258
  37.5 0.1 collective-permute-start.15
  37.5 1.3 %gamma_other.1.refs_0_ = bf16[256,512]{1,0:T(8,128)(2,1)S(1)} custom-call(bf16[256,4096]{1,0:T(8,128)(2,1)S(1)} %get-tuple-element.24.amp_ref, bf16[512,4096]{1,0:T(8,128)(2,1)S(1)} %get-tuple-element.20.fitted_ref), custom_call_target="tpu_custom_call" | custom-call | flops 1073741824 | bytes 6291456 | tf_op jit(solution)/shard_map/gamma_other/pallas_call | solution.py:258
  38.8 0.1 collective-permute-done.15.arrived
  38.9 2.7 %collective-permute-start.16 = (f32[2,32,256]{2,1,0:T(8,128)S(1)}, f32[2,32,256]{2,1,0:T(8,128)S(1)}, u32[]{:S(2)}, u32[]{:S(2)}) collective-permute-start(f32[2,32,256]{2,1,0:T(8,128)S(1)} %get-tuple-element.25), channel_id=1, source_target_pairs={{0,6},{1,3},{2,4},{3,1},{4,2},{5,7},{6,0},{7,5},{8,14},{9,11},{10,... | collective-permute-start | bytes 196616 | tf_op jit(solution)/shard_map/ppermute | solution.py:337
  41.6 0.7 %collective-permute-start.17 = (f32[2,32,256]{2,1,0:T(8,128)S(1)}, f32[2,32,256]{2,1,0:T(8,128)S(1)}, u32[]{:S(2)}, u32[]{:S(2)}) collective-permute-start(f32[2,32,256]{2,1,0:T(8,128)S(1)} %get-tuple-element.26), channel_id=1, source_target_pairs={{0,0},{1,5},{2,2},{3,7},{4,4},{5,1},{6,6},{7,3},{8,8},{9,13},{10,1... | collective-permute-start | bytes 196616 | tf_op jit(solution)/shard_map/ppermute | solution.py:338
  42.3 1.6 %collective-permute-start.20 = (bf16[256,512]{1,0:T(8,128)(2,1)S(1)}, bf16[256,512]{1,0:T(8,128)(2,1)S(1)}, u32[]{:S(2)}, u32[]{:S(2)}) collective-permute-start(bf16[256,512]{1,0:T(8,128)(2,1)S(1)} %gamma_other.1.refs_0_), channel_id=1, source_target_pairs={{0,16},{16,0},{1,17},{17,1},{2,18},{18,2},{3,19},{19,3},{4,20},{20... | collective-permute-start | bytes 786440 | tf_op jit(solution)/shard_map/ppermute | solution.py:331
  43.8 0.3 collective-permute-done.16.one_in
  44.1 0.0 collective-permute-done.17.two_in
  44.2 2.8 %collective-permute-start.18 = (f32[32,256]{1,0:T(8,128)S(1)}, f32[32,256]{1,0:T(8,128)S(1)}, u32[]{:S(2)}, u32[]{:S(2)}) collective-permute-start(f32[32,256]{1,0:T(8,128)S(1)} %get-tuple-element.28), channel_id=1, source_target_pairs={{0,8},{1,9},{2,10},{3,11},{4,12},{5,13},{6,14},{7,15},{8,0},{9,1},... | collective-permute-start | bytes 98312 | tf_op jit(solution)/shard_map/ppermute | solution.py:342
  46.9 1.3 %gamma_same.1.refs_0_.gamma_in = f32[256,512]{1,0:T(8,128)S(1)} custom-call(bf16[256,4096]{1,0:T(8,128)(2,1)S(1)} %get-tuple-element.29.amp_ref, bf16[512,4096]{1,0:T(8,128)(2,1)S(1)} %get-tuple-element.20.fitted_ref), custom_call_target="tpu_custom_call" | custom-call | flops 2147483648 | bytes 6291456 | tf_op jit(solution)/shard_map/gamma_same/pallas_call | solution.py:258
  48.2 0.8 %collective-permute-done.18.arrived = f32[32,256]{1,0:T(8,128)S(1)} collective-permute-done((f32[32,256]{1,0:T(8,128)S(1)}, f32[32,256]{1,0:T(8,128)S(1)}, u32[]{:S(2)}, u32[]{:S(2)}) %collective-permute-start.18) | collective-permute-done | bytes 32800 | tf_op jit(solution)/shard_map/ppermute | solution.py:342
  49.1 1.2 %collective-permute-start.19 = (f32[16,256]{1,0:T(8,128)S(1)}, f32[16,256]{1,0:T(8,128)S(1)}, u32[]{:S(2)}, u32[]{:S(2)}) collective-permute-start(f32[16,256]{1,0:T(8,128)S(1)} %get-tuple-element.31), channel_id=1, source_target_pairs={{0,1},{1,0},{2,3},{3,2},{4,5},{5,4},{6,7},{7,6},{8,9},{9,8},{10,11... | collective-permute-start | bytes 49160 | tf_op jit(solution)/shard_map/ppermute | solution.py:346
  50.3 0.8 %collective-permute-done.19.arrived = f32[16,256]{1,0:T(8,128)S(1)} collective-permute-done((f32[16,256]{1,0:T(8,128)S(1)}, f32[16,256]{1,0:T(8,128)S(1)}, u32[]{:S(2)}, u32[]{:S(2)}) %collective-permute-start.19) | collective-permute-done | bytes 16416 | tf_op jit(solution)/shard_map/ppermute | solution.py:346
  51.1 0.0 collective-permute-done.20.refs_0_
  51.1 0.8 %finish.1 = (f32[256,512]{1,0:T(8,128)}, f32[1,16,256]{2,1,0:T(8,128)}) custom-call(f32[16,256]{1,0:T(8,128)S(1)} %get-tuple-element.30.kept_in, f32[16,256]{1,0:T(8,128)S(1)} %collective-permute-done.19.arrived, f32[256,512]{1,0:T(8,128)S(1)} %gamma_same.1.refs_0_.gamma_in, bf16[256,512]{1,0:T(8,128)(2,1)S(1)} %collective-permute-done.20.refs_0_), custom_call_target="tpu_custom_call" | custom-call | tf_op jit(solution)/shard_map/finish/pallas_call | solution.py:258
  (9 shorter events, 0.2 us)
Async XLA Ops:
  0.6 23.7 %copy-start = (bf16[512,512]{1,0:T(8,128)(2,1)S(1)}, bf16[512,512]{1,0:T(8,128)(2,1)}, u32[]{:S(2)}) copy-start(bf16[512,512]{1,0:T(8,128)(2,1)} %given_ref.1) | copy-start | bytes 1572868
  0.6 3.2 %collective-permute-start = (bf16[16,32,256]{2,1,0:T(8,128)(2,1)}, bf16[16,32,256]{2,1,0:T(8,128)(2,1)S(1)}, u32[]{:S(2)}, u32[]{:S(2)}) collective-permute-start(bf16[16,32,256]{2,1,0:T(8,128)(2,1)} %bitcast.5), channel_id=1, source_target_pairs={{0,1},{1,0},{2,3},{3,2},{4,5},{5,4},{6,7},{7,6},{8,9},{9,8},{10,11... | collective-permute-start | bytes 786440 | tf_op jit(solution)/shard_map/ppermute | solution.py:282
  1.2 7.1 %collective-permute-start.1 = (bf16[16,32,256]{2,1,0:T(8,128)(2,1)}, bf16[16,32,256]{2,1,0:T(8,128)(2,1)S(1)}, u32[]{:S(2)}, u32[]{:S(2)}) collective-permute-start(bf16[16,32,256]{2,1,0:T(8,128)(2,1)} %bitcast.6), channel_id=1, source_target_pairs={{0,4},{4,8},{8,12},{12,14},{14,10},{10,6},{6,2},{2,0},{5,1},{9,5},... | collective-permute-start | bytes 786440 | tf_op jit(solution)/shard_map/ppermute | solution.py:286
  3.8 7.3 %collective-permute-start.2 = (bf16[16,32,256]{2,1,0:T(8,128)(2,1)S(1)}, bf16[16,32,256]{2,1,0:T(8,128)(2,1)S(1)}, u32[]{:S(2)}, u32[]{:S(2)}) collective-permute-start(bf16[16,32,256]{2,1,0:T(8,128)(2,1)S(1)} %collective-permute-done.refs_2_.refs_0_), channel_id=1, source_target_pairs={{0,4},{4,8},{8,12},{12,14},{14,10},{10,6},{6,2},{2,0},{5,1},{9,5},... | collective-permute-start | bytes 786440 | tf_op jit(solution)/shard_map/ppermute | solution.py:286
  8.3 6.4 %collective-permute-start.3 = (bf16[16,32,256]{2,1,0:T(8,128)(2,1)S(1)}, bf16[16,32,256]{2,1,0:T(8,128)(2,1)S(1)}, u32[]{:S(2)}, u32[]{:S(2)}) collective-permute-start(bf16[16,32,256]{2,1,0:T(8,128)(2,1)S(1)} %collective-permute-done.1.refs_0_.refs_1_), channel_id=1, source_target_pairs={{0,4},{4,8},{8,12},{12,14},{14,10},{10,6},{6,2},{2,0},{5,1},{9,5},... | collective-permute-start | bytes 786440 | tf_op jit(solution)/shard_map/ppermute | solution.py:286
  11.2 13.2 %collective-permute-start.5 = (bf16[3,16,32,256]{3,2,1,0:T(8,128)(2,1)S(1)}, bf16[3,16,32,256]{3,2,1,0:T(8,128)(2,1)S(1)}, u32[]{:S(2)}, u32[]{:S(2)}) collective-permute-start(bf16[3,16,32,256]{3,2,1,0:T(8,128)(2,1)S(1)} %stack.4), channel_id=1, source_target_pairs={{0,1},{1,0},{2,3},{3,2},{4,5},{5,4},{6,7},{7,6},{8,9},{9,8},{10,11... | collective-permute-start | bytes 2359304 | tf_op jit(solution)/shard_map/ppermute | solution.py:302
  11.2 6.4 %collective-permute-start.4 = (bf16[16,32,256]{2,1,0:T(8,128)(2,1)S(1)}, bf16[16,32,256]{2,1,0:T(8,128)(2,1)S(1)}, u32[]{:S(2)}, u32[]{:S(2)}) collective-permute-start(bf16[16,32,256]{2,1,0:T(8,128)(2,1)S(1)} %collective-permute-done.2.refs_1_.refs_2_), channel_id=1, source_target_pairs={{0,4},{4,8},{8,12},{12,14},{14,10},{10,6},{6,2},{2,0},{5,1},{9,5},... | collective-permute-start | bytes 786440 | tf_op jit(solution)/shard_map/ppermute | solution.py:286
  14.7 6.7 %collective-permute-start.8 = (bf16[16,32,256]{2,1,0:T(8,128)(2,1)S(1)}, bf16[16,32,256]{2,1,0:T(8,128)(2,1)S(1)}, u32[]{:S(2)}, u32[]{:S(2)}) collective-permute-start(bf16[16,32,256]{2,1,0:T(8,128)(2,1)S(1)} %collective-permute-done.3.refs_3_.refs_0_), channel_id=1, source_target_pairs={{0,4},{4,8},{8,12},{12,14},{14,10},{10,6},{6,2},{2,0},{5,1},{9,5},... | collective-permute-start | bytes 786440 | tf_op jit(solution)/shard_map/ppermute | solution.py:286
  17.7 6.5 %collective-permute-start.9 = (bf16[16,32,256]{2,1,0:T(8,128)(2,1)S(1)}, bf16[16,32,256]{2,1,0:T(8,128)(2,1)S(1)}, u32[]{:S(2)}, u32[]{:S(2)}) collective-permute-start(bf16[16,32,256]{2,1,0:T(8,128)(2,1)S(1)} %collective-permute-done.4.refs_4_.refs_1_), channel_id=1, source_target_pairs={{0,4},{4,8},{8,12},{12,14},{14,10},{10,6},{6,2},{2,0},{5,1},{9,5},... | collective-permute-start | bytes 786440 | tf_op jit(solution)/shard_map/ppermute | solution.py:286
  19.8 4.4 %collective-permute-start.6 = (bf16[160,256]{1,0:T(8,128)(2,1)S(1)}, bf16[160,256]{1,0:T(8,128)(2,1)S(1)}, u32[]{:S(2)}, u32[]{:S(2)}) collective-permute-start(bf16[160,256]{1,0:T(8,128)(2,1)S(1)} %early_row.1), channel_id=1, source_target_pairs={{0,16},{16,0},{1,17},{17,1},{2,18},{18,2},{3,19},{19,3},{4,20},{20... | collective-permute-start | bytes 245768 | tf_op jit(solution)/shard_map/ppermute | solution.py:291
  21.3 6.6 %collective-permute-start.7 = (bf16[2,16,32,256]{3,2,1,0:T(8,128)(2,1)S(1)}, bf16[2,16,32,256]{3,2,1,0:T(8,128)(2,1)S(1)}, u32[]{:S(2)}, u32[]{:S(2)}) collective-permute-start(bf16[2,16,32,256]{3,2,1,0:T(8,128)(2,1)S(1)} %stack.5), channel_id=1, source_target_pairs={{0,1},{1,0},{2,3},{3,2},{4,5},{5,4},{6,7},{7,6},{8,9},{9,8},{10,11... | collective-permute-start | bytes 1572872 | tf_op jit(solution)/shard_map/ppermute | solution.py:302
  21.4 6.4 %collective-permute-start.12 = (bf16[16,32,256]{2,1,0:T(8,128)(2,1)S(1)}, bf16[16,32,256]{2,1,0:T(8,128)(2,1)S(1)}, u32[]{:S(2)}, u32[]{:S(2)}) collective-permute-start(bf16[16,32,256]{2,1,0:T(8,128)(2,1)S(1)} %collective-permute-done.8.refs_2_.refs_0_.refs_1_), channel_id=1, source_target_pairs={{0,4},{4,8},{8,12},{12,14},{14,10},{10,6},{6,2},{2,0},{5,1},{9,5},... | collective-permute-start | bytes 786440 | tf_op jit(solution)/shard_map/ppermute | solution.py:286
  24.2 5.4 %collective-permute-start.11 = (bf16[2,16,32,256]{3,2,1,0:T(8,128)(2,1)S(1)}, bf16[2,16,32,256]{3,2,1,0:T(8,128)(2,1)S(1)}, u32[]{:S(2)}, u32[]{:S(2)}) collective-permute-start(bf16[2,16,32,256]{3,2,1,0:T(8,128)(2,1)S(1)} %stack.6), channel_id=1, source_target_pairs={{0,1},{1,0},{2,3},{3,2},{4,5},{5,4},{6,7},{7,6},{8,9},{9,8},{10,11... | collective-permute-start | bytes 1572872 | tf_op jit(solution)/shard_map/ppermute | solution.py:302
  27.8 3.2 %copy-start.1 = (f32[2,256]{1,0:T(2,128)S(1)}, f32[2,256]{1,0:T(2,128)}, u32[]{:S(2)}) copy-start(f32[2,256]{1,0:T(2,128)} %virt_ref.3) | copy-start | bytes 6148
  27.8 3.2 %copy-start.2 = (f32[2,16]{1,0:T(2,128)S(1)}, f32[2,16]{1,0:T(2,128)}, u32[]{:S(2)}) copy-start(f32[2,16]{1,0:T(2,128)} %occ_ref.3) | copy-start | bytes 388
  27.8 1.8 %collective-permute-start.13 = (bf16[1,16,32,256]{3,2,1,0:T(8,128)(2,1)S(1)}, bf16[1,16,32,256]{3,2,1,0:T(8,128)(2,1)S(1)}, u32[]{:S(2)}, u32[]{:S(2)}) collective-permute-start(bf16[1,16,32,256]{3,2,1,0:T(8,128)(2,1)S(1)} %stack.7), channel_id=1, source_target_pairs={{0,1},{1,0},{2,3},{3,2},{4,5},{5,4},{6,7},{7,6},{8,9},{9,8},{10,11... | collective-permute-start | bytes 786440 | tf_op jit(solution)/shard_map/ppermute | solution.py:302
  27.9 6.8 %collective-permute-start.10 = (bf16[224,256]{1,0:T(8,128)(2,1)S(1)}, bf16[224,256]{1,0:T(8,128)(2,1)S(1)}, u32[]{:S(2)}, u32[]{:S(2)}) collective-permute-start(bf16[224,256]{1,0:T(8,128)(2,1)S(1)} %late_row.2), channel_id=1, source_target_pairs={{0,16},{16,0},{1,17},{17,1},{2,18},{18,2},{3,19},{19,3},{4,20},{20... | collective-permute-start | bytes 344072 | tf_op jit(solution)/shard_map/ppermute | solution.py:309
  29.6 5.3 %collective-permute-start.14 = (bf16[128,256]{1,0:T(8,128)(2,1)S(1)}, bf16[128,256]{1,0:T(8,128)(2,1)S(1)}, u32[]{:S(2)}, u32[]{:S(2)}) collective-permute-start(bf16[128,256]{1,0:T(8,128)(2,1)S(1)} %late_row.3), channel_id=1, source_target_pairs={{0,16},{16,0},{1,17},{17,1},{2,18},{18,2},{3,19},{19,3},{4,20},{20... | collective-permute-start | bytes 196616 | tf_op jit(solution)/shard_map/ppermute | solution.py:309
  37.5 1.4 %collective-permute-start.15 = (f32[2,2,32,256]{3,2,1,0:T(8,128)S(1)}, f32[2,2,32,256]{3,2,1,0:T(8,128)S(1)}, u32[]{:S(2)}, u32[]{:S(2)}) collective-permute-start(f32[2,2,32,256]{3,2,1,0:T(8,128)S(1)} %get-tuple-element.23), channel_id=1, source_target_pairs={{0,1},{1,0},{2,3},{3,2},{4,5},{5,4},{6,7},{7,6},{8,9},{9,8},{10,11... | collective-permute-start | bytes 393224 | tf_op jit(solution)/shard_map/ppermute | solution.py:332
  38.9 5.2 %collective-permute-start.16 = (f32[2,32,256]{2,1,0:T(8,128)S(1)}, f32[2,32,256]{2,1,0:T(8,128)S(1)}, u32[]{:S(2)}, u32[]{:S(2)}) collective-permute-start(f32[2,32,256]{2,1,0:T(8,128)S(1)} %get-tuple-element.25), channel_id=1, source_target_pairs={{0,6},{1,3},{2,4},{3,1},{4,2},{5,7},{6,0},{7,5},{8,14},{9,11},{10,... | collective-permute-start | bytes 196616 | tf_op jit(solution)/shard_map/ppermute | solution.py:337
  41.6 2.5 %collective-permute-start.17 = (f32[2,32,256]{2,1,0:T(8,128)S(1)}, f32[2,32,256]{2,1,0:T(8,128)S(1)}, u32[]{:S(2)}, u32[]{:S(2)}) collective-permute-start(f32[2,32,256]{2,1,0:T(8,128)S(1)} %get-tuple-element.26), channel_id=1, source_target_pairs={{0,0},{1,5},{2,2},{3,7},{4,4},{5,1},{6,6},{7,3},{8,8},{9,13},{10,1... | collective-permute-start | bytes 196616 | tf_op jit(solution)/shard_map/ppermute | solution.py:338
  42.3 8.8 %collective-permute-start.20 = (bf16[256,512]{1,0:T(8,128)(2,1)S(1)}, bf16[256,512]{1,0:T(8,128)(2,1)S(1)}, u32[]{:S(2)}, u32[]{:S(2)}) collective-permute-start(bf16[256,512]{1,0:T(8,128)(2,1)S(1)} %gamma_other.1.refs_0_), channel_id=1, source_target_pairs={{0,16},{16,0},{1,17},{17,1},{2,18},{18,2},{3,19},{19,3},{4,20},{20... | collective-permute-start | bytes 786440 | tf_op jit(solution)/shard_map/ppermute | solution.py:331
  44.2 4.9 %collective-permute-start.18 = (f32[32,256]{1,0:T(8,128)S(1)}, f32[32,256]{1,0:T(8,128)S(1)}, u32[]{:S(2)}, u32[]{:S(2)}) collective-permute-start(f32[32,256]{1,0:T(8,128)S(1)} %get-tuple-element.28), channel_id=1, source_target_pairs={{0,8},{1,9},{2,10},{3,11},{4,12},{5,13},{6,14},{7,15},{8,0},{9,1},... | collective-permute-start | bytes 98312 | tf_op jit(solution)/shard_map/ppermute | solution.py:342
  49.1 2.1 %collective-permute-start.19 = (f32[16,256]{1,0:T(8,128)S(1)}, f32[16,256]{1,0:T(8,128)S(1)}, u32[]{:S(2)}, u32[]{:S(2)}) collective-permute-start(f32[16,256]{1,0:T(8,128)S(1)} %get-tuple-element.31), channel_id=1, source_target_pairs={{0,1},{1,0},{2,3},{3,2},{4,5},{5,4},{6,7},{7,6},{8,9},{9,8},{10,11... | collective-permute-start | bytes 49160 | tf_op jit(solution)/shard_map/ppermute | solution.py:346

commit v7 on v6

--- a/solution.py
+++ b/solution.py
@@ -10,7 +10,7 @@
 
 VMEM_LIMIT = 20 * 1024 * 1024
 GROUP = 4
-PIECES = 1
+PIECES = 2
 NN = (((1,), (0,)), ((), ()))
 NT = (((1,), (1,)), ((), ()))
 TN = (((0,), (0,)), ((), ()))
@@ -303,7 +303,7 @@
         if step >= steps - 2:
             slices += swapped
             swapped = []
-    rows_sent, cut = [early_row], sent + 4
+    rows_sent, cut = [early_row], sent + 3
     for part in (slices[sent:cut], slices[cut:]):
         (row,) = vmem_call(row_kernel, "late_row", part, [((depth(part), nv), half)])
         rows_sent.append(lax.ppermute(row, "spin", across))
@@ -326,7 +326,7 @@
         flops=pair * naux,
     )
     (gamma_same,) = vmem_call(
-        gamma_kernel, "gamma_same", [amp_same, fitted], [((nv, naux), full)], flops=2 * pair * naux
+        gamma_kernel, "gamma_same", [amp_same, fitted], [((nv, naux), full)], flops=3 * pair * naux
     )
     returned = [lax.ppermute(piece, "spin", across) for piece in gamma_other]
     arrived = lax.ppermute(sent, "orb", swap)

time: 52.1 us -> 52.1 us (level)
    ppermute x2, waiting for transfers between devices: 0.89 us -> 0.32 us  [local_in_vmem(): arrived = lax.ppermute(sent, 'orb', swap)]
    ppermute x1 -> x2, waiting for transfers between devices: 0.01 us -> 0.57 us  [local_in_vmem(): returned = [lax.ppermute(piece, 'spin', across) for piece in gamma_other]]
    ppermute x1 -> x2, starting transfers between devices: 1.55 us -> 2.09 us  [local_in_vmem(): returned = [lax.ppermute(piece, 'spin', across) for piece in gamma_other]]
  transfers between devices with their start and end apart: 21 -> 22, of which waited for: 11 -> 11; matrix products, arithmetic and copies ran while one was open for 0% -> 0% of each run, Pallas kernels for 15% -> 15%
where the time goes in v7:
time: 52.1 us; the launch traced here: 51.9 us
  starting transfers between devices  29 us (56%)
  Pallas kernels  11.1 us (21%)
  waiting for transfers between devices  11 us (21%)
  between operations  0.81 us (2%)
    ppermute x7, starting transfers between devices, local_in_vmem(): lax.ppermute(lane, 'orb', moves)  14.4 us
    pallas_call x16, Pallas kernels, vmem_call(): pl.pallas_call(kernel, in_specs=[hbm] * in_hbm + [vmem] * (len(operands)...  11.1 us
    ppermute x7, waiting for transfers between devices, local_in_vmem(): lax.ppermute(lane, 'orb', moves)  7.9 us
    ppermute x2, starting transfers between devices, local_in_vmem(): rows_sent.append(lax.ppermute(row, 'spin', across))  3.09 us
    ppermute x1, starting transfers between devices, local_in_vmem(): one = lax.ppermute(one, 'orb', chip_moves(3, 1))  2.73 us
    ppermute x1, starting transfers between devices, local_in_vmem(): lax.ppermute(sent, 'orb', chip_moves(orb_count // 4, orb_count // 4))  2.66 us
    ppermute x2, starting transfers between devices, local_in_vmem(): returned = [lax.ppermute(piece, 'spin', across) for piece in gamma_other]  2.09 us
    ppermute x1, starting transfers between devices, local_in_vmem(): early_row = lax.ppermute(row, 'spin', across)  1.49 us
  transfers between devices with their start and end apart: 22, of which 11 were waited for; matrix products, arithmetic and copies ran while one was open for 0% of the time, Pallas kernels for 15%

profile of v7, /device:TPU:0, one launch (start us, length us, event | category | flops | bytes accessed | tf_op | source)
XLA Modules:
  0.0 51.9 jit_solution(5518399646378434894)
XLA Ops:
  0.6 0.0 copy-start
  0.6 0.5 collective-permute-start
  1.2 2.6 %collective-permute-start.1 = (bf16[16,32,256]{2,1,0:T(8,128)(2,1)}, bf16[16,32,256]{2,1,0:T(8,128)(2,1)S(1)}, u32[]{:S(2)}, u32[]{:S(2)}) collective-permute-start(bf16[16,32,256]{2,1,0:T(8,128)(2,1)} %bitcast.6), channel_id=1, source_target_pairs={{0,4},{4,8},{8,12},{12,14},{14,10},{10,6},{6,2},{2,0},{5,1},{9,5},... | collective-permute-start | bytes 786440 | tf_op jit(solution)/shard_map/ppermute | solution.py:286
  3.8 0.0 collective-permute-done.refs_2_.refs_0_
  3.8 1.7 %collective-permute-start.2 = (bf16[16,32,256]{2,1,0:T(8,128)(2,1)S(1)}, bf16[16,32,256]{2,1,0:T(8,128)(2,1)S(1)}, u32[]{:S(2)}, u32[]{:S(2)}) collective-permute-start(bf16[16,32,256]{2,1,0:T(8,128)(2,1)S(1)} %collective-permute-done.refs_2_.refs_0_), channel_id=1, source_target_pairs={{0,4},{4,8},{8,12},{12,14},{14,10},{10,6},{6,2},{2,0},{5,1},{9,5},... | collective-permute-start | bytes 786440 | tf_op jit(solution)/shard_map/ppermute | solution.py:286
  5.5 2.8 %collective-permute-done.1.refs_0_.refs_1_ = bf16[16,32,256]{2,1,0:T(8,128)(2,1)S(1)} collective-permute-done((bf16[16,32,256]{2,1,0:T(8,128)(2,1)}, bf16[16,32,256]{2,1,0:T(8,128)(2,1)S(1)}, u32[]{:S(2)}, u32[]{:S(2)}) %collective-permute-start.1) | collective-permute-done | bytes 262176 | tf_op jit(solution)/shard_map/ppermute | solution.py:286
  8.3 2.1 %collective-permute-start.3 = (bf16[16,32,256]{2,1,0:T(8,128)(2,1)S(1)}, bf16[16,32,256]{2,1,0:T(8,128)(2,1)S(1)}, u32[]{:S(2)}, u32[]{:S(2)}) collective-permute-start(bf16[16,32,256]{2,1,0:T(8,128)(2,1)S(1)} %collective-permute-done.1.refs_0_.refs_1_), channel_id=1, source_target_pairs={{0,4},{4,8},{8,12},{12,14},{14,10},{10,6},{6,2},{2,0},{5,1},{9,5},... | collective-permute-start | bytes 786440 | tf_op jit(solution)/shard_map/ppermute | solution.py:286
  10.4 0.7 %collective-permute-done.2.refs_1_.refs_2_ = bf16[16,32,256]{2,1,0:T(8,128)(2,1)S(1)} collective-permute-done((bf16[16,32,256]{2,1,0:T(8,128)(2,1)S(1)}, bf16[16,32,256]{2,1,0:T(8,128)(2,1)S(1)}, u32[]{:S(2)}, u32[]{:S(2)}) %collective-permute-start.2) | collective-permute-done | bytes 262176 | tf_op jit(solution)/shard_map/ppermute | solution.py:286
  11.1 0.1 stack.4
  11.2 0.1 collective-permute-start.5
  11.2 2.1 %collective-permute-start.4 = (bf16[16,32,256]{2,1,0:T(8,128)(2,1)S(1)}, bf16[16,32,256]{2,1,0:T(8,128)(2,1)S(1)}, u32[]{:S(2)}, u32[]{:S(2)}) collective-permute-start(bf16[16,32,256]{2,1,0:T(8,128)(2,1)S(1)} %collective-permute-done.2.refs_1_.refs_2_), channel_id=1, source_target_pairs={{0,4},{4,8},{8,12},{12,14},{14,10},{10,6},{6,2},{2,0},{5,1},{9,5},... | collective-permute-start | bytes 786440 | tf_op jit(solution)/shard_map/ppermute | solution.py:286
  13.4 1.3 %collective-permute-done.3.refs_3_.refs_0_ = bf16[16,32,256]{2,1,0:T(8,128)(2,1)S(1)} collective-permute-done((bf16[16,32,256]{2,1,0:T(8,128)(2,1)S(1)}, bf16[16,32,256]{2,1,0:T(8,128)(2,1)S(1)}, u32[]{:S(2)}, u32[]{:S(2)}) %collective-permute-start.3) | collective-permute-done | bytes 262176 | tf_op jit(solution)/shard_map/ppermute | solution.py:286
  14.7 2.1 %collective-permute-start.8 = (bf16[16,32,256]{2,1,0:T(8,128)(2,1)S(1)}, bf16[16,32,256]{2,1,0:T(8,128)(2,1)S(1)}, u32[]{:S(2)}, u32[]{:S(2)}) collective-permute-start(bf16[16,32,256]{2,1,0:T(8,128)(2,1)S(1)} %collective-permute-done.3.refs_3_.refs_0_), channel_id=1, source_target_pairs={{0,4},{4,8},{8,12},{12,14},{14,10},{10,6},{6,2},{2,0},{5,1},{9,5},... | collective-permute-start | bytes 786440 | tf_op jit(solution)/shard_map/ppermute | solution.py:286
  16.7 0.9 %collective-permute-done.4.refs_4_.refs_1_ = bf16[16,32,256]{2,1,0:T(8,128)(2,1)S(1)} collective-permute-done((bf16[16,32,256]{2,1,0:T(8,128)(2,1)S(1)}, bf16[16,32,256]{2,1,0:T(8,128)(2,1)S(1)}, u32[]{:S(2)}, u32[]{:S(2)}) %collective-permute-start.4) | collective-permute-done | bytes 262176 | tf_op jit(solution)/shard_map/ppermute | solution.py:286
  17.7 2.1 %collective-permute-start.10 = (bf16[16,32,256]{2,1,0:T(8,128)(2,1)S(1)}, bf16[16,32,256]{2,1,0:T(8,128)(2,1)S(1)}, u32[]{:S(2)}, u32[]{:S(2)}) collective-permute-start(bf16[16,32,256]{2,1,0:T(8,128)(2,1)S(1)} %collective-permute-done.4.refs_4_.refs_1_), channel_id=1, source_target_pairs={{0,4},{4,8},{8,12},{12,14},{14,10},{10,6},{6,2},{2,0},{5,1},{9,5},... | collective-permute-start | bytes 786440 | tf_op jit(solution)/shard_map/ppermute | solution.py:286
  19.8 1.5 %collective-permute-start.6 = (bf16[160,256]{1,0:T(8,128)(2,1)S(1)}, bf16[160,256]{1,0:T(8,128)(2,1)S(1)}, u32[]{:S(2)}, u32[]{:S(2)}) collective-permute-start(bf16[160,256]{1,0:T(8,128)(2,1)S(1)} %early_row.1), channel_id=1, source_target_pairs={{0,16},{16,0},{1,17},{17,1},{2,18},{18,2},{3,19},{19,3},{4,20},{20... | collective-permute-start | bytes 245768 | tf_op jit(solution)/shard_map/ppermute | solution.py:291
  21.3 0.1 collective-permute-start.7
  21.4 0.0 collective-permute-done.8.refs_2_.refs_0_.refs_1_
  21.4 1.8 %collective-permute-start.12 = (bf16[16,32,256]{2,1,0:T(8,128)(2,1)S(1)}, bf16[16,32,256]{2,1,0:T(8,128)(2,1)S(1)}, u32[]{:S(2)}, u32[]{:S(2)}) collective-permute-start(bf16[16,32,256]{2,1,0:T(8,128)(2,1)S(1)} %collective-permute-done.8.refs_2_.refs_0_.refs_1_), channel_id=1, source_target_pairs={{0,4},{4,8},{8,12},{12,14},{14,10},{10,6},{6,2},{2,0},{5,1},{9,5},... | collective-permute-start | bytes 786440 | tf_op jit(solution)/shard_map/ppermute | solution.py:286
  23.1 1.1 %collective-permute-done.6.refs_2_.early_ref = bf16[160,256]{1,0:T(8,128)(2,1)S(1)} collective-permute-done((bf16[160,256]{1,0:T(8,128)(2,1)S(1)}, bf16[160,256]{1,0:T(8,128)(2,1)S(1)}, u32[]{:S(2)}, u32[]{:S(2)}) %collective-permute-start.6) | collective-permute-done | bytes 81952 | tf_op jit(solution)/shard_map/ppermute | solution.py:291
  24.2 0.0 collective-permute-done.10.refs_1_.refs_0_.refs_2_
  24.2 0.1 collective-permute-start.11
  24.3 0.0 collective-permute-done.5.refs_5_.refs_0_
  24.3 0.0 copy-done
  24.3 1.3 %early_fit.1 = (bf16[512,512]{1,0:T(8,128)(2,1)S(1)}, f32[512,4096]{1,0:T(8,128)S(1)}) custom-call(bf16[512,512]{1,0:T(8,128)(2,1)S(1)} %copy-done, bf16[16,32,256]{2,1,0:T(8,128)(2,1)S(1)} %collective-permute-done.refs_2_.refs_0_, bf16[16,32,256]{2,1,0:T(8,128)(2,1)S(1)} %collective-permute-done.1.refs_0_.refs_1_, ...), custom_call_target="tpu_custom_call" | custom-call | tf_op jit(solution)/shard_map/early_fit/pallas_call | solution.py:258
  25.7 2.1 %collective-permute-done.12.refs_0_.refs_2_.refs_4_ = bf16[16,32,256]{2,1,0:T(8,128)(2,1)S(1)} collective-permute-done((bf16[16,32,256]{2,1,0:T(8,128)(2,1)S(1)}, bf16[16,32,256]{2,1,0:T(8,128)(2,1)S(1)}, u32[]{:S(2)}, u32[]{:S(2)}) %collective-permute-start.12) | collective-permute-done | bytes 262176 | tf_op jit(solution)/shard_map/ppermute | solution.py:286
  27.8 0.0 copy-start.1
  27.8 0.0 copy-start.2
  27.8 0.1 collective-permute-start.13
  27.9 0.0 collective-permute-done.7.refs_1_.refs_0_
  27.9 1.7 %collective-permute-start.9 = (bf16[192,256]{1,0:T(8,128)(2,1)S(1)}, bf16[192,256]{1,0:T(8,128)(2,1)S(1)}, u32[]{:S(2)}, u32[]{:S(2)}) collective-permute-start(bf16[192,256]{1,0:T(8,128)(2,1)S(1)} %late_row.2), channel_id=1, source_target_pairs={{0,16},{16,0},{1,17},{17,1},{2,18},{18,2},{3,19},{19,3},{4,20},{20... | collective-permute-start | bytes 294920 | tf_op jit(solution)/shard_map/ppermute | solution.py:309
  29.6 0.0 collective-permute-done.11.refs_1_.refs_3_
  29.6 0.0 collective-permute-done.13.refs_3_.refs_5_
  29.6 1.4 %collective-permute-start.14 = (bf16[160,256]{1,0:T(8,128)(2,1)S(1)}, bf16[160,256]{1,0:T(8,128)(2,1)S(1)}, u32[]{:S(2)}, u32[]{:S(2)}) collective-permute-start(bf16[160,256]{1,0:T(8,128)(2,1)S(1)} %late_row.3), channel_id=1, source_target_pairs={{0,16},{16,0},{1,17},{17,1},{2,18},{18,2},{3,19},{19,3},{4,20},{20... | collective-permute-start | bytes 245768 | tf_op jit(solution)/shard_map/ppermute | solution.py:309
  31.0 0.0 copy-done.1
  31.0 0.0 copy-done.2
  31.0 3.6 %fit_same.1 = (bf16[512,4096]{1,0:T(8,128)(2,1)S(1)}, bf16[256,4096]{1,0:T(8,128)(2,1)S(1)}, f32[256,256]{1,0:T(8,128)S(1)}) custom-call(f32[2,16]{1,0:T(2,128)S(1)} %copy-done.2, f32[2,256]{1,0:T(2,128)S(1)} %copy-done.1, bf16[512,512]{1,0:T(8,128)(2,1)S(1)} %get-tuple-element.20.factor_ref, f32[512,4096]{1,0:T(8,128)S(1)} %get-tuple-element.21.refs_1_.early_ref, ...), custom_call_target="tpu_custom_call" | custom-call | tf_op jit(solution)/shard_map/fit_same/pallas_call | solution.py:258
  34.7 0.0 collective-permute-done.9.late_ref
  34.7 0.2 collective-permute-done.14.last_ref
  34.9 2.5 %opposite.1 = (bf16[256,4096]{1,0:T(8,128)(2,1)S(1)}, f32[2,2,32,256]{3,2,1,0:T(8,128)S(1)}, f32[2,2,32,256]{3,2,1,0:T(8,128)S(1)}) custom-call(f32[2,16]{1,0:T(2,128)S(1)} %copy-done.2, f32[2,256]{1,0:T(2,128)S(1)} %copy-done.1, bf16[512,512]{1,0:T(8,128)(2,1)S(1)} %get-tuple-element.20.factor_ref, ...), custom_call_target="tpu_custom_call" | custom-call | flops 1610612736 | bytes 5245056 | tf_op jit(solution)/shard_map/opposite/pallas_call | solution.py:258
  37.5 0.1 collective-permute-start.15
  37.5 1.3 %gamma_other.1 = (bf16[128,512]{1,0:T(8,128)(2,1)S(1)}, bf16[128,512]{1,0:T(8,128)(2,1)S(1)}) custom-call(bf16[256,4096]{1,0:T(8,128)(2,1)S(1)} %get-tuple-element.26.amp_ref, bf16[512,4096]{1,0:T(8,128)(2,1)S(1)} %get-tuple-element.22.fitted_ref), custom_call_target="tpu_custom_call" | custom-call | flops 1073741824 | bytes 6291456 | tf_op jit(solution)/shard_map/gamma_other/pallas_call | solution.py:258
  38.8 0.1 collective-permute-done.15.arrived
  38.9 2.7 %collective-permute-start.16 = (f32[2,32,256]{2,1,0:T(8,128)S(1)}, f32[2,32,256]{2,1,0:T(8,128)S(1)}, u32[]{:S(2)}, u32[]{:S(2)}) collective-permute-start(f32[2,32,256]{2,1,0:T(8,128)S(1)} %get-tuple-element.29), channel_id=1, source_target_pairs={{0,6},{1,3},{2,4},{3,1},{4,2},{5,7},{6,0},{7,5},{8,14},{9,11},{10,... | collective-permute-start | bytes 196616 | tf_op jit(solution)/shard_map/ppermute | solution.py:337
  41.6 0.7 %collective-permute-start.17 = (f32[2,32,256]{2,1,0:T(8,128)S(1)}, f32[2,32,256]{2,1,0:T(8,128)S(1)}, u32[]{:S(2)}, u32[]{:S(2)}) collective-permute-start(f32[2,32,256]{2,1,0:T(8,128)S(1)} %get-tuple-element.30), channel_id=1, source_target_pairs={{0,0},{1,5},{2,2},{3,7},{4,4},{5,1},{6,6},{7,3},{8,8},{9,13},{10,1... | collective-permute-start | bytes 196616 | tf_op jit(solution)/shard_map/ppermute | solution.py:338
  42.3 1.6 %collective-permute-start.20 = (bf16[128,512]{1,0:T(8,128)(2,1)S(1)}, bf16[128,512]{1,0:T(8,128)(2,1)S(1)}, u32[]{:S(2)}, u32[]{:S(2)}) collective-permute-start(bf16[128,512]{1,0:T(8,128)(2,1)S(1)} %get-tuple-element.27.refs_0_), channel_id=1, source_target_pairs={{0,16},{16,0},{1,17},{17,1},{2,18},{18,2},{3,19},{19,3},{4,20},{20... | collective-permute-start | bytes 393224 | tf_op jit(solution)/shard_map/ppermute | solution.py:331
  43.9 0.5 %collective-permute-start.21 = (bf16[128,512]{1,0:T(8,128)(2,1)S(1)}, bf16[128,512]{1,0:T(8,128)(2,1)S(1)}, u32[]{:S(2)}, u32[]{:S(2)}) collective-permute-start(bf16[128,512]{1,0:T(8,128)(2,1)S(1)} %get-tuple-element.28.refs_1_), channel_id=1, source_target_pairs={{0,16},{16,0},{1,17},{17,1},{2,18},{18,2},{3,19},{19,3},{4,20},{20... | collective-permute-start | bytes 393224 | tf_op jit(solution)/shard_map/ppermute | solution.py:331
  44.4 0.0 collective-permute-done.16.one_in
  44.4 0.0 collective-permute-done.17.two_in
  44.4 2.7 %collective-permute-start.18 = (f32[32,256]{1,0:T(8,128)S(1)}, f32[32,256]{1,0:T(8,128)S(1)}, u32[]{:S(2)}, u32[]{:S(2)}) collective-permute-start(f32[32,256]{1,0:T(8,128)S(1)} %get-tuple-element.32), channel_id=1, source_target_pairs={{0,8},{1,9},{2,10},{3,11},{4,12},{5,13},{6,14},{7,15},{8,0},{9,1},... | collective-permute-start | bytes 98312 | tf_op jit(solution)/shard_map/ppermute | solution.py:342
  47.1 1.3 %gamma_same.1.refs_0_.gamma_in = f32[256,512]{1,0:T(8,128)S(1)} custom-call(bf16[256,4096]{1,0:T(8,128)(2,1)S(1)} %get-tuple-element.33.amp_ref, bf16[512,4096]{1,0:T(8,128)(2,1)S(1)} %get-tuple-element.22.fitted_ref), custom_call_target="tpu_custom_call" | custom-call | flops 3221225472 | bytes 6291456 | tf_op jit(solution)/shard_map/gamma_same/pallas_call | solution.py:258
  48.4 0.9 %collective-permute-done.18.arrived = f32[32,256]{1,0:T(8,128)S(1)} collective-permute-done((f32[32,256]{1,0:T(8,128)S(1)}, f32[32,256]{1,0:T(8,128)S(1)}, u32[]{:S(2)}, u32[]{:S(2)}) %collective-permute-start.18) | collective-permute-done | bytes 32800 | tf_op jit(solution)/shard_map/ppermute | solution.py:342
  49.3 1.0 %collective-permute-start.19 = (f32[16,256]{1,0:T(8,128)S(1)}, f32[16,256]{1,0:T(8,128)S(1)}, u32[]{:S(2)}, u32[]{:S(2)}) collective-permute-start(f32[16,256]{1,0:T(8,128)S(1)} %get-tuple-element.35), channel_id=1, source_target_pairs={{0,1},{1,0},{2,3},{3,2},{4,5},{5,4},{6,7},{7,6},{8,9},{9,8},{10,11... | collective-permute-start | bytes 49160 | tf_op jit(solution)/shard_map/ppermute | solution.py:346
  50.3 0.0 collective-permute-done.20.refs_0_
  50.3 0.6 %collective-permute-done.21.refs_1_ = bf16[128,512]{1,0:T(8,128)(2,1)S(1)} collective-permute-done((bf16[128,512]{1,0:T(8,128)(2,1)S(1)}, bf16[128,512]{1,0:T(8,128)(2,1)S(1)}, u32[]{:S(2)}, u32[]{:S(2)}) %collective-permute-start.21) | collective-permute-done | bytes 131104 | tf_op jit(solution)/shard_map/ppermute | solution.py:331
  50.8 0.3 collective-permute-done.19.arrived
  51.1 0.8 %finish.1 = (f32[256,512]{1,0:T(8,128)}, f32[1,16,256]{2,1,0:T(8,128)}) custom-call(f32[16,256]{1,0:T(8,128)S(1)} %get-tuple-element.34.kept_in, f32[16,256]{1,0:T(8,128)S(1)} %collective-permute-done.19.arrived, f32[256,512]{1,0:T(8,128)S(1)} %gamma_same.1.refs_0_.gamma_in, bf16[128,512]{1,0:T(8,128)(2,1)S(1)} %collective-permute-done.20.refs_0_, ...), custom_call_target="tpu_custom_call" | custom-call | tf_op jit(solution)/shard_map/finish/pallas_call | solution.py:258
  (9 shorter events, 0.2 us)
Async XLA Ops:
  0.6 23.7 %copy-start = (bf16[512,512]{1,0:T(8,128)(2,1)S(1)}, bf16[512,512]{1,0:T(8,128)(2,1)}, u32[]{:S(2)}) copy-start(bf16[512,512]{1,0:T(8,128)(2,1)} %given_ref.1) | copy-start | bytes 1572868
  0.6 3.2 %collective-permute-start = (bf16[16,32,256]{2,1,0:T(8,128)(2,1)}, bf16[16,32,256]{2,1,0:T(8,128)(2,1)S(1)}, u32[]{:S(2)}, u32[]{:S(2)}) collective-permute-start(bf16[16,32,256]{2,1,0:T(8,128)(2,1)} %bitcast.5), channel_id=1, source_target_pairs={{0,1},{1,0},{2,3},{3,2},{4,5},{5,4},{6,7},{7,6},{8,9},{9,8},{10,11... | collective-permute-start | bytes 786440 | tf_op jit(solution)/shard_map/ppermute | solution.py:282
  1.2 7.1 %collective-permute-start.1 = (bf16[16,32,256]{2,1,0:T(8,128)(2,1)}, bf16[16,32,256]{2,1,0:T(8,128)(2,1)S(1)}, u32[]{:S(2)}, u32[]{:S(2)}) collective-permute-start(bf16[16,32,256]{2,1,0:T(8,128)(2,1)} %bitcast.6), channel_id=1, source_target_pairs={{0,4},{4,8},{8,12},{12,14},{14,10},{10,6},{6,2},{2,0},{5,1},{9,5},... | collective-permute-start | bytes 786440 | tf_op jit(solution)/shard_map/ppermute | solution.py:286
  3.8 7.3 %collective-permute-start.2 = (bf16[16,32,256]{2,1,0:T(8,128)(2,1)S(1)}, bf16[16,32,256]{2,1,0:T(8,128)(2,1)S(1)}, u32[]{:S(2)}, u32[]{:S(2)}) collective-permute-start(bf16[16,32,256]{2,1,0:T(8,128)(2,1)S(1)} %collective-permute-done.refs_2_.refs_0_), channel_id=1, source_target_pairs={{0,4},{4,8},{8,12},{12,14},{14,10},{10,6},{6,2},{2,0},{5,1},{9,5},... | collective-permute-start | bytes 786440 | tf_op jit(solution)/shard_map/ppermute | solution.py:286
  8.3 6.4 %collective-permute-start.3 = (bf16[16,32,256]{2,1,0:T(8,128)(2,1)S(1)}, bf16[16,32,256]{2,1,0:T(8,128)(2,1)S(1)}, u32[]{:S(2)}, u32[]{:S(2)}) collective-permute-start(bf16[16,32,256]{2,1,0:T(8,128)(2,1)S(1)} %collective-permute-done.1.refs_0_.refs_1_), channel_id=1, source_target_pairs={{0,4},{4,8},{8,12},{12,14},{14,10},{10,6},{6,2},{2,0},{5,1},{9,5},... | collective-permute-start | bytes 786440 | tf_op jit(solution)/shard_map/ppermute | solution.py:286
  11.2 13.2 %collective-permute-start.5 = (bf16[3,16,32,256]{3,2,1,0:T(8,128)(2,1)S(1)}, bf16[3,16,32,256]{3,2,1,0:T(8,128)(2,1)S(1)}, u32[]{:S(2)}, u32[]{:S(2)}) collective-permute-start(bf16[3,16,32,256]{3,2,1,0:T(8,128)(2,1)S(1)} %stack.4), channel_id=1, source_target_pairs={{0,1},{1,0},{2,3},{3,2},{4,5},{5,4},{6,7},{7,6},{8,9},{9,8},{10,11... | collective-permute-start | bytes 2359304 | tf_op jit(solution)/shard_map/ppermute | solution.py:302
  11.2 6.4 %collective-permute-start.4 = (bf16[16,32,256]{2,1,0:T(8,128)(2,1)S(1)}, bf16[16,32,256]{2,1,0:T(8,128)(2,1)S(1)}, u32[]{:S(2)}, u32[]{:S(2)}) collective-permute-start(bf16[16,32,256]{2,1,0:T(8,128)(2,1)S(1)} %collective-permute-done.2.refs_1_.refs_2_), channel_id=1, source_target_pairs={{0,4},{4,8},{8,12},{12,14},{14,10},{10,6},{6,2},{2,0},{5,1},{9,5},... | collective-permute-start | bytes 786440 | tf_op jit(solution)/shard_map/ppermute | solution.py:286
  14.7 6.7 %collective-permute-start.8 = (bf16[16,32,256]{2,1,0:T(8,128)(2,1)S(1)}, bf16[16,32,256]{2,1,0:T(8,128)(2,1)S(1)}, u32[]{:S(2)}, u32[]{:S(2)}) collective-permute-start(bf16[16,32,256]{2,1,0:T(8,128)(2,1)S(1)} %collective-permute-done.3.refs_3_.refs_0_), channel_id=1, source_target_pairs={{0,4},{4,8},{8,12},{12,14},{14,10},{10,6},{6,2},{2,0},{5,1},{9,5},... | collective-permute-start | bytes 786440 | tf_op jit(solution)/shard_map/ppermute | solution.py:286
  17.7 6.5 %collective-permute-start.10 = (bf16[16,32,256]{2,1,0:T(8,128)(2,1)S(1)}, bf16[16,32,256]{2,1,0:T(8,128)(2,1)S(1)}, u32[]{:S(2)}, u32[]{:S(2)}) collective-permute-start(bf16[16,32,256]{2,1,0:T(8,128)(2,1)S(1)} %collective-permute-done.4.refs_4_.refs_1_), channel_id=1, source_target_pairs={{0,4},{4,8},{8,12},{12,14},{14,10},{10,6},{6,2},{2,0},{5,1},{9,5},... | collective-permute-start | bytes 786440 | tf_op jit(solution)/shard_map/ppermute | solution.py:286
  19.8 4.4 %collective-permute-start.6 = (bf16[160,256]{1,0:T(8,128)(2,1)S(1)}, bf16[160,256]{1,0:T(8,128)(2,1)S(1)}, u32[]{:S(2)}, u32[]{:S(2)}) collective-permute-start(bf16[160,256]{1,0:T(8,128)(2,1)S(1)} %early_row.1), channel_id=1, source_target_pairs={{0,16},{16,0},{1,17},{17,1},{2,18},{18,2},{3,19},{19,3},{4,20},{20... | collective-permute-start | bytes 245768 | tf_op jit(solution)/shard_map/ppermute | solution.py:291
  21.3 6.6 %collective-permute-start.7 = (bf16[2,16,32,256]{3,2,1,0:T(8,128)(2,1)S(1)}, bf16[2,16,32,256]{3,2,1,0:T(8,128)(2,1)S(1)}, u32[]{:S(2)}, u32[]{:S(2)}) collective-permute-start(bf16[2,16,32,256]{3,2,1,0:T(8,128)(2,1)S(1)} %stack.5), channel_id=1, source_target_pairs={{0,1},{1,0},{2,3},{3,2},{4,5},{5,4},{6,7},{7,6},{8,9},{9,8},{10,11... | collective-permute-start | bytes 1572872 | tf_op jit(solution)/shard_map/ppermute | solution.py:302
  21.4 6.4 %collective-permute-start.12 = (bf16[16,32,256]{2,1,0:T(8,128)(2,1)S(1)}, bf16[16,32,256]{2,1,0:T(8,128)(2,1)S(1)}, u32[]{:S(2)}, u32[]{:S(2)}) collective-permute-start(bf16[16,32,256]{2,1,0:T(8,128)(2,1)S(1)} %collective-permute-done.8.refs_2_.refs_0_.refs_1_), channel_id=1, source_target_pairs={{0,4},{4,8},{8,12},{12,14},{14,10},{10,6},{6,2},{2,0},{5,1},{9,5},... | collective-permute-start | bytes 786440 | tf_op jit(solution)/shard_map/ppermute | solution.py:286
  24.2 5.4 %collective-permute-start.11 = (bf16[2,16,32,256]{3,2,1,0:T(8,128)(2,1)S(1)}, bf16[2,16,32,256]{3,2,1,0:T(8,128)(2,1)S(1)}, u32[]{:S(2)}, u32[]{:S(2)}) collective-permute-start(bf16[2,16,32,256]{3,2,1,0:T(8,128)(2,1)S(1)} %stack.6), channel_id=1, source_target_pairs={{0,1},{1,0},{2,3},{3,2},{4,5},{5,4},{6,7},{7,6},{8,9},{9,8},{10,11... | collective-permute-start | bytes 1572872 | tf_op jit(solution)/shard_map/ppermute | solution.py:302
  27.8 3.3 %copy-start.1 = (f32[2,256]{1,0:T(2,128)S(1)}, f32[2,256]{1,0:T(2,128)}, u32[]{:S(2)}) copy-start(f32[2,256]{1,0:T(2,128)} %virt_ref.3) | copy-start | bytes 6148
  27.8 3.3 %copy-start.2 = (f32[2,16]{1,0:T(2,128)S(1)}, f32[2,16]{1,0:T(2,128)}, u32[]{:S(2)}) copy-start(f32[2,16]{1,0:T(2,128)} %occ_ref.3) | copy-start | bytes 388
  27.8 1.8 %collective-permute-start.13 = (bf16[1,16,32,256]{3,2,1,0:T(8,128)(2,1)S(1)}, bf16[1,16,32,256]{3,2,1,0:T(8,128)(2,1)S(1)}, u32[]{:S(2)}, u32[]{:S(2)}) collective-permute-start(bf16[1,16,32,256]{3,2,1,0:T(8,128)(2,1)S(1)} %stack.7), channel_id=1, source_target_pairs={{0,1},{1,0},{2,3},{3,2},{4,5},{5,4},{6,7},{7,6},{8,9},{9,8},{10,11... | collective-permute-start | bytes 786440 | tf_op jit(solution)/shard_map/ppermute | solution.py:302
  27.9 6.8 %collective-permute-start.9 = (bf16[192,256]{1,0:T(8,128)(2,1)S(1)}, bf16[192,256]{1,0:T(8,128)(2,1)S(1)}, u32[]{:S(2)}, u32[]{:S(2)}) collective-permute-start(bf16[192,256]{1,0:T(8,128)(2,1)S(1)} %late_row.2), channel_id=1, source_target_pairs={{0,16},{16,0},{1,17},{17,1},{2,18},{18,2},{3,19},{19,3},{4,20},{20... | collective-permute-start | bytes 294920 | tf_op jit(solution)/shard_map/ppermute | solution.py:309
  29.6 5.3 %collective-permute-start.14 = (bf16[160,256]{1,0:T(8,128)(2,1)S(1)}, bf16[160,256]{1,0:T(8,128)(2,1)S(1)}, u32[]{:S(2)}, u32[]{:S(2)}) collective-permute-start(bf16[160,256]{1,0:T(8,128)(2,1)S(1)} %late_row.3), channel_id=1, source_target_pairs={{0,16},{16,0},{1,17},{17,1},{2,18},{18,2},{3,19},{19,3},{4,20},{20... | collective-permute-start | bytes 245768 | tf_op jit(solution)/shard_map/ppermute | solution.py:309
  37.5 1.4 %collective-permute-start.15 = (f32[2,2,32,256]{3,2,1,0:T(8,128)S(1)}, f32[2,2,32,256]{3,2,1,0:T(8,128)S(1)}, u32[]{:S(2)}, u32[]{:S(2)}) collective-permute-start(f32[2,2,32,256]{3,2,1,0:T(8,128)S(1)} %get-tuple-element.25), channel_id=1, source_target_pairs={{0,1},{1,0},{2,3},{3,2},{4,5},{5,4},{6,7},{7,6},{8,9},{9,8},{10,11... | collective-permute-start | bytes 393224 | tf_op jit(solution)/shard_map/ppermute | solution.py:332
  38.9 5.5 %collective-permute-start.16 = (f32[2,32,256]{2,1,0:T(8,128)S(1)}, f32[2,32,256]{2,1,0:T(8,128)S(1)}, u32[]{:S(2)}, u32[]{:S(2)}) collective-permute-start(f32[2,32,256]{2,1,0:T(8,128)S(1)} %get-tuple-element.29), channel_id=1, source_target_pairs={{0,6},{1,3},{2,4},{3,1},{4,2},{5,7},{6,0},{7,5},{8,14},{9,11},{10,... | collective-permute-start | bytes 196616 | tf_op jit(solution)/shard_map/ppermute | solution.py:337
  41.6 2.8 %collective-permute-start.17 = (f32[2,32,256]{2,1,0:T(8,128)S(1)}, f32[2,32,256]{2,1,0:T(8,128)S(1)}, u32[]{:S(2)}, u32[]{:S(2)}) collective-permute-start(f32[2,32,256]{2,1,0:T(8,128)S(1)} %get-tuple-element.30), channel_id=1, source_target_pairs={{0,0},{1,5},{2,2},{3,7},{4,4},{5,1},{6,6},{7,3},{8,8},{9,13},{10,1... | collective-permute-start | bytes 196616 | tf_op jit(solution)/shard_map/ppermute | solution.py:338
  42.3 8.0 %collective-permute-start.20 = (bf16[128,512]{1,0:T(8,128)(2,1)S(1)}, bf16[128,512]{1,0:T(8,128)(2,1)S(1)}, u32[]{:S(2)}, u32[]{:S(2)}) collective-permute-start(bf16[128,512]{1,0:T(8,128)(2,1)S(1)} %get-tuple-element.27.refs_0_), channel_id=1, source_target_pairs={{0,16},{16,0},{1,17},{17,1},{2,18},{18,2},{3,19},{19,3},{4,20},{20... | collective-permute-start | bytes 393224 | tf_op jit(solution)/shard_map/ppermute | solution.py:331
  43.9 7.0 %collective-permute-start.21 = (bf16[128,512]{1,0:T(8,128)(2,1)S(1)}, bf16[128,512]{1,0:T(8,128)(2,1)S(1)}, u32[]{:S(2)}, u32[]{:S(2)}) collective-permute-start(bf16[128,512]{1,0:T(8,128)(2,1)S(1)} %get-tuple-element.28.refs_1_), channel_id=1, source_target_pairs={{0,16},{16,0},{1,17},{17,1},{2,18},{18,2},{3,19},{19,3},{4,20},{20... | collective-permute-start | bytes 393224 | tf_op jit(solution)/shard_map/ppermute | solution.py:331
  44.4 4.9 %collective-permute-start.18 = (f32[32,256]{1,0:T(8,128)S(1)}, f32[32,256]{1,0:T(8,128)S(1)}, u32[]{:S(2)}, u32[]{:S(2)}) collective-permute-start(f32[32,256]{1,0:T(8,128)S(1)} %get-tuple-element.32), channel_id=1, source_target_pairs={{0,8},{1,9},{2,10},{3,11},{4,12},{5,13},{6,14},{7,15},{8,0},{9,1},... | collective-permute-start | bytes 98312 | tf_op jit(solution)/shard_map/ppermute | solution.py:342
  49.3 1.8 %collective-permute-start.19 = (f32[16,256]{1,0:T(8,128)S(1)}, f32[16,256]{1,0:T(8,128)S(1)}, u32[]{:S(2)}, u32[]{:S(2)}) collective-permute-start(f32[16,256]{1,0:T(8,128)S(1)} %get-tuple-element.35), channel_id=1, source_target_pairs={{0,1},{1,0},{2,3},{3,2},{4,5},{5,4},{6,7},{7,6},{8,9},{9,8},{10,11... | collective-permute-start | bytes 49160 | tf_op jit(solution)/shard_map/ppermute | solution.py:346

commit v8 on v6

--- a/solution.py
+++ b/solution.py
@@ -128,7 +128,10 @@
 
 
 def amplitudes(coupling, occupied_pair, virtual_pair):
-    return (coupling / (occupied_pair - virtual_pair)).astype(jnp.bfloat16)
+    denominator = occupied_pair - virtual_pair
+    inverse = pltpu.reciprocal(denominator, approx=True)
+    inverse = inverse * (2.0 - denominator * inverse)
+    return (coupling * inverse).astype(jnp.bfloat16)
 
 
 def early_fit_kernel(orb_count, given_ref, *refs):

time: 52.1 us -> 52.4 us (level)
  no operation moved by 1% of the time
where the time goes in v8:
time: 52.4 us; the launch traced here: 52.2 us
  starting transfers between devices  28.8 us (55%)
  Pallas kernels  11.5 us (22%)
  waiting for transfers between devices  11.1 us (21%)
  between operations  0.81 us (2%)
    ppermute x7, starting transfers between devices, local_in_vmem(): lax.ppermute(lane, 'orb', moves)  14.4 us
    pallas_call x16, Pallas kernels, vmem_call(): pl.pallas_call(kernel, in_specs=[hbm] * in_hbm + [vmem] * (len(operands)...  11.5 us
    ppermute x7, waiting for transfers between devices, local_in_vmem(): lax.ppermute(lane, 'orb', moves)  7.9 us
    ppermute x2, starting transfers between devices, local_in_vmem(): rows_sent.append(lax.ppermute(row, 'spin', across))  3.09 us
    ppermute x1, starting transfers between devices, local_in_vmem(): lax.ppermute(sent, 'orb', chip_moves(orb_count // 4, orb_count // 4))  2.78 us
    ppermute x1, starting transfers between devices, local_in_vmem(): one = lax.ppermute(one, 'orb', chip_moves(3, 1))  2.73 us
    ppermute x1, starting transfers between devices, local_in_vmem(): returned = [lax.ppermute(piece, 'spin', across) for piece in gamma_other]  1.54 us
    ppermute x1, starting transfers between devices, local_in_vmem(): early_row = lax.ppermute(row, 'spin', across)  1.49 us
  transfers between devices with their start and end apart: 21, of which 11 were waited for; matrix products, arithmetic and copies ran while one was open for 0% of the time, Pallas kernels for 15%

profile of v8, /device:TPU:0, one launch (start us, length us, event | category | flops | bytes accessed | tf_op | source)
XLA Modules:
  0.0 52.2 jit_solution(6323272861279874511)
XLA Ops:
  0.6 0.0 copy-start
  0.6 0.5 collective-permute-start
  1.2 2.6 %collective-permute-start.1 = (bf16[16,32,256]{2,1,0:T(8,128)(2,1)}, bf16[16,32,256]{2,1,0:T(8,128)(2,1)S(1)}, u32[]{:S(2)}, u32[]{:S(2)}) collective-permute-start(bf16[16,32,256]{2,1,0:T(8,128)(2,1)} %bitcast.6), channel_id=1, source_target_pairs={{0,4},{4,8},{8,12},{12,14},{14,10},{10,6},{6,2},{2,0},{5,1},{9,5},... | collective-permute-start | bytes 786440 | tf_op jit(solution)/shard_map/ppermute | solution.py:289
  3.8 0.0 collective-permute-done.refs_2_.refs_0_
  3.8 1.7 %collective-permute-start.2 = (bf16[16,32,256]{2,1,0:T(8,128)(2,1)S(1)}, bf16[16,32,256]{2,1,0:T(8,128)(2,1)S(1)}, u32[]{:S(2)}, u32[]{:S(2)}) collective-permute-start(bf16[16,32,256]{2,1,0:T(8,128)(2,1)S(1)} %collective-permute-done.refs_2_.refs_0_), channel_id=1, source_target_pairs={{0,4},{4,8},{8,12},{12,14},{14,10},{10,6},{6,2},{2,0},{5,1},{9,5},... | collective-permute-start | bytes 786440 | tf_op jit(solution)/shard_map/ppermute | solution.py:289
  5.5 2.8 %collective-permute-done.1.refs_0_.refs_1_ = bf16[16,32,256]{2,1,0:T(8,128)(2,1)S(1)} collective-permute-done((bf16[16,32,256]{2,1,0:T(8,128)(2,1)}, bf16[16,32,256]{2,1,0:T(8,128)(2,1)S(1)}, u32[]{:S(2)}, u32[]{:S(2)}) %collective-permute-start.1) | collective-permute-done | bytes 262176 | tf_op jit(solution)/shard_map/ppermute | solution.py:289
  8.3 2.1 %collective-permute-start.3 = (bf16[16,32,256]{2,1,0:T(8,128)(2,1)S(1)}, bf16[16,32,256]{2,1,0:T(8,128)(2,1)S(1)}, u32[]{:S(2)}, u32[]{:S(2)}) collective-permute-start(bf16[16,32,256]{2,1,0:T(8,128)(2,1)S(1)} %collective-permute-done.1.refs_0_.refs_1_), channel_id=1, source_target_pairs={{0,4},{4,8},{8,12},{12,14},{14,10},{10,6},{6,2},{2,0},{5,1},{9,5},... | collective-permute-start | bytes 786440 | tf_op jit(solution)/shard_map/ppermute | solution.py:289
  10.4 0.7 %collective-permute-done.2.refs_1_.refs_2_ = bf16[16,32,256]{2,1,0:T(8,128)(2,1)S(1)} collective-permute-done((bf16[16,32,256]{2,1,0:T(8,128)(2,1)S(1)}, bf16[16,32,256]{2,1,0:T(8,128)(2,1)S(1)}, u32[]{:S(2)}, u32[]{:S(2)}) %collective-permute-start.2) | collective-permute-done | bytes 262176 | tf_op jit(solution)/shard_map/ppermute | solution.py:289
  11.1 0.1 stack.4
  11.2 0.1 collective-permute-start.5
  11.2 2.1 %collective-permute-start.4 = (bf16[16,32,256]{2,1,0:T(8,128)(2,1)S(1)}, bf16[16,32,256]{2,1,0:T(8,128)(2,1)S(1)}, u32[]{:S(2)}, u32[]{:S(2)}) collective-permute-start(bf16[16,32,256]{2,1,0:T(8,128)(2,1)S(1)} %collective-permute-done.2.refs_1_.refs_2_), channel_id=1, source_target_pairs={{0,4},{4,8},{8,12},{12,14},{14,10},{10,6},{6,2},{2,0},{5,1},{9,5},... | collective-permute-start | bytes 786440 | tf_op jit(solution)/shard_map/ppermute | solution.py:289
  13.4 1.3 %collective-permute-done.3.refs_3_.refs_0_ = bf16[16,32,256]{2,1,0:T(8,128)(2,1)S(1)} collective-permute-done((bf16[16,32,256]{2,1,0:T(8,128)(2,1)S(1)}, bf16[16,32,256]{2,1,0:T(8,128)(2,1)S(1)}, u32[]{:S(2)}, u32[]{:S(2)}) %collective-permute-start.3) | collective-permute-done | bytes 262176 | tf_op jit(solution)/shard_map/ppermute | solution.py:289
  14.7 2.1 %collective-permute-start.8 = (bf16[16,32,256]{2,1,0:T(8,128)(2,1)S(1)}, bf16[16,32,256]{2,1,0:T(8,128)(2,1)S(1)}, u32[]{:S(2)}, u32[]{:S(2)}) collective-permute-start(bf16[16,32,256]{2,1,0:T(8,128)(2,1)S(1)} %collective-permute-done.3.refs_3_.refs_0_), channel_id=1, source_target_pairs={{0,4},{4,8},{8,12},{12,14},{14,10},{10,6},{6,2},{2,0},{5,1},{9,5},... | collective-permute-start | bytes 786440 | tf_op jit(solution)/shard_map/ppermute | solution.py:289
  16.7 0.9 %collective-permute-done.4.refs_4_.refs_1_ = bf16[16,32,256]{2,1,0:T(8,128)(2,1)S(1)} collective-permute-done((bf16[16,32,256]{2,1,0:T(8,128)(2,1)S(1)}, bf16[16,32,256]{2,1,0:T(8,128)(2,1)S(1)}, u32[]{:S(2)}, u32[]{:S(2)}) %collective-permute-start.4) | collective-permute-done | bytes 262176 | tf_op jit(solution)/shard_map/ppermute | solution.py:289
  17.7 2.1 %collective-permute-start.9 = (bf16[16,32,256]{2,1,0:T(8,128)(2,1)S(1)}, bf16[16,32,256]{2,1,0:T(8,128)(2,1)S(1)}, u32[]{:S(2)}, u32[]{:S(2)}) collective-permute-start(bf16[16,32,256]{2,1,0:T(8,128)(2,1)S(1)} %collective-permute-done.4.refs_4_.refs_1_), channel_id=1, source_target_pairs={{0,4},{4,8},{8,12},{12,14},{14,10},{10,6},{6,2},{2,0},{5,1},{9,5},... | collective-permute-start | bytes 786440 | tf_op jit(solution)/shard_map/ppermute | solution.py:289
  19.8 1.5 %collective-permute-start.6 = (bf16[160,256]{1,0:T(8,128)(2,1)S(1)}, bf16[160,256]{1,0:T(8,128)(2,1)S(1)}, u32[]{:S(2)}, u32[]{:S(2)}) collective-permute-start(bf16[160,256]{1,0:T(8,128)(2,1)S(1)} %early_row.1), channel_id=1, source_target_pairs={{0,16},{16,0},{1,17},{17,1},{2,18},{18,2},{3,19},{19,3},{4,20},{20... | collective-permute-start | bytes 245768 | tf_op jit(solution)/shard_map/ppermute | solution.py:294
  21.3 0.1 collective-permute-start.7
  21.4 0.0 collective-permute-done.8.refs_2_.refs_0_.refs_1_
  21.4 1.8 %collective-permute-start.12 = (bf16[16,32,256]{2,1,0:T(8,128)(2,1)S(1)}, bf16[16,32,256]{2,1,0:T(8,128)(2,1)S(1)}, u32[]{:S(2)}, u32[]{:S(2)}) collective-permute-start(bf16[16,32,256]{2,1,0:T(8,128)(2,1)S(1)} %collective-permute-done.8.refs_2_.refs_0_.refs_1_), channel_id=1, source_target_pairs={{0,4},{4,8},{8,12},{12,14},{14,10},{10,6},{6,2},{2,0},{5,1},{9,5},... | collective-permute-start | bytes 786440 | tf_op jit(solution)/shard_map/ppermute | solution.py:289
  23.1 1.1 %collective-permute-done.6.refs_2_.early_ref = bf16[160,256]{1,0:T(8,128)(2,1)S(1)} collective-permute-done((bf16[160,256]{1,0:T(8,128)(2,1)S(1)}, bf16[160,256]{1,0:T(8,128)(2,1)S(1)}, u32[]{:S(2)}, u32[]{:S(2)}) %collective-permute-start.6) | collective-permute-done | bytes 81952 | tf_op jit(solution)/shard_map/ppermute | solution.py:294
  24.2 0.0 collective-permute-done.9.refs_3_.refs_1_.refs_2_
  24.2 0.1 collective-permute-start.11
  24.3 0.0 collective-permute-done.5.refs_5_.refs_0_
  24.3 0.0 copy-done
  24.3 1.3 %early_fit.1 = (bf16[512,512]{1,0:T(8,128)(2,1)S(1)}, f32[512,4096]{1,0:T(8,128)S(1)}) custom-call(bf16[512,512]{1,0:T(8,128)(2,1)S(1)} %copy-done, bf16[16,32,256]{2,1,0:T(8,128)(2,1)S(1)} %collective-permute-done.refs_2_.refs_0_, bf16[16,32,256]{2,1,0:T(8,128)(2,1)S(1)} %collective-permute-done.1.refs_0_.refs_1_, ...), custom_call_target="tpu_custom_call" | custom-call | tf_op jit(solution)/shard_map/early_fit/pallas_call | solution.py:261
  25.7 2.1 %collective-permute-done.12.refs_0_.refs_1_.refs_4_ = bf16[16,32,256]{2,1,0:T(8,128)(2,1)S(1)} collective-permute-done((bf16[16,32,256]{2,1,0:T(8,128)(2,1)S(1)}, bf16[16,32,256]{2,1,0:T(8,128)(2,1)S(1)}, u32[]{:S(2)}, u32[]{:S(2)}) %collective-permute-start.12) | collective-permute-done | bytes 262176 | tf_op jit(solution)/shard_map/ppermute | solution.py:289
  27.8 0.0 copy-start.1
  27.8 0.0 copy-start.2
  27.8 0.1 collective-permute-start.13
  27.9 0.0 collective-permute-done.7.refs_1_.refs_0_
  27.9 1.7 %collective-permute-start.10 = (bf16[224,256]{1,0:T(8,128)(2,1)S(1)}, bf16[224,256]{1,0:T(8,128)(2,1)S(1)}, u32[]{:S(2)}, u32[]{:S(2)}) collective-permute-start(bf16[224,256]{1,0:T(8,128)(2,1)S(1)} %late_row.2), channel_id=1, source_target_pairs={{0,16},{16,0},{1,17},{17,1},{2,18},{18,2},{3,19},{19,3},{4,20},{20... | collective-permute-start | bytes 344072 | tf_op jit(solution)/shard_map/ppermute | solution.py:312
  29.6 0.0 collective-permute-done.11.refs_0_.refs_3_
  29.6 0.0 collective-permute-done.13.refs_2_.refs_5_
  29.6 1.4 %collective-permute-start.14 = (bf16[128,256]{1,0:T(8,128)(2,1)S(1)}, bf16[128,256]{1,0:T(8,128)(2,1)S(1)}, u32[]{:S(2)}, u32[]{:S(2)}) collective-permute-start(bf16[128,256]{1,0:T(8,128)(2,1)S(1)} %late_row.3), channel_id=1, source_target_pairs={{0,16},{16,0},{1,17},{17,1},{2,18},{18,2},{3,19},{19,3},{4,20},{20... | collective-permute-start | bytes 196616 | tf_op jit(solution)/shard_map/ppermute | solution.py:312
  31.0 0.0 copy-done.1
  31.0 0.0 copy-done.2
  31.0 3.7 %fit_same.1 = (bf16[512,4096]{1,0:T(8,128)(2,1)S(1)}, bf16[256,4096]{1,0:T(8,128)(2,1)S(1)}, f32[256,256]{1,0:T(8,128)S(1)}) custom-call(f32[2,16]{1,0:T(2,128)S(1)} %copy-done.2, f32[2,256]{1,0:T(2,128)S(1)} %copy-done.1, bf16[512,512]{1,0:T(8,128)(2,1)S(1)} %get-tuple-element.18.factor_ref, f32[512,4096]{1,0:T(8,128)S(1)} %get-tuple-element.19.refs_1_.early_ref, ...), custom_call_target="tpu_custom_call" | custom-call | tf_op jit(solution)/shard_map/fit_same/pallas_call | solution.py:261
  34.8 0.0 collective-permute-done.10.late_ref
  34.8 0.1 collective-permute-done.14.last_ref
  34.9 2.8 %opposite.1 = (bf16[256,4096]{1,0:T(8,128)(2,1)S(1)}, f32[2,2,32,256]{3,2,1,0:T(8,128)S(1)}, f32[2,2,32,256]{3,2,1,0:T(8,128)S(1)}) custom-call(f32[2,16]{1,0:T(2,128)S(1)} %copy-done.2, f32[2,256]{1,0:T(2,128)S(1)} %copy-done.1, bf16[512,512]{1,0:T(8,128)(2,1)S(1)} %get-tuple-element.18.factor_ref, ...), custom_call_target="tpu_custom_call" | custom-call | flops 1610612736 | bytes 5245056 | tf_op jit(solution)/shard_map/opposite/pallas_call | solution.py:261
  37.7 0.1 collective-permute-start.15
  37.8 1.3 %gamma_other.1.refs_0_ = bf16[256,512]{1,0:T(8,128)(2,1)S(1)} custom-call(bf16[256,4096]{1,0:T(8,128)(2,1)S(1)} %get-tuple-element.24.amp_ref, bf16[512,4096]{1,0:T(8,128)(2,1)S(1)} %get-tuple-element.20.fitted_ref), custom_call_target="tpu_custom_call" | custom-call | flops 1073741824 | bytes 6291456 | tf_op jit(solution)/shard_map/gamma_other/pallas_call | solution.py:261
  39.1 0.1 collective-permute-done.15.arrived
  39.2 2.7 %collective-permute-start.16 = (f32[2,32,256]{2,1,0:T(8,128)S(1)}, f32[2,32,256]{2,1,0:T(8,128)S(1)}, u32[]{:S(2)}, u32[]{:S(2)}) collective-permute-start(f32[2,32,256]{2,1,0:T(8,128)S(1)} %get-tuple-element.25), channel_id=1, source_target_pairs={{0,6},{1,3},{2,4},{3,1},{4,2},{5,7},{6,0},{7,5},{8,14},{9,11},{10,... | collective-permute-start | bytes 196616 | tf_op jit(solution)/shard_map/ppermute | solution.py:340
  41.9 0.7 %collective-permute-start.17 = (f32[2,32,256]{2,1,0:T(8,128)S(1)}, f32[2,32,256]{2,1,0:T(8,128)S(1)}, u32[]{:S(2)}, u32[]{:S(2)}) collective-permute-start(f32[2,32,256]{2,1,0:T(8,128)S(1)} %get-tuple-element.26), channel_id=1, source_target_pairs={{0,0},{1,5},{2,2},{3,7},{4,4},{5,1},{6,6},{7,3},{8,8},{9,13},{10,1... | collective-permute-start | bytes 196616 | tf_op jit(solution)/shard_map/ppermute | solution.py:341
  42.6 1.5 %collective-permute-start.20 = (bf16[256,512]{1,0:T(8,128)(2,1)S(1)}, bf16[256,512]{1,0:T(8,128)(2,1)S(1)}, u32[]{:S(2)}, u32[]{:S(2)}) collective-permute-start(bf16[256,512]{1,0:T(8,128)(2,1)S(1)} %gamma_other.1.refs_0_), channel_id=1, source_target_pairs={{0,16},{16,0},{1,17},{17,1},{2,18},{18,2},{3,19},{19,3},{4,20},{20... | collective-permute-start | bytes 786440 | tf_op jit(solution)/shard_map/ppermute | solution.py:334
  44.1 0.3 collective-permute-done.16.one_in
  44.4 0.0 collective-permute-done.17.two_in
  44.4 2.8 %collective-permute-start.18 = (f32[32,256]{1,0:T(8,128)S(1)}, f32[32,256]{1,0:T(8,128)S(1)}, u32[]{:S(2)}, u32[]{:S(2)}) collective-permute-start(f32[32,256]{1,0:T(8,128)S(1)} %get-tuple-element.28), channel_id=1, source_target_pairs={{0,8},{1,9},{2,10},{3,11},{4,12},{5,13},{6,14},{7,15},{8,0},{9,1},... | collective-permute-start | bytes 98312 | tf_op jit(solution)/shard_map/ppermute | solution.py:345
  47.2 1.3 %gamma_same.1.refs_0_.gamma_in = f32[256,512]{1,0:T(8,128)S(1)} custom-call(bf16[256,4096]{1,0:T(8,128)(2,1)S(1)} %get-tuple-element.29.amp_ref, bf16[512,4096]{1,0:T(8,128)(2,1)S(1)} %get-tuple-element.20.fitted_ref), custom_call_target="tpu_custom_call" | custom-call | flops 2147483648 | bytes 6291456 | tf_op jit(solution)/shard_map/gamma_same/pallas_call | solution.py:261
  48.5 0.8 %collective-permute-done.18.arrived = f32[32,256]{1,0:T(8,128)S(1)} collective-permute-done((f32[32,256]{1,0:T(8,128)S(1)}, f32[32,256]{1,0:T(8,128)S(1)}, u32[]{:S(2)}, u32[]{:S(2)}) %collective-permute-start.18) | collective-permute-done | bytes 32800 | tf_op jit(solution)/shard_map/ppermute | solution.py:345
  49.3 1.2 %collective-permute-start.19 = (f32[16,256]{1,0:T(8,128)S(1)}, f32[16,256]{1,0:T(8,128)S(1)}, u32[]{:S(2)}, u32[]{:S(2)}) collective-permute-start(f32[16,256]{1,0:T(8,128)S(1)} %get-tuple-element.31), channel_id=1, source_target_pairs={{0,1},{1,0},{2,3},{3,2},{4,5},{5,4},{6,7},{7,6},{8,9},{9,8},{10,11... | collective-permute-start | bytes 49160 | tf_op jit(solution)/shard_map/ppermute | solution.py:349
  50.5 0.8 %collective-permute-done.19.arrived = f32[16,256]{1,0:T(8,128)S(1)} collective-permute-done((f32[16,256]{1,0:T(8,128)S(1)}, f32[16,256]{1,0:T(8,128)S(1)}, u32[]{:S(2)}, u32[]{:S(2)}) %collective-permute-start.19) | collective-permute-done | bytes 16416 | tf_op jit(solution)/shard_map/ppermute | solution.py:349
  51.4 0.0 collective-permute-done.20.refs_0_
  51.4 0.8 %finish.1 = (f32[256,512]{1,0:T(8,128)}, f32[1,16,256]{2,1,0:T(8,128)}) custom-call(f32[16,256]{1,0:T(8,128)S(1)} %get-tuple-element.30.kept_in, f32[16,256]{1,0:T(8,128)S(1)} %collective-permute-done.19.arrived, f32[256,512]{1,0:T(8,128)S(1)} %gamma_same.1.refs_0_.gamma_in, bf16[256,512]{1,0:T(8,128)(2,1)S(1)} %collective-permute-done.20.refs_0_), custom_call_target="tpu_custom_call" | custom-call | tf_op jit(solution)/shard_map/finish/pallas_call | solution.py:261
  (9 shorter events, 0.2 us)
Async XLA Ops:
  0.6 23.7 %copy-start = (bf16[512,512]{1,0:T(8,128)(2,1)S(1)}, bf16[512,512]{1,0:T(8,128)(2,1)}, u32[]{:S(2)}) copy-start(bf16[512,512]{1,0:T(8,128)(2,1)} %given_ref.1) | copy-start | bytes 1572868
  0.6 3.2 %collective-permute-start = (bf16[16,32,256]{2,1,0:T(8,128)(2,1)}, bf16[16,32,256]{2,1,0:T(8,128)(2,1)S(1)}, u32[]{:S(2)}, u32[]{:S(2)}) collective-permute-start(bf16[16,32,256]{2,1,0:T(8,128)(2,1)} %bitcast.5), channel_id=1, source_target_pairs={{0,1},{1,0},{2,3},{3,2},{4,5},{5,4},{6,7},{7,6},{8,9},{9,8},{10,11... | collective-permute-start | bytes 786440 | tf_op jit(solution)/shard_map/ppermute | solution.py:285
  1.2 7.1 %collective-permute-start.1 = (bf16[16,32,256]{2,1,0:T(8,128)(2,1)}, bf16[16,32,256]{2,1,0:T(8,128)(2,1)S(1)}, u32[]{:S(2)}, u32[]{:S(2)}) collective-permute-start(bf16[16,32,256]{2,1,0:T(8,128)(2,1)} %bitcast.6), channel_id=1, source_target_pairs={{0,4},{4,8},{8,12},{12,14},{14,10},{10,6},{6,2},{2,0},{5,1},{9,5},... | collective-permute-start | bytes 786440 | tf_op jit(solution)/shard_map/ppermute | solution.py:289
  3.8 7.3 %collective-permute-start.2 = (bf16[16,32,256]{2,1,0:T(8,128)(2,1)S(1)}, bf16[16,32,256]{2,1,0:T(8,128)(2,1)S(1)}, u32[]{:S(2)}, u32[]{:S(2)}) collective-permute-start(bf16[16,32,256]{2,1,0:T(8,128)(2,1)S(1)} %collective-permute-done.refs_2_.refs_0_), channel_id=1, source_target_pairs={{0,4},{4,8},{8,12},{12,14},{14,10},{10,6},{6,2},{2,0},{5,1},{9,5},... | collective-permute-start | bytes 786440 | tf_op jit(solution)/shard_map/ppermute | solution.py:289
  8.3 6.4 %collective-permute-start.3 = (bf16[16,32,256]{2,1,0:T(8,128)(2,1)S(1)}, bf16[16,32,256]{2,1,0:T(8,128)(2,1)S(1)}, u32[]{:S(2)}, u32[]{:S(2)}) collective-permute-start(bf16[16,32,256]{2,1,0:T(8,128)(2,1)S(1)} %collective-permute-done.1.refs_0_.refs_1_), channel_id=1, source_target_pairs={{0,4},{4,8},{8,12},{12,14},{14,10},{10,6},{6,2},{2,0},{5,1},{9,5},... | collective-permute-start | bytes 786440 | tf_op jit(solution)/shard_map/ppermute | solution.py:289
  11.2 13.2 %collective-permute-start.5 = (bf16[3,16,32,256]{3,2,1,0:T(8,128)(2,1)S(1)}, bf16[3,16,32,256]{3,2,1,0:T(8,128)(2,1)S(1)}, u32[]{:S(2)}, u32[]{:S(2)}) collective-permute-start(bf16[3,16,32,256]{3,2,1,0:T(8,128)(2,1)S(1)} %stack.4), channel_id=1, source_target_pairs={{0,1},{1,0},{2,3},{3,2},{4,5},{5,4},{6,7},{7,6},{8,9},{9,8},{10,11... | collective-permute-start | bytes 2359304 | tf_op jit(solution)/shard_map/ppermute | solution.py:305
  11.2 6.4 %collective-permute-start.4 = (bf16[16,32,256]{2,1,0:T(8,128)(2,1)S(1)}, bf16[16,32,256]{2,1,0:T(8,128)(2,1)S(1)}, u32[]{:S(2)}, u32[]{:S(2)}) collective-permute-start(bf16[16,32,256]{2,1,0:T(8,128)(2,1)S(1)} %collective-permute-done.2.refs_1_.refs_2_), channel_id=1, source_target_pairs={{0,4},{4,8},{8,12},{12,14},{14,10},{10,6},{6,2},{2,0},{5,1},{9,5},... | collective-permute-start | bytes 786440 | tf_op jit(solution)/shard_map/ppermute | solution.py:289
  14.7 6.7 %collective-permute-start.8 = (bf16[16,32,256]{2,1,0:T(8,128)(2,1)S(1)}, bf16[16,32,256]{2,1,0:T(8,128)(2,1)S(1)}, u32[]{:S(2)}, u32[]{:S(2)}) collective-permute-start(bf16[16,32,256]{2,1,0:T(8,128)(2,1)S(1)} %collective-permute-done.3.refs_3_.refs_0_), channel_id=1, source_target_pairs={{0,4},{4,8},{8,12},{12,14},{14,10},{10,6},{6,2},{2,0},{5,1},{9,5},... | collective-permute-start | bytes 786440 | tf_op jit(solution)/shard_map/ppermute | solution.py:289
  17.7 6.5 %collective-permute-start.9 = (bf16[16,32,256]{2,1,0:T(8,128)(2,1)S(1)}, bf16[16,32,256]{2,1,0:T(8,128)(2,1)S(1)}, u32[]{:S(2)}, u32[]{:S(2)}) collective-permute-start(bf16[16,32,256]{2,1,0:T(8,128)(2,1)S(1)} %collective-permute-done.4.refs_4_.refs_1_), channel_id=1, source_target_pairs={{0,4},{4,8},{8,12},{12,14},{14,10},{10,6},{6,2},{2,0},{5,1},{9,5},... | collective-permute-start | bytes 786440 | tf_op jit(solution)/shard_map/ppermute | solution.py:289
  19.8 4.4 %collective-permute-start.6 = (bf16[160,256]{1,0:T(8,128)(2,1)S(1)}, bf16[160,256]{1,0:T(8,128)(2,1)S(1)}, u32[]{:S(2)}, u32[]{:S(2)}) collective-permute-start(bf16[160,256]{1,0:T(8,128)(2,1)S(1)} %early_row.1), channel_id=1, source_target_pairs={{0,16},{16,0},{1,17},{17,1},{2,18},{18,2},{3,19},{19,3},{4,20},{20... | collective-permute-start | bytes 245768 | tf_op jit(solution)/shard_map/ppermute | solution.py:294
  21.3 6.6 %collective-permute-start.7 = (bf16[2,16,32,256]{3,2,1,0:T(8,128)(2,1)S(1)}, bf16[2,16,32,256]{3,2,1,0:T(8,128)(2,1)S(1)}, u32[]{:S(2)}, u32[]{:S(2)}) collective-permute-start(bf16[2,16,32,256]{3,2,1,0:T(8,128)(2,1)S(1)} %stack.5), channel_id=1, source_target_pairs={{0,1},{1,0},{2,3},{3,2},{4,5},{5,4},{6,7},{7,6},{8,9},{9,8},{10,11... | collective-permute-start | bytes 1572872 | tf_op jit(solution)/shard_map/ppermute | solution.py:305
  21.4 6.4 %collective-permute-start.12 = (bf16[16,32,256]{2,1,0:T(8,128)(2,1)S(1)}, bf16[16,32,256]{2,1,0:T(8,128)(2,1)S(1)}, u32[]{:S(2)}, u32[]{:S(2)}) collective-permute-start(bf16[16,32,256]{2,1,0:T(8,128)(2,1)S(1)} %collective-permute-done.8.refs_2_.refs_0_.refs_1_), channel_id=1, source_target_pairs={{0,4},{4,8},{8,12},{12,14},{14,10},{10,6},{6,2},{2,0},{5,1},{9,5},... | collective-permute-start | bytes 786440 | tf_op jit(solution)/shard_map/ppermute | solution.py:289
  24.2 5.4 %collective-permute-start.11 = (bf16[2,16,32,256]{3,2,1,0:T(8,128)(2,1)S(1)}, bf16[2,16,32,256]{3,2,1,0:T(8,128)(2,1)S(1)}, u32[]{:S(2)}, u32[]{:S(2)}) collective-permute-start(bf16[2,16,32,256]{3,2,1,0:T(8,128)(2,1)S(1)} %stack.6), channel_id=1, source_target_pairs={{0,1},{1,0},{2,3},{3,2},{4,5},{5,4},{6,7},{7,6},{8,9},{9,8},{10,11... | collective-permute-start | bytes 1572872 | tf_op jit(solution)/shard_map/ppermute | solution.py:305
  27.8 3.2 %copy-start.1 = (f32[2,256]{1,0:T(2,128)S(1)}, f32[2,256]{1,0:T(2,128)}, u32[]{:S(2)}) copy-start(f32[2,256]{1,0:T(2,128)} %virt_ref.3) | copy-start | bytes 6148
  27.8 3.2 %copy-start.2 = (f32[2,16]{1,0:T(2,128)S(1)}, f32[2,16]{1,0:T(2,128)}, u32[]{:S(2)}) copy-start(f32[2,16]{1,0:T(2,128)} %occ_ref.3) | copy-start | bytes 388
  27.8 1.8 %collective-permute-start.13 = (bf16[1,16,32,256]{3,2,1,0:T(8,128)(2,1)S(1)}, bf16[1,16,32,256]{3,2,1,0:T(8,128)(2,1)S(1)}, u32[]{:S(2)}, u32[]{:S(2)}) collective-permute-start(bf16[1,16,32,256]{3,2,1,0:T(8,128)(2,1)S(1)} %stack.7), channel_id=1, source_target_pairs={{0,1},{1,0},{2,3},{3,2},{4,5},{5,4},{6,7},{7,6},{8,9},{9,8},{10,11... | collective-permute-start | bytes 786440 | tf_op jit(solution)/shard_map/ppermute | solution.py:305
  27.9 6.8 %collective-permute-start.10 = (bf16[224,256]{1,0:T(8,128)(2,1)S(1)}, bf16[224,256]{1,0:T(8,128)(2,1)S(1)}, u32[]{:S(2)}, u32[]{:S(2)}) collective-permute-start(bf16[224,256]{1,0:T(8,128)(2,1)S(1)} %late_row.2), channel_id=1, source_target_pairs={{0,16},{16,0},{1,17},{17,1},{2,18},{18,2},{3,19},{19,3},{4,20},{20... | collective-permute-start | bytes 344072 | tf_op jit(solution)/shard_map/ppermute | solution.py:312
  29.6 5.3 %collective-permute-start.14 = (bf16[128,256]{1,0:T(8,128)(2,1)S(1)}, bf16[128,256]{1,0:T(8,128)(2,1)S(1)}, u32[]{:S(2)}, u32[]{:S(2)}) collective-permute-start(bf16[128,256]{1,0:T(8,128)(2,1)S(1)} %late_row.3), channel_id=1, source_target_pairs={{0,16},{16,0},{1,17},{17,1},{2,18},{18,2},{3,19},{19,3},{4,20},{20... | collective-permute-start | bytes 196616 | tf_op jit(solution)/shard_map/ppermute | solution.py:312
  37.7 1.4 %collective-permute-start.15 = (f32[2,2,32,256]{3,2,1,0:T(8,128)S(1)}, f32[2,2,32,256]{3,2,1,0:T(8,128)S(1)}, u32[]{:S(2)}, u32[]{:S(2)}) collective-permute-start(f32[2,2,32,256]{3,2,1,0:T(8,128)S(1)} %get-tuple-element.23), channel_id=1, source_target_pairs={{0,1},{1,0},{2,3},{3,2},{4,5},{5,4},{6,7},{7,6},{8,9},{9,8},{10,11... | collective-permute-start | bytes 393224 | tf_op jit(solution)/shard_map/ppermute | solution.py:335
  39.2 5.2 %collective-permute-start.16 = (f32[2,32,256]{2,1,0:T(8,128)S(1)}, f32[2,32,256]{2,1,0:T(8,128)S(1)}, u32[]{:S(2)}, u32[]{:S(2)}) collective-permute-start(f32[2,32,256]{2,1,0:T(8,128)S(1)} %get-tuple-element.25), channel_id=1, source_target_pairs={{0,6},{1,3},{2,4},{3,1},{4,2},{5,7},{6,0},{7,5},{8,14},{9,11},{10,... | collective-permute-start | bytes 196616 | tf_op jit(solution)/shard_map/ppermute | solution.py:340
  41.9 2.5 %collective-permute-start.17 = (f32[2,32,256]{2,1,0:T(8,128)S(1)}, f32[2,32,256]{2,1,0:T(8,128)S(1)}, u32[]{:S(2)}, u32[]{:S(2)}) collective-permute-start(f32[2,32,256]{2,1,0:T(8,128)S(1)} %get-tuple-element.26), channel_id=1, source_target_pairs={{0,0},{1,5},{2,2},{3,7},{4,4},{5,1},{6,6},{7,3},{8,8},{9,13},{10,1... | collective-permute-start | bytes 196616 | tf_op jit(solution)/shard_map/ppermute | solution.py:341
  42.6 8.8 %collective-permute-start.20 = (bf16[256,512]{1,0:T(8,128)(2,1)S(1)}, bf16[256,512]{1,0:T(8,128)(2,1)S(1)}, u32[]{:S(2)}, u32[]{:S(2)}) collective-permute-start(bf16[256,512]{1,0:T(8,128)(2,1)S(1)} %gamma_other.1.refs_0_), channel_id=1, source_target_pairs={{0,16},{16,0},{1,17},{17,1},{2,18},{18,2},{3,19},{19,3},{4,20},{20... | collective-permute-start | bytes 786440 | tf_op jit(solution)/shard_map/ppermute | solution.py:334
  44.4 4.9 %collective-permute-start.18 = (f32[32,256]{1,0:T(8,128)S(1)}, f32[32,256]{1,0:T(8,128)S(1)}, u32[]{:S(2)}, u32[]{:S(2)}) collective-permute-start(f32[32,256]{1,0:T(8,128)S(1)} %get-tuple-element.28), channel_id=1, source_target_pairs={{0,8},{1,9},{2,10},{3,11},{4,12},{5,13},{6,14},{7,15},{8,0},{9,1},... | collective-permute-start | bytes 98312 | tf_op jit(solution)/shard_map/ppermute | solution.py:345
  49.3 2.0 %collective-permute-start.19 = (f32[16,256]{1,0:T(8,128)S(1)}, f32[16,256]{1,0:T(8,128)S(1)}, u32[]{:S(2)}, u32[]{:S(2)}) collective-permute-start(f32[16,256]{1,0:T(8,128)S(1)} %get-tuple-element.31), channel_id=1, source_target_pairs={{0,1},{1,0},{2,3},{3,2},{4,5},{5,4},{6,7},{7,6},{8,9},{9,8},{10,11... | collective-permute-start | bytes 49160 | tf_op jit(solution)/shard_map/ppermute | solution.py:349
